TPU v7x, 32 devices: a whole 2x2x4 slice. The times are simulated.
32 devices in a mesh: rows: 8 (over z, y), seq: 4 (over x, core).
Axes of the slice: x: 2, y: 2, z: 4, core: 2. Of those that a mesh axis runs over, the one named last changes fastest.
Arguments:
- decoder_input: bfloat16 [8, 1408, 768], P('rows', 'seq'), may hold values from -6 to 6
- encoder_output: bfloat16 [8, 4096, 768], P('rows', 'seq'), may hold values from -6 to 6
- cotangent: bfloat16 [8, 1408, 768], P('rows', 'seq'), may hold values from -6 to 6
- decoder_segment: int32 [8, 1408], P('rows'), may hold values from 0 to 2, as said below
- decoder_padding: int32 [8, 1408], P('rows'), may hold values from 0 to 1, as said below
- encoder_segment: int32 [8, 4096], P('rows'), may hold values from 0 to 2, as said below
- encoder_padding: int32 [8, 4096], P('rows'), may hold values from 0 to 1, as said below
- distance_bucket: int32 [1408], replicated, may hold values from 0 to 31, as said below
- attention_weight: float32 [768, 8, 768], P(('rows', 'seq'))
- attention_moment: float32 [768, 8, 768], P(('rows', 'seq')), may hold values from -64 to 64
- attention_rowwise: float32 [8, 768], P(None, ('rows', 'seq')), may hold values from 11.264 to 45.056
- attention_colwise: float32 [8, 768], replicated, may hold values from 11.264 to 45.056
- expand_weight: float32 [768, 2, 2048], P(('rows', 'seq')), may hold values from -0.21875 to 0.21875
- expand_moment: float32 [768, 2, 2048], P(('rows', 'seq')), may hold values from -64 to 64
- expand_rowwise: float32 [2, 768], P(None, ('rows', 'seq')), may hold values from 11.264 to 45.056
- expand_colwise: float32 [2, 2048], replicated, may hold values from 11.264 to 45.056
- contract_weight: float32 [2048, 768], P(('rows', 'seq')), may hold values from -0.25 to 0.25
- contract_moment: float32 [2048, 768], P(('rows', 'seq')), may hold values from -64 to 64
- contract_rowwise: float32 [2048], P(('rows', 'seq')), may hold values from 11.264 to 45.056
- contract_colwise: float32 [768], replicated, may hold values from 11.264 to 45.056
- norm_gain: float32 [3, 768], replicated
- gain_moment: float32 [3, 768], replicated, may hold values from -64 to 64
- gain_second: float32 [3, 768], replicated, may hold values from 11.264 to 45.056
- relative_table: float32 [32, 12], replicated, may hold values from -4 to 4
- table_moment: float32 [32, 12], replicated, may hold values from -64 to 64
- table_second: float32 [32, 12], replicated, may hold values from 11.264 to 45.056
Outputs:
- layer_output: bfloat16 [8, 1408, 768], P('rows', 'seq')
- input_gradient: float32 [8, 1408, 768], P('rows', 'seq')
- encoder_gradient: float32 [8, 4096, 768], P('rows', 'seq')
- attention_gradient: float32 [768, 8, 768], P(('rows', 'seq'))
- moment_attention: float32 [768, 8, 768], P(('rows', 'seq'))
- rowwise_attention: float32 [8, 768], P(None, ('rows', 'seq'))
- colwise_attention: float32 [8, 768], replicated
- updated_attention: float32 [768, 8, 768], P(('rows', 'seq'))
- expand_gradient: float32 [768, 2, 2048], P(('rows', 'seq'))
- moment_expand: float32 [768, 2, 2048], P(('rows', 'seq'))
- rowwise_expand: float32 [2, 768], P(None, ('rows', 'seq'))
- colwise_expand: float32 [2, 2048], replicated
- updated_expand: float32 [768, 2, 2048], P(('rows', 'seq'))
- contract_gradient: float32 [2048, 768], P(('rows', 'seq'))
- moment_contract: float32 [2048, 768], P(('rows', 'seq'))
- rowwise_contract: float32 [2048], P(('rows', 'seq'))
- colwise_contract: float32 [768], replicated
- updated_contract: float32 [2048, 768], P(('rows', 'seq'))
- gain_gradient: float32 [3, 768], replicated
- moment_gain: float32 [3, 768], replicated
- second_gain: float32 [3, 768], replicated
- updated_gain: float32 [3, 768], replicated
- table_gradient: float32 [32, 12], replicated
- moment_table: float32 [32, 12], replicated
- second_table: float32 [32, 12], replicated
- updated_table: float32 [32, 12], replicated
Inputs may be any that keep to these rules, and one draw needn't show every extreme that they name: `decoder_segment`: never falls along a row; every row holds documents 0, 1 and 2, and document 1 starts among the first 352 positions and ends among the last 352. `decoder_padding`: in each row the zeros form a non-empty tail inside document 2, which keeps a real position. `encoder_segment`: never falls along a row; every row holds documents 0, 1 and 2, and document 1 starts among the first 1024 positions and ends among the last 1024. `encoder_padding`: in each row the zeros form a non-empty tail inside document 2, which keeps a real position. `distance_bucket`: never falls; entry d is d for d below 16, and the last entry is 31.
All inputs are finite; a program needn't handle non-finite values.
Results may differ from a plain program's by a relative error of at most 0.024.
The roundings to bfloat16 on the way count: a program that leaves them out, or rounds other values in their place, can miss the bound.
Values may be sent and summed in bfloat16 or wider, within the bound.
A program may use at most 384 MiB of HBM per device.

v0:
```python
import jax
import jax.numpy as jnp
from jax import lax
from jax.sharding import PartitionSpec as P

D = 768
FF = 2048
HEADS = 12
BUCKETS = 32
DEC_LEN = 1408
STEP = 10


HIGHEST = lax.Precision.HIGHEST
NORM_EPS = 1e-06
MASKED = -1e30
BETA_ONE = 0.9
BETA_TWO = 0.999
ADAM_EPS = 1e-08
WEIGHT_DECAY = 0.01
MATRIX_RATE = 0.15
VECTOR_RATE = 1.0


def normalize(values, scaling):
    return values * lax.rsqrt(jnp.mean(values * values, -1, keepdims=True) + NORM_EPS) * scaling


def gated(gate_values, up_values):
    return jax.nn.gelu(gate_values, approximate=True) * up_values


def split_heads(values):
    leading, length, features = values.shape
    return jnp.transpose(values.reshape(leading, length, HEADS, features // HEADS), (2, 0, 1, 3))


def merge_heads(values):
    head_count, leading, length, inner_size = values.shape
    return jnp.transpose(values, (1, 2, 0, 3)).reshape(leading, length, head_count * inner_size)


def project(values, matrix):
    return jnp.einsum("rsn,nm->rsm", values, matrix, preferred_element_type=jnp.float32)


def project_many(values, matrices):
    return jnp.einsum("rsn,njm->rsjm", values, matrices, preferred_element_type=jnp.float32)


def back_one(gradient, matrix):
    return jnp.einsum("rsm,nm->rsn", gradient, matrix, preferred_element_type=jnp.float32)


def back_many(gradient, matrices):
    return jnp.einsum("rsjm,njm->rsn", gradient, matrices, preferred_element_type=jnp.float32)


def outer_one(values, gradient):
    return jnp.einsum("rsn,rsm->nm", values, gradient, preferred_element_type=jnp.float32)


def outer_many(values, gradient):
    return jnp.einsum("rsn,rsjm->njm", values, gradient, preferred_element_type=jnp.float32)


def scores(queries, key_rows, allowed, offset):
    factor = queries.shape[-1] ** (-0.5)
    scored = (
        jnp.einsum("rqd,rkd->rqk", queries, key_rows, preferred_element_type=jnp.float32) * factor
        + offset
    )
    return jnp.where(allowed, scored, MASKED)


def forward_heads(query_heads, key_heads, value_heads, allowed, offsets):

    def attend_head(items):
        queries, key_rows, value_rows = (items[0], items[1], items[2])
        offset = 0.0 if offsets is None else items[3][None]
        scored = scores(queries, key_rows, allowed, offset)
        maximum = jnp.max(scored, -1, keepdims=True)
        exponent = jnp.exp(scored - maximum)
        denominator = jnp.sum(exponent, -1, keepdims=True)
        probability = (exponent / denominator).astype(jnp.bfloat16)
        result = jnp.einsum(
            "rqk,rkd->rqd", probability, value_rows, preferred_element_type=jnp.float32
        )
        return (result.astype(jnp.bfloat16), maximum[..., 0], denominator[..., 0])

    items = (query_heads, key_heads, value_heads)
    if offsets is not None:
        items = items + (offsets,)
    return lax.map(attend_head, items)


def backward_heads(
    query_heads, key_heads, value_heads, output_heads, maxima, totals, allowed, offsets
):

    def head_grad(items):
        queries, key_rows, value_rows, grad_rows, maximum, denominator = items[:6]
        offset = 0.0 if offsets is None else items[6][None]
        scored = scores(queries, key_rows, allowed, offset)
        probability = jnp.exp(scored - maximum[..., None]) / denominator[..., None]
        grad_prob = jnp.einsum(
            "rqd,rkd->rqk", grad_rows, value_rows, preferred_element_type=jnp.float32
        )
        centre = jnp.sum(probability * grad_prob, -1, keepdims=True)
        grad_score = jnp.where(allowed, probability * (grad_prob - centre), 0.0).astype(
            jnp.bfloat16
        )
        factor = queries.shape[-1] ** (-0.5)
        grad_query = (
            jnp.einsum("rqk,rkd->rqd", grad_score, key_rows, preferred_element_type=jnp.float32)
            * factor
        )
        result = (grad_query, centre[..., 0])
        if offsets is not None:
            result = result + (jnp.sum(grad_score.astype(jnp.float32), 0),)
        grad_key = (
            jnp.einsum("rqk,rqd->rkd", grad_score, queries, preferred_element_type=jnp.float32)
            * factor
        )
        grad_value = jnp.einsum(
            "rqk,rqd->rkd",
            probability.astype(jnp.bfloat16),
            grad_rows,
            preferred_element_type=jnp.float32,
        )
        result = result + (grad_key, grad_value)
        return result

    items = (query_heads, key_heads, value_heads, output_heads, maxima, totals)
    if offsets is not None:
        items = items + (offsets,)
    return lax.map(head_grad, items)


def factored_start(gradient, rowwise):
    square = gradient * gradient
    rowwise_new = BETA_TWO * rowwise + (1.0 - BETA_TWO) * jnp.mean(square, 2).T
    return (rowwise_new, jnp.sum(square, 0), jnp.sum(rowwise_new, 1))


def factored_finish(
    gradient, moment, rowwise_new, colwise, weight, column_sum, row_sum, total_rows
):
    colwise_new = BETA_TWO * colwise + (1.0 - BETA_TWO) * (column_sum / total_rows)
    moment_new = BETA_ONE * moment + (1.0 - BETA_ONE) * gradient
    second = rowwise_new.T[:, :, None] * colwise_new[None] / (row_sum / total_rows)[None, :, None]
    stepped = (
        moment_new / (1.0 - BETA_ONE**STEP) / (jnp.sqrt(second / (1.0 - BETA_TWO**STEP)) + ADAM_EPS)
    )
    updated = weight - MATRIX_RATE * (stepped + WEIGHT_DECAY * weight)
    return (moment_new, colwise_new, updated)


def adaptive(gradient, moment, second, weight):
    moment_new = BETA_ONE * moment + (1.0 - BETA_ONE) * gradient
    second_new = BETA_TWO * second + (1.0 - BETA_TWO) * gradient * gradient
    stepped = (
        moment_new
        / (1.0 - BETA_ONE**STEP)
        / (jnp.sqrt(second_new / (1.0 - BETA_TWO**STEP)) + ADAM_EPS)
    )
    return (moment_new, second_new, weight - VECTOR_RATE * stepped)


def shards(
    decoder_input,
    encoder_output,
    cotangent,
    decoder_segment,
    decoder_padding,
    encoder_segment,
    encoder_padding,
    distance_bucket,
    attention_weight,
    attention_moment,
    attention_rowwise,
    attention_colwise,
    expand_weight,
    expand_moment,
    expand_rowwise,
    expand_colwise,
    contract_weight,
    contract_moment,
    contract_rowwise,
    contract_colwise,
    norm_gain,
    gain_moment,
    gain_second,
    relative_table,
    table_moment,
    table_second,
):
    shard_index = lax.axis_index("seq")
    local_count = decoder_input.shape[1]
    decoder_start = shard_index * local_count
    bucket_ids = jnp.arange(BUCKETS + 1, dtype=jnp.int32)
    bucket_bounds = jnp.sum((distance_bucket[None, :] < bucket_ids[:, None]).astype(jnp.int32), 1)
    attention_full, expand_full, contract_full = (
        lax.all_gather(attention_weight.astype(jnp.bfloat16), ("rows", "seq"), axis=0, tiled=True),
        lax.all_gather(expand_weight.astype(jnp.bfloat16), ("rows", "seq"), axis=0, tiled=True),
        lax.all_gather(contract_weight.astype(jnp.bfloat16), ("rows", "seq"), axis=0, tiled=True),
    )
    inputs = decoder_input.astype(jnp.float32)
    first_norm = normalize(inputs, norm_gain[0]).astype(jnp.bfloat16)
    self_proj = project_many(first_norm, attention_full[:, 0:3]).astype(jnp.bfloat16)
    self_query, self_key, self_value = (self_proj[:, :, 0], self_proj[:, :, 1], self_proj[:, :, 2])
    key_all, value_all = (
        lax.all_gather(self_key, "seq", axis=1, tiled=True),
        lax.all_gather(self_value, "seq", axis=1, tiled=True),
    )
    query_place = decoder_start + jnp.arange(local_count, dtype=jnp.int32)
    key_place = jnp.arange(DEC_LEN, dtype=jnp.int32)
    query_segment = lax.dynamic_slice_in_dim(decoder_segment, decoder_start, local_count, 1)
    key_segment = decoder_segment
    key_real = decoder_padding == 1
    causal = key_place[None, :] <= query_place[:, None]
    itself = key_place[None, :] == query_place[:, None]
    allowed = (
        causal[None]
        & (query_segment[:, :, None] == key_segment[:, None, :])
        & (key_real[:, None, :] | itself[None])
    )
    distance = jnp.clip(query_place[:, None] - key_place[None, :], 0, DEC_LEN - 1)[:, :, None]
    bucket_onehot = (
        (distance >= bucket_bounds[None, None, :-1]) & (distance < bucket_bounds[None, None, 1:])
    ).astype(jnp.float32)
    self_offsets = jnp.einsum("qkb,bh->hqk", bucket_onehot, relative_table, precision=HIGHEST)
    self_qheads = split_heads(self_query)
    self_kheads = split_heads(key_all)
    self_vheads = split_heads(value_all)
    self_heads, self_top, self_total = forward_heads(
        self_qheads, self_kheads, self_vheads, allowed, self_offsets
    )
    self_out = merge_heads(self_heads)
    after_self = inputs + project(self_out, attention_full[:, 3])
    cross_norm = normalize(after_self, norm_gain[1]).astype(jnp.bfloat16)
    cross_query = project(cross_norm, attention_full[:, 4]).astype(jnp.bfloat16)
    cross_pair = project_many(encoder_output, attention_full[:, 5:7]).astype(jnp.bfloat16)
    cross_key, cross_value = (cross_pair[:, :, 0], cross_pair[:, :, 1])
    cross_key_all, cross_value_all = (
        lax.all_gather(cross_key, "seq", axis=1, tiled=True),
        lax.all_gather(cross_value, "seq", axis=1, tiled=True),
    )
    query_segment = lax.dynamic_slice_in_dim(decoder_segment, decoder_start, local_count, 1)
    key_segment = encoder_segment
    key_real = encoder_padding == 1
    cross_allowed = (query_segment[:, :, None] == key_segment[:, None, :]) & key_real[:, None, :]
    cross_qheads = split_heads(cross_query)
    cross_kheads = split_heads(cross_key_all)
    cross_vheads = split_heads(cross_value_all)
    cross_heads, cross_top, cross_total = forward_heads(
        cross_qheads, cross_kheads, cross_vheads, cross_allowed, None
    )
    cross_out = merge_heads(cross_heads)
    after_cross = after_self + project(cross_out, attention_full[:, 7])
    feed_norm = normalize(after_cross, norm_gain[2]).astype(jnp.bfloat16)
    hidden_pair = project_many(feed_norm, expand_full)
    gate_values, up_values = (hidden_pair[:, :, 0], hidden_pair[:, :, 1])
    hidden = gated(gate_values, up_values).astype(jnp.bfloat16)
    result = after_cross + project(hidden, contract_full)
    layer_output = result.astype(jnp.bfloat16)
    grad_result = cotangent.astype(jnp.float32)
    feed_branch = grad_result.astype(jnp.bfloat16)
    contract_local = outer_one(hidden, feed_branch)
    grad_hidden = back_one(feed_branch, contract_full)
    unused_gated, gated_back = jax.vjp(gated, gate_values, up_values)
    grad_gate, grad_up = gated_back(grad_hidden)
    grad_pair = jnp.stack((grad_gate, grad_up), 2).astype(jnp.bfloat16)
    expand_local = outer_many(feed_norm, grad_pair)
    unused_norm, norm_back = jax.vjp(normalize, after_cross, norm_gain[2])
    feed_part, feed_gain = norm_back(back_many(grad_pair, expand_full))
    grad_after_cross = grad_result + feed_part
    cross_branch = grad_after_cross.astype(jnp.bfloat16)
    cross_out_local = outer_one(cross_out, cross_branch)
    cross_grad_out = back_one(cross_branch, attention_full[:, 7]).astype(jnp.bfloat16)
    cross_oheads = split_heads(cross_grad_out)
    cross_qgrad, unused_centre, cross_kparts, cross_vparts = backward_heads(
        cross_qheads,
        cross_kheads,
        cross_vheads,
        cross_oheads,
        cross_top,
        cross_total,
        cross_allowed,
        None,
    )
    cross_key_grad, cross_value_grad = (
        lax.psum_scatter(merge_heads(cross_kparts), "seq", scatter_dimension=1, tiled=True),
        lax.psum_scatter(merge_heads(cross_vparts), "seq", scatter_dimension=1, tiled=True),
    )
    grad_cross_query = merge_heads(cross_qgrad).astype(jnp.bfloat16)
    grad_cross_pair = jnp.stack((cross_key_grad, cross_value_grad), 2).astype(jnp.bfloat16)
    encoder_gradient = back_many(grad_cross_pair, attention_full[:, 5:7])
    cross_pair_local = outer_many(encoder_output, grad_cross_pair)
    cross_query_local = outer_one(cross_norm, grad_cross_query)
    unused_norm, norm_back = jax.vjp(normalize, after_self, norm_gain[1])
    cross_part, cross_gain = norm_back(back_one(grad_cross_query, attention_full[:, 4]))
    grad_after_self = grad_after_cross + cross_part
    self_branch = grad_after_self.astype(jnp.bfloat16)
    self_out_local = outer_one(self_out, self_branch)
    self_grad_out = back_one(self_branch, attention_full[:, 3]).astype(jnp.bfloat16)
    self_oheads = split_heads(self_grad_out)
    self_qgrad, unused_centre, pair_grad, self_kparts, self_vparts = backward_heads(
        self_qheads,
        self_kheads,
        self_vheads,
        self_oheads,
        self_top,
        self_total,
        allowed,
        self_offsets,
    )
    self_key_grad, self_value_grad = (
        lax.psum_scatter(merge_heads(self_kparts), "seq", scatter_dimension=1, tiled=True),
        lax.psum_scatter(merge_heads(self_vparts), "seq", scatter_dimension=1, tiled=True),
    )
    grad_self_proj = jnp.stack((merge_heads(self_qgrad), self_key_grad, self_value_grad), 2).astype(
        jnp.bfloat16
    )
    self_proj_local = outer_many(first_norm, grad_self_proj)
    unused_norm, norm_back = jax.vjp(normalize, inputs, norm_gain[0])
    self_part, self_gain = norm_back(back_many(grad_self_proj, attention_full[:, 0:3]))
    input_gradient = grad_after_self + self_part
    table_local = jnp.einsum("hqk,qkb->bh", pair_grad, bucket_onehot, precision=HIGHEST)
    attention_local = jnp.concatenate(
        (
            self_proj_local,
            self_out_local[:, None],
            cross_query_local[:, None],
            cross_pair_local,
            cross_out_local[:, None],
        ),
        1,
    )
    attention_sum, expand_sum, contract_sum = (
        lax.psum_scatter(attention_local, ("rows", "seq"), scatter_dimension=0, tiled=True),
        lax.psum_scatter(expand_local, ("rows", "seq"), scatter_dimension=0, tiled=True),
        lax.psum_scatter(contract_local, ("rows", "seq"), scatter_dimension=0, tiled=True),
    )
    attention_rows, attention_columns, attention_rowsum = factored_start(
        attention_sum, attention_rowwise
    )
    expand_rows, expand_columns, expand_rowsum = factored_start(expand_sum, expand_rowwise)
    contract_rows, contract_columns, contract_rowsum = factored_start(
        contract_sum[:, None, :], contract_rowwise[None, :]
    )
    gain_local = jnp.stack((self_gain, cross_gain, feed_gain), 0)
    summed = lax.psum(
        (
            attention_columns,
            expand_columns,
            contract_columns,
            attention_rowsum,
            expand_rowsum,
            contract_rowsum,
            gain_local,
            table_local,
        ),
        ("rows", "seq"),
    )
    (
        attention_total,
        expand_total,
        contract_total,
        attention_rowtotal,
        expand_rowtotal,
        contract_rowtotal,
        gain_gradient,
        table_gradient,
    ) = summed
    attention_new = factored_finish(
        attention_sum,
        attention_moment,
        attention_rows,
        attention_colwise,
        attention_weight,
        attention_total,
        attention_rowtotal,
        D,
    )
    expand_new = factored_finish(
        expand_sum,
        expand_moment,
        expand_rows,
        expand_colwise,
        expand_weight,
        expand_total,
        expand_rowtotal,
        D,
    )
    contract_new = factored_finish(
        contract_sum[:, None, :],
        contract_moment[:, None, :],
        contract_rows,
        contract_colwise[None, :],
        contract_weight[:, None, :],
        contract_total,
        contract_rowtotal,
        FF,
    )
    gain_new = adaptive(gain_gradient, gain_moment, gain_second, norm_gain)
    table_new = adaptive(table_gradient, table_moment, table_second, relative_table)
    return (
        layer_output,
        input_gradient,
        encoder_gradient,
        attention_sum,
        attention_new[0],
        attention_rows,
        attention_new[1],
        attention_new[2],
        expand_sum,
        expand_new[0],
        expand_rows,
        expand_new[1],
        expand_new[2],
        contract_sum,
        contract_new[0][:, 0],
        contract_rows[0],
        contract_new[1][0],
        contract_new[2][:, 0],
        gain_gradient,
        gain_new[0],
        gain_new[1],
        gain_new[2],
        table_gradient,
        table_new[0],
        table_new[1],
        table_new[2],
    )


def solution(mesh):
    placed = (
        P("rows", "seq", None),
        P("rows", "seq", None),
        P("rows", "seq", None),
        P("rows", None),
        P("rows", None),
        P("rows", None),
        P("rows", None),
        P(),
        P(("rows", "seq"), None, None),
        P(("rows", "seq"), None, None),
        P(None, ("rows", "seq")),
        P(),
        P(("rows", "seq"), None, None),
        P(("rows", "seq"), None, None),
        P(None, ("rows", "seq")),
        P(),
        P(("rows", "seq"), None),
        P(("rows", "seq"), None),
        P(("rows", "seq")),
        P(),
        P(),
        P(),
        P(),
        P(),
        P(),
        P(),
    )
    return jax.shard_map(
        shards,
        mesh=mesh,
        in_specs=placed,
        out_specs=(
            P("rows", "seq", None),
            P("rows", "seq", None),
            P("rows", "seq", None),
            P(("rows", "seq"), None, None),
            P(("rows", "seq"), None, None),
            P(None, ("rows", "seq")),
            P(),
            P(("rows", "seq"), None, None),
            P(("rows", "seq"), None, None),
            P(("rows", "seq"), None, None),
            P(None, ("rows", "seq")),
            P(),
            P(("rows", "seq"), None, None),
            P(("rows", "seq"), None),
            P(("rows", "seq"), None),
            P(("rows", "seq")),
            P(),
            P(("rows", "seq"), None),
            P(),
            P(),
            P(),
            P(),
            P(),
            P(),
            P(),
            P(),
        ),
        check_vma=False,
    )
```

profile of v0, /device:TPU:0, one launch (start us, length us, event | category | flops | bytes accessed | tf_op | source)
XLA Modules:
  0.0 2097.8 jit_solution(3755284931769804453)
XLA Ops:
  12.7 83.7 %all-gather.12.cloned.1.call-done = bf16[768,8,768]{2,0,1:T(8,128)(2,1)} async-done(((bf16[24,8,768]{2,0,1:T(8,128)(2,1)}), bf16[768,8,768]{2,0,1:T(8,128)(2,1)}) %all-gather.12.cloned.1.call-update) | async-done | bytes 9437200 | tf_op jit(solution)/shard_map/all_gather | solution.py:204
  115.1 25.4 %fusion.123 = f32[12,352,1408]{2,0,1:T(8,128)} fusion(s32[352,1408]{1,0:T(8,128)S(1)} %subtract_clamp_fusion, s32[32]{0:T(128)S(1)} %get-tuple-element.760, s32[32]{0:T(128)S(1)} %get-tuple-element.759, f32[32,12]{0,1:T(8,128)S(1)} %copy-done.68), kind=kOutput, calls=%fused_computation.152 | convolution fusion | flops 2331377664 | bytes 25773824 | tf_op jit(solution)/shard_map/qkb,bh->hqk/dot_general | solution.py:232
  140.6 25.4 %copy.140 = f32[12,352,1408]{2,1,0:T(8,128)} copy(f32[12,352,1408]{2,0,1:T(8,128)} %fusion.123) | data formatting | bytes 47579136
  188.9 67.0 %while.62 = (s32[]{:T(128)}, bf16[12,1,352,64]{2,3,1,0:T(8,128)(2,1)S(1)}, f32[12,1,352]{2,1,0:T(1,128)}, f32[12,1,352]{2,1,0:T(1,128)}, bf16[12,1,352,64]{3,2,1...) while((s32[]{:T(128)}, ...), condition=%wide.region_5.6_spmd.clone, body=%wide.region_2.5_spmd.clone.sunk | while | flops 134333760 | bytes 8821257 | solution.py:94
  262.7 8.8 copy.143
  271.5 12.0 copy.146
  292.2 12.2 copy.147
  304.5 77.0 %while.63 = (s32[]{:T(128)}, bf16[12,1,352,64]{2,3,1,0:T(8,128)(2,1)S(1)}, f32[12,1,352]{2,1,0:T(1,128)S(1)}, f32[12,1,352]{2,1,0:T(1,128)S(1)}, bf16[12,1,352,6...) while((s32[]{:T(128)}, ...), condition=%wide.region_10.11_spmd.clone, body=%wide.region_7.10_spmd.clone.sunk | while | flops 383538496 | bytes 19578104 | solution.py:94
  407.2 201.5 %while.64 = (s32[]{:T(128)}, bf16[12,1,352,64]{2,3,1,0:T(8,128)(2,1)S(1)}, f32[12,1,4096,64]{2,3,1,0:T(8,128)}, f32[12,1,4096,64]{2,3,1,0:T(8,128)}, bf16[12,1,3...) while((s32[]{:T(128)}, ...), condition=%wide.region_15.16_spmd.clone, body=%wide.region_13.15_spmd.clone.sunk | while | flops 944658048 | bytes 48934416 | solution.py:137
  617.3 621.6 %while.65 = (s32[]{:T(128)}, bf16[12,1,352,64]{2,3,1,0:T(8,128)(2,1)}, f32[12,352,1408]{2,0,1:T(8,128)}, f32[12,1,1408,64]{2,3,1,0:T(8,128)}, f32[12,1,1408,64]{...) while((s32[]{:T(128)}, ...), condition=%wide.region_19.20_spmd.clone, body=%wide.region_17.19_spmd.clone.sunk | while | flops 329201312 | bytes 26009908 | solution.py:137
  632.4 37.0 %dynamic_update_slice.91 = f32[12,352,1408]{2,0,1:T(8,128)} dynamic-update-slice(f32[12,352,1408]{2,0,1:T(8,128)} %get-tuple-element.1244, f32[1,352,1408]{2,0,1:T(1,128)S(1)} %copy.223, s32[]{:T(128)S(6)} %copy.278, s32[]{:T(128)} %constant.103.clone.1..sunk, s32[]{:T(128)} %constant.103.clone.1..sunk) | dynamic-update-slice | bytes 3964932 | tf_op jit(solution)/shard_map/while/body/jit(dynamic_update_index_in_dim)/dynamic_update_slice | solution.py:137
  684.2 37.0 %dynamic_update_slice.91 = f32[12,352,1408]{2,0,1:T(8,128)} dynamic-update-slice(f32[12,352,1408]{2,0,1:T(8,128)} %get-tuple-element.1244, f32[1,352,1408]{2,0,1:T(1,128)S(1)} %copy.223, s32[]{:T(128)S(6)} %copy.278, s32[]{:T(128)} %constant.103.clone.1..sunk, s32[]{:T(128)} %constant.103.clone.1..sunk) | dynamic-update-slice | bytes 3964932 | tf_op jit(solution)/shard_map/while/body/jit(dynamic_update_index_in_dim)/dynamic_update_slice | solution.py:137
  736.0 37.0 %dynamic_update_slice.91 = f32[12,352,1408]{2,0,1:T(8,128)} dynamic-update-slice(f32[12,352,1408]{2,0,1:T(8,128)} %get-tuple-element.1244, f32[1,352,1408]{2,0,1:T(1,128)S(1)} %copy.223, s32[]{:T(128)S(6)} %copy.278, s32[]{:T(128)} %constant.103.clone.1..sunk, s32[]{:T(128)} %constant.103.clone.1..sunk) | dynamic-update-slice | bytes 3964932 | tf_op jit(solution)/shard_map/while/body/jit(dynamic_update_index_in_dim)/dynamic_update_slice | solution.py:137
  787.7 37.0 %dynamic_update_slice.91 = f32[12,352,1408]{2,0,1:T(8,128)} dynamic-update-slice(f32[12,352,1408]{2,0,1:T(8,128)} %get-tuple-element.1244, f32[1,352,1408]{2,0,1:T(1,128)S(1)} %copy.223, s32[]{:T(128)S(6)} %copy.278, s32[]{:T(128)} %constant.103.clone.1..sunk, s32[]{:T(128)} %constant.103.clone.1..sunk) | dynamic-update-slice | bytes 3964932 | tf_op jit(solution)/shard_map/while/body/jit(dynamic_update_index_in_dim)/dynamic_update_slice | solution.py:137
  839.5 37.0 %dynamic_update_slice.91 = f32[12,352,1408]{2,0,1:T(8,128)} dynamic-update-slice(f32[12,352,1408]{2,0,1:T(8,128)} %get-tuple-element.1244, f32[1,352,1408]{2,0,1:T(1,128)S(1)} %copy.223, s32[]{:T(128)S(6)} %copy.278, s32[]{:T(128)} %constant.103.clone.1..sunk, s32[]{:T(128)} %constant.103.clone.1..sunk) | dynamic-update-slice | bytes 3964932 | tf_op jit(solution)/shard_map/while/body/jit(dynamic_update_index_in_dim)/dynamic_update_slice | solution.py:137
  891.2 37.0 %dynamic_update_slice.91 = f32[12,352,1408]{2,0,1:T(8,128)} dynamic-update-slice(f32[12,352,1408]{2,0,1:T(8,128)} %get-tuple-element.1244, f32[1,352,1408]{2,0,1:T(1,128)S(1)} %copy.223, s32[]{:T(128)S(6)} %copy.278, s32[]{:T(128)} %constant.103.clone.1..sunk, s32[]{:T(128)} %constant.103.clone.1..sunk) | dynamic-update-slice | bytes 3964932 | tf_op jit(solution)/shard_map/while/body/jit(dynamic_update_index_in_dim)/dynamic_update_slice | solution.py:137
  943.0 37.0 %dynamic_update_slice.91 = f32[12,352,1408]{2,0,1:T(8,128)} dynamic-update-slice(f32[12,352,1408]{2,0,1:T(8,128)} %get-tuple-element.1244, f32[1,352,1408]{2,0,1:T(1,128)S(1)} %copy.223, s32[]{:T(128)S(6)} %copy.278, s32[]{:T(128)} %constant.103.clone.1..sunk, s32[]{:T(128)} %constant.103.clone.1..sunk) | dynamic-update-slice | bytes 3964932 | tf_op jit(solution)/shard_map/while/body/jit(dynamic_update_index_in_dim)/dynamic_update_slice | solution.py:137
  994.8 37.0 %dynamic_update_slice.91 = f32[12,352,1408]{2,0,1:T(8,128)} dynamic-update-slice(f32[12,352,1408]{2,0,1:T(8,128)} %get-tuple-element.1244, f32[1,352,1408]{2,0,1:T(1,128)S(1)} %copy.223, s32[]{:T(128)S(6)} %copy.278, s32[]{:T(128)} %constant.103.clone.1..sunk, s32[]{:T(128)} %constant.103.clone.1..sunk) | dynamic-update-slice | bytes 3964932 | tf_op jit(solution)/shard_map/while/body/jit(dynamic_update_index_in_dim)/dynamic_update_slice | solution.py:137
  1046.6 37.0 %dynamic_update_slice.91 = f32[12,352,1408]{2,0,1:T(8,128)} dynamic-update-slice(f32[12,352,1408]{2,0,1:T(8,128)} %get-tuple-element.1244, f32[1,352,1408]{2,0,1:T(1,128)S(1)} %copy.223, s32[]{:T(128)S(6)} %copy.278, s32[]{:T(128)} %constant.103.clone.1..sunk, s32[]{:T(128)} %constant.103.clone.1..sunk) | dynamic-update-slice | bytes 3964932 | tf_op jit(solution)/shard_map/while/body/jit(dynamic_update_index_in_dim)/dynamic_update_slice | solution.py:137
  1098.3 37.0 %dynamic_update_slice.91 = f32[12,352,1408]{2,0,1:T(8,128)} dynamic-update-slice(f32[12,352,1408]{2,0,1:T(8,128)} %get-tuple-element.1244, f32[1,352,1408]{2,0,1:T(1,128)S(1)} %copy.223, s32[]{:T(128)S(6)} %copy.278, s32[]{:T(128)} %constant.103.clone.1..sunk, s32[]{:T(128)} %constant.103.clone.1..sunk) | dynamic-update-slice | bytes 3964932 | tf_op jit(solution)/shard_map/while/body/jit(dynamic_update_index_in_dim)/dynamic_update_slice | solution.py:137
  1150.1 37.0 %dynamic_update_slice.91 = f32[12,352,1408]{2,0,1:T(8,128)} dynamic-update-slice(f32[12,352,1408]{2,0,1:T(8,128)} %get-tuple-element.1244, f32[1,352,1408]{2,0,1:T(1,128)S(1)} %copy.223, s32[]{:T(128)S(6)} %copy.278, s32[]{:T(128)} %constant.103.clone.1..sunk, s32[]{:T(128)} %constant.103.clone.1..sunk) | dynamic-update-slice | bytes 3964932 | tf_op jit(solution)/shard_map/while/body/jit(dynamic_update_index_in_dim)/dynamic_update_slice | solution.py:137
  1201.9 37.0 %dynamic_update_slice.91 = f32[12,352,1408]{2,0,1:T(8,128)} dynamic-update-slice(f32[12,352,1408]{2,0,1:T(8,128)} %get-tuple-element.1244, f32[1,352,1408]{2,0,1:T(1,128)S(1)} %copy.223, s32[]{:T(128)S(6)} %copy.278, s32[]{:T(128)} %constant.103.clone.1..sunk, s32[]{:T(128)} %constant.103.clone.1..sunk) | dynamic-update-slice | bytes 3964932 | tf_op jit(solution)/shard_map/while/body/jit(dynamic_update_index_in_dim)/dynamic_update_slice | solution.py:137
  1250.7 13.2 copy.168
  1264.0 12.6 copy.166
  1299.2 37.9 %reduce-scatter.8.cloned.1.call-done = f32[1,352,768]{2,1,0:T(8,128)} async-done(((f32[1,1408,768]{2,1,0:T(8,128)}), f32[1,352,768]{2,1,0:T(8,128)}) %reduce-scatter.8.cloned.1.call-update) | async-done | bytes 1081360 | tf_op jit(solution)/shard_map/reduce_scatter | solution.py:319
  1349.6 89.0 %reduce-scatter.14.cloned.1.call-done = f32[1,1024,768]{2,1,0:T(8,128)} async-done(((f32[1,4096,768]{2,1,0:T(8,128)}), f32[1,1024,768]{2,1,0:T(8,128)}) %reduce-scatter.14.cloned.1.call-update) | async-done | bytes 3145744 | tf_op jit(solution)/shard_map/reduce_scatter | solution.py:294
  1441.9 98.5 %reduce-scatter.12.cloned.1.call-done = f32[1,1024,768]{2,1,0:T(8,128)} async-done(((f32[1,4096,768]{2,1,0:T(8,128)}), f32[1,1024,768]{2,1,0:T(8,128)}) %reduce-scatter.12.cloned.1.call-update) | async-done | bytes 3145744 | tf_op jit(solution)/shard_map/reduce_scatter | solution.py:293
  1557.8 39.7 %fusion.185 = f32[32,12]{0,1:T(8,128)} fusion(f32[12,352,1408]{2,0,1:T(8,128)} %get-tuple-element.260, s32[352,1408]{1,0:T(8,128)S(1)} %copy-done.23, s32[32]{0:T(128)S(1)} %copy-done.87, s32[32]{0:T(128)S(1)} %copy-done.85), kind=kOutput, calls=%fused_computation.237 | convolution fusion | flops 2331377664 | bytes 25773824 | tf_op jit(solution)/shard_map/hqk,qkb->bh/dot_general | solution.py:329
  1597.6 63.4 %reduce-scatter.20.cloned.1.call-done = f32[64,768]{1,0:T(8,128)} async-done(((f32[2048,768]{1,0:T(8,128)}), f32[64,768]{1,0:T(8,128)}) %reduce-scatter.20.cloned.1.call-update) | async-done | bytes 196624 | tf_op jit(solution)/shard_map/reduce_scatter | solution.py:343
  1669.8 152.9 %reduce-scatter.18.cloned.1.call-done = f32[24,2,2048]{2,0,1:T(8,128)} async-done(((f32[768,2,2048]{2,0,1:T(8,128)}), f32[24,2,2048]{2,0,1:T(8,128)}) %reduce-scatter.18.cloned.1.call-update) | async-done | bytes 393232 | tf_op jit(solution)/shard_map/reduce_scatter | solution.py:342
  1834.1 199.1 %reduce-scatter.16.cloned.1.call-done = f32[24,8,768]{2,0,1:T(8,128)} async-done(((f32[768,8,768]{2,0,1:T(8,128)}), f32[24,8,768]{2,0,1:T(8,128)}) %reduce-scatter.16.cloned.1.call-update) | async-done | bytes 589840 | tf_op jit(solution)/shard_map/reduce_scatter | solution.py:341
  2037.0 41.2 %all-reduce = (f32[8,768]{1,0:T(8,128)}, f32[8]{0:T(128)}, f32[2,2048]{1,0:T(2,128)}, f32[2]{0:T(128)}, f32[1,768]{1,0:T(1,128)}, /*index=5*/f32[1]{0:T(128)}, f32[3,768]{1,0:T(4,128)}, f32[32,12]{0,1:T(8,128)}) all-reduce(f32[8,768]{1,0:T(8,128)} %get-tuple-element.599, ...), channel_id=1, replica_groups=mesh['rows'=8,'seq'=4] {'rows','seq'}, use_global_device_ids=true, to_apply=%region_28.29 | all-reduce | flops 13707 | bytes 109656 | tf_op jit(solution)/shard_map/psum | solution.py:353
  (591 shorter events, 720.9 us)
Async XLA Ops:
  7.2 94.8 %copy-start = (bf16[1,1024,768]{2,1,0:T(8,128)(2,1)S(1)}, bf16[1,1024,768]{2,1,0:T(8,128)(2,1)}, u32[]{:S(2)}) copy-start(bf16[1,1024,768]{2,1,0:T(8,128)(2,1)} %param.35) | copy-start | bytes 4718596
  7.2 89.1 %all-gather.12.cloned.1.call-start = ((), (), s32[]{:S(2)}) async-start(), calls=%async_computation.7 | async-start | bytes 9732096 | tf_op jit(solution)/shard_map/all_gather | solution.py:204
  9.3 158.3 %all-gather.18.cloned.1.call-start = ((), (), s32[]{:S(2)}) async-start(), calls=%async_computation.17 | async-start | bytes 2703360 | tf_op jit(solution)/shard_map/all_gather | solution.py:213
  10.8 89.2 %copy-start.60 = (f32[768]{0:T(1024)}, f32[768]{0:T(1024)S(1)}, u32[]{:S(2)}) copy-start(f32[768]{0:T(1024)S(1)} %get-tuple-element.607) | copy-start | bytes 9220
  10.8 247.3 %copy-start.46 = (f32[768]{0:T(1024)}, f32[768]{0:T(1024)S(1)}, u32[]{:S(2)}) copy-start(f32[768]{0:T(1024)S(1)} %get-tuple-element.606) | copy-start | bytes 9220
  12.7 87.4 %copy-start.66 = (f32[352]{0:T(512)}, f32[352]{0:T(512)S(1)}, u32[]{:S(2)}) copy-start(f32[352]{0:T(512)S(1)} %fusion.219) | copy-start | bytes 4228
  101.2 76.4 %all-gather.20.cloned.1.call-start = ((), (), s32[]{:S(2)}) async-start(), calls=%async_computation.18 | async-start | bytes 2703360 | tf_op jit(solution)/shard_map/all_gather | solution.py:214
  101.9 160.8 %all-gather.22.cloned.1.call-start = ((), (), s32[]{:S(2)}) async-start(), calls=%async_computation.19 | async-start | bytes 7864320 | tf_op jit(solution)/shard_map/all_gather | solution.py:246
  108.4 175.1 %all-gather.24.cloned.1.call-start = ((), (), s32[]{:S(2)}) async-start(), calls=%async_computation.20 | async-start | bytes 7864320 | tf_op jit(solution)/shard_map/all_gather | solution.py:247
  109.0 275.1 %all-gather.14.cloned.1.call-start = ((), (), s32[]{:S(2)}) async-start(), calls=%async_computation.8 | async-start | bytes 6488064 | tf_op jit(solution)/shard_map/all_gather | solution.py:205
  110.2 281.9 %all-gather.16.cloned.1.call-start = ((), (), s32[]{:S(2)}) async-start(), calls=%async_computation.9 | async-start | bytes 3244032 | tf_op jit(solution)/shard_map/all_gather | solution.py:206
  111.0 1186.1 %reduce-scatter.10.cloned.1.call-start = ((), (), s32[]{:S(2)}) async-start(), calls=%async_computation.11 | async-start | bytes 5406720 | tf_op jit(solution)/shard_map/reduce_scatter | solution.py:320
  112.1 28.5 %copy-start.86 = (s32[32]{0:T(128)}, s32[32]{0:T(128)S(1)}, u32[]{:S(2)}) copy-start(s32[32]{0:T(128)S(1)} %get-tuple-element.760) | copy-start | bytes 388
  188.9 67.0 %copy-start.20 = (bf16[1,352,768]{2,1,0:T(8,128)(2,1)S(1)}, bf16[1,352,768]{2,1,0:T(8,128)(2,1)}, u32[]{:S(2)}) copy-start(bf16[1,352,768]{2,1,0:T(8,128)(2,1)} %param.34) | copy-start | bytes 1622020
  403.7 208.3 %copy-start.1 = (f32[1,352,768]{2,1,0:T(8,128)}, f32[1,352,768]{2,1,0:T(8,128)S(1)}, u32[]{:S(2)}) copy-start(f32[1,352,768]{2,1,0:T(8,128)S(1)} %fusion.188) | copy-start | bytes 3244036
  407.1 201.6 %copy-start.47 = (f32[768]{0:T(1024)S(1)}, f32[768]{0:T(1024)}, u32[]{:S(2)}) copy-start(f32[768]{0:T(1024)} %copy-done.46) | copy-start | bytes 9220
  407.2 201.6 %copy-start.52 = (f32[352]{0:T(512)S(1)}, f32[352]{0:T(512)}, u32[]{:S(2)}) copy-start(f32[352]{0:T(512)} %copy-done.51) | copy-start | bytes 4228
  1244.8 92.4 %reduce-scatter.8.cloned.1.call-start = ((), (), s32[]{:S(2)}) async-start(), calls=%async_computation.10 | async-start | bytes 5406720 | tf_op jit(solution)/shard_map/reduce_scatter | solution.py:319
  1250.7 188.0 %reduce-scatter.14.cloned.1.call-start = ((), (), s32[]{:S(2)}) async-start(), calls=%async_computation.13 | async-start | bytes 15728640 | tf_op jit(solution)/shard_map/reduce_scatter | solution.py:294
  1264.0 276.4 %reduce-scatter.12.cloned.1.call-start = ((), (), s32[]{:S(2)}) async-start(), calls=%async_computation.12 | async-start | bytes 15728640 | tf_op jit(solution)/shard_map/reduce_scatter | solution.py:293
  1276.6 384.4 %reduce-scatter.20.cloned.1.call-start = ((), (), s32[]{:S(2)}) async-start(), calls=%async_computation.16 | async-start | bytes 6488064 | tf_op jit(solution)/shard_map/reduce_scatter | solution.py:343
  1285.4 537.3 %reduce-scatter.18.cloned.1.call-start = ((), (), s32[]{:S(2)}) async-start(), calls=%async_computation.15 | async-start | bytes 12976128 | tf_op jit(solution)/shard_map/reduce_scatter | solution.py:342
  1294.9 43.6 %copy-start.21 = (bf16[1,352,768]{2,1,0:T(8,128)(2,1)S(1)}, bf16[1,352,768]{2,1,0:T(8,128)(2,1)}, u32[]{:S(2)}) copy-start(bf16[1,352,768]{2,1,0:T(8,128)(2,1)} %param.34) | copy-start | bytes 1622020
  1294.9 43.6 %copy-start.61 = (f32[768]{0:T(1024)S(1)}, f32[768]{0:T(1024)}, u32[]{:S(2)}) copy-start(f32[768]{0:T(1024)} %copy-done.60) | copy-start | bytes 9220
  1294.9 43.6 %copy-start.67 = (f32[352]{0:T(512)S(1)}, f32[352]{0:T(512)}, u32[]{:S(2)}) copy-start(f32[352]{0:T(512)} %copy-done.66) | copy-start | bytes 4228
  1294.9 738.3 %reduce-scatter.16.cloned.1.call-start = ((), (), s32[]{:S(2)}) async-start(), calls=%async_computation.14 | async-start | bytes 19464192 | tf_op jit(solution)/shard_map/reduce_scatter | solution.py:341
  1557.8 104.9 %copy-start.83 = (f32[64]{0:T(128)S(1)}, f32[64]{0:T(128)}, u32[]{:S(2)}) copy-start(f32[64]{0:T(128)} %param.52) | copy-start | bytes 772
  1667.9 158.0 %copy-start.82 = (f32[2,24]{1,0:T(2,128)S(1)}, f32[2,24]{1,0:T(2,128)}, u32[]{:S(2)}) copy-start(f32[2,24]{1,0:T(2,128)} %param.48) | copy-start | bytes 580
  1827.1 253.3 %copy-start.14 = (f32[24,2,2048]{2,0,1:T(8,128)S(1)}, f32[24,2,2048]{2,0,1:T(8,128)}, u32[]{:S(2)}) copy-start(f32[24,2,2048]{2,0,1:T(8,128)} %reduce-scatter.18.cloned.1.call-done) | copy-start | bytes 1179652
  1827.1 253.3 %copy-start.27 = (f32[24,2,2048]{2,1,0:T(2,128)S(1)}, f32[24,2,2048]{2,1,0:T(2,128)}, u32[]{:S(2)}) copy-start(f32[24,2,2048]{2,1,0:T(2,128)} %param.46) | copy-start | bytes 1179652
  1834.1 250.2 %copy-start.15 = (f32[24,8,768]{2,1,0:T(8,128)S(1)}, f32[24,8,768]{2,1,0:T(8,128)}, u32[]{:S(2)}) copy-start(f32[24,8,768]{2,1,0:T(8,128)} %param.42) | copy-start | bytes 1769476
  2033.2 51.1 %copy-start.13 = (f32[24,8,768]{2,0,1:T(8,128)S(1)}, f32[24,8,768]{2,0,1:T(8,128)}, u32[]{:S(2)}) copy-start(f32[24,8,768]{2,0,1:T(8,128)} %reduce-scatter.16.cloned.1.call-done) | copy-start | bytes 1769476
  (70 other events, 358.4 us)
Sparse Core Ops, SparseCore 0:
  11.6 84.7 all-gather.11
  101.3 21.5 all-gather.17
  125.0 22.9 all-gather.19
  149.4 46.3 all-gather.21
  197.2 46.3 all-gather.23
  246.9 69.6 all-gather.13
  320.0 57.4 all-gather.15
  1244.9 44.1 reduce-scatter.9
  1291.8 45.3 reduce-scatter.7
  1339.6 99.0 reduce-scatter.13
  1441.3 99.0 reduce-scatter.11
  1546.4 114.5 reduce-scatter.19
  1668.1 154.5 reduce-scatter.17
  1829.0 204.1 reduce-scatter.15
where the time goes:
time: 2120 us; the launch traced here: 2100 us
  waiting for transfers between devices  726 us (34%)
  local copies, waits for them, and re-layouts  635 us (30%)
  matrix products  567 us (27%)
  other arithmetic  110 us (5%)
  blocking collectives  41.2 us (2%)
    dynamic_update_slice x24, local copies, waits for them, and re-layouts, backward_heads(): return lax.map(head_grad, items)  462 us
    reduce_scatter x1, waiting for transfers between devices, shards(): lax.psum_scatter(attention_local, ('rows', 'seq'), scatter_dimension=0, t...  199 us
    dot_general x48, matrix products, scores(): jnp.einsum('rqd,rkd->rqk', queries, key_rows, preferred_element_type=jnp....  160 us
    reduce_scatter x1, waiting for transfers between devices, shards(): lax.psum_scatter(expand_local, ('rows', 'seq'), scatter_dimension=0, tile...  153 us
    reduce_scatter x1, waiting for transfers between devices, shards(): lax.psum_scatter(merge_heads(cross_kparts), 'seq', scatter_dimension=1, t...  98.5 us
    reduce_scatter x1, waiting for transfers between devices, shards(): lax.psum_scatter(merge_heads(cross_vparts), 'seq', scatter_dimension=1, t...  89 us
    all_gather x1, waiting for transfers between devices, shards(): lax.all_gather(attention_weight.astype(jnp.bfloat16), ('rows', 'seq'), ax...  83.7 us
    unnamed x191, local copies, waits for them, and re-layouts  80.3 us
  transfers between devices with their start and end apart: 14, of which 7 were waited for; matrix products, arithmetic and copies ran while one was open for 21% of the time, Pallas kernels for 0%

commit v1 on v0

v1 whole, which is shorter than its diff:
```python
import jax
import jax.numpy as jnp
from jax import lax
from jax.experimental import pallas as pl
from jax.experimental.pallas import tpu as pltpu
from jax.sharding import PartitionSpec as P

D = 768
FF = 2048
HEADS = 12
BUCKETS = 32
STEP = 10
HIGHEST = lax.Precision.HIGHEST
NORM_EPS = 1e-06
BETA_ONE = 0.9
BETA_TWO = 0.999
ADAM_EPS = 1e-08
WEIGHT_DECAY = 0.01
MATRIX_RATE = 0.15
VECTOR_RATE = 1.0
HD = 64
NEG = -1e30
F32 = jnp.float32
BF = jnp.bfloat16

def nt(a,b): return lax.dot_general(a,b,(((1,),(1,)),((),())),preferred_element_type=F32)
def nn(a,b): return lax.dot_general(a,b,(((1,),(0,)),((),())),preferred_element_type=F32)
def tn(a,b): return lax.dot_general(a,b,(((0,),(0,)),((),())),preferred_element_type=F32)

def cross_fwd(q,k,v,qa,ka,qb=352,kc=1024):
    Lq,W=q.shape; Lk=k.shape[0]; H=W//HD
    nk=Lk//kc
    def kern(q_ref,k_ref,v_ref,qa_ref,ka_ref,o_ref,of_ref,lse_ref,kaug,vs,s_s,m_s,l_s,acc):
        @pl.when(pl.program_id(0)==0)
        def _():
            for h in range(H):
                kaug[h,:,0:HD]=k_ref[:,h*HD:(h+1)*HD]
                kaug[h,:,HD:2*HD]=ka_ref[...]
                vs[h]=v_ref[:,h*HD:(h+1)*HD]
        lane=lax.broadcasted_iota(jnp.int32,(qb,128),1)
        lses=jnp.zeros((qb,128),F32)
        outs=[]
        for h in range(H):
            qh=(q_ref[:,h*HD:(h+1)*HD]*BF(0.125)).astype(BF)
            qg=jnp.concatenate([qh,qa_ref[...]],axis=1)
            m_s[...]=jnp.full((qb,128),-3e38,F32)
            for c in range(nk):
                s=nt(qg,kaug[h,c*kc:(c+1)*kc,:])
                s_s[:,c*kc:(c+1)*kc]=s
                mm=m_s[...]
                for t in range(kc//128): mm=jnp.maximum(mm,s[:,t*128:(t+1)*128])
                m_s[...]=mm
            m=jnp.max(m_s[...],axis=1,keepdims=True)
            l_s[...]=jnp.zeros((qb,128),F32)
            acc[...]=jnp.zeros((qb,HD),F32)
            for c in range(nk):
                p=jnp.exp(s_s[:,c*kc:(c+1)*kc]-m)
                ll=l_s[...]
                for t in range(kc//128): ll=ll+p[:,t*128:(t+1)*128]
                l_s[...]=ll
                acc[...]+=nn(p.astype(BF),vs[h,c*kc:(c+1)*kc,:])
            l=jnp.sum(l_s[...],axis=1,keepdims=True)
            o=acc[...]/l
            outs.append(o)
            lses=jnp.where(lane==h,m+jnp.log(l),lses)
        oo=jnp.concatenate(outs,axis=1)
        o_ref[...]=oo.astype(BF)
        of_ref[...]=oo
        lse_ref[...]=lses
    full=lambda s: pl.BlockSpec(s,lambda i:(0,)*len(s))
    row=lambda w: pl.BlockSpec((qb,w),lambda i:(i,0))
    return pl.pallas_call(kern,grid=(Lq//qb,),
        out_shape=(jax.ShapeDtypeStruct((Lq,W),BF),jax.ShapeDtypeStruct((Lq,W),F32),jax.ShapeDtypeStruct((Lq,128),F32)),
        in_specs=[row(W),full((Lk,W)),full((Lk,W)),row(HD),full((Lk,HD))],
        out_specs=(row(W),row(W),row(128)),
        scratch_shapes=[pltpu.VMEM((H,Lk,2*HD),BF),pltpu.VMEM((H,Lk,HD),BF),pltpu.VMEM((qb,Lk),F32),pltpu.VMEM((qb,128),F32),pltpu.VMEM((qb,128),F32),pltpu.VMEM((qb,HD),F32)],
        compiler_params=pltpu.CompilerParams(vmem_limit_bytes=56*2**20),name="cross_fwd")(q,k,v,qa,ka)

def split3(x):
    a=x.astype(BF); r=x-a.astype(F32)
    b=r.astype(BF); c=(r-b.astype(F32)).astype(BF)
    return a,b,c

def cross_bwd(q,k,v,do,of,lse,qa,ka,qb=256,kc=1024):
    Lq,W=q.shape; Lk=k.shape[0]; H=W//HD
    nq=-(-Lq//qb); Lp=nq*qb; nk=Lk//kc
    def kern(q_ref,k_ref,v_ref,do_ref,of_ref,lse_ref,qa_ref,ka_ref,dq_ref,dk_ref,dv_ref,kaug,vaug,qaug,doaug,dkacc,dvacc,dqs,dks,dvs):
        h=pl.program_id(0); i=pl.program_id(1)
        for hh in range(H):
            @pl.when((h==hh)&(i==0))
            def _():
                sl=slice(hh*HD,(hh+1)*HD)
                kaug[:,0:HD]=k_ref[:,sl]
                lane=lax.broadcasted_iota(jnp.int32,(Lk,HD),1)
                kaug[:,HD:2*HD]=jnp.where((lane>=3)&(lane<6),BF(1),ka_ref[...])
                vaug[:,0:HD]=v_ref[:,sl]
                vaug[:,HD:2*HD]=jnp.where(lane<3,BF(1),BF(0)).astype(BF)
                lq=lax.broadcasted_iota(jnp.int32,(Lq,HD),1)
                a,b,c=split3(-lse_ref[:,hh:hh+1])
                aug=jnp.where(lq==3,a,jnp.where(lq==4,b,jnp.where(lq==5,c,qa_ref[...])))
                qaug[0:Lq,0:HD]=q_ref[:,sl]*BF(0.125)
                qaug[0:Lq,HD:2*HD]=aug
                dd=do_ref[:,sl]
                delta=jnp.sum(dd.astype(F32)*of_ref[:,sl],axis=1,keepdims=True)
                a,b,c=split3(-delta)
                aug=jnp.where(lq==0,a,jnp.where(lq==1,b,jnp.where(lq==2,c,BF(0))))
                doaug[0:Lq,0:HD]=dd
                doaug[0:Lq,HD:2*HD]=aug
                if Lp>Lq:
                    qaug[Lq:Lp,:]=jnp.zeros((Lp-Lq,2*HD),BF)
                    doaug[Lq:Lp,:]=jnp.zeros((Lp-Lq,2*HD),BF)
                dkacc[...]=jnp.zeros_like(dkacc)
                dvacc[...]=jnp.zeros_like(dvacc)
        off=pl.multiple_of(i*qb,qb)
        qg=qaug[pl.ds(off,qb),:]
        dg=doaug[pl.ds(off,qb),:]
        qp=qg[:,0:HD]; dp_=dg[:,0:HD]
        dq=jnp.zeros((qb,HD),F32)
        def step(c,dq):
            o=pl.multiple_of(c*kc,kc)
            kk=kaug[pl.ds(o,kc),:]
            p=jnp.exp(nt(kk,qg))
            g=nt(vaug[pl.ds(o,kc),:],dg)
            ds=(p*g).astype(BF)
            dvacc[pl.ds(o,kc),:]+=nn(p.astype(BF),dp_)
            dkacc[pl.ds(o,kc),:]+=nn(ds,qp)
            return dq+tn(ds,kk[:,0:HD])
        for c in range(nk): dq=step(c,dq)
        dqs[h,pl.ds(off,qb),:]=(dq*0.125).astype(BF)
        @pl.when(i==nq-1)
        def _():
            dks[h]=dkacc[...].astype(BF)
            dvs[h]=dvacc[...].astype(BF)
        @pl.when((i==nq-1)&(h==H-1))
        def _():
            dq_ref[...]=jnp.concatenate([dqs[t,0:Lq,:] for t in range(H)],axis=1)
            dk_ref[...]=jnp.concatenate([dks[t] for t in range(H)],axis=1)
            dv_ref[...]=jnp.concatenate([dvs[t] for t in range(H)],axis=1)
    full=lambda s: pl.BlockSpec(s,lambda h,i:(0,)*len(s))
    return pl.pallas_call(kern,grid=(H,nq),
        out_shape=(jax.ShapeDtypeStruct((Lq,W),BF),jax.ShapeDtypeStruct((Lk,W),BF),jax.ShapeDtypeStruct((Lk,W),BF)),
        in_specs=[full((Lq,W)),full((Lk,W)),full((Lk,W)),full((Lq,W)),full((Lq,W)),full((Lq,128)),full((Lq,HD)),full((Lk,HD))],
        out_specs=(full((Lq,W)),full((Lk,W)),full((Lk,W))),
        scratch_shapes=[pltpu.VMEM((Lk,2*HD),BF),pltpu.VMEM((Lk,2*HD),BF),pltpu.VMEM((Lp,2*HD),BF),pltpu.VMEM((Lp,2*HD),BF),
            pltpu.VMEM((Lk,HD),F32),pltpu.VMEM((Lk,HD),F32),pltpu.VMEM((H,Lp,HD),BF),pltpu.VMEM((H,Lk,HD),BF),pltpu.VMEM((H,Lk,HD),BF)],
        compiler_params=pltpu.CompilerParams(vmem_limit_bytes=60*2**20),name="cross_bwd")(q,k,v,do,of,lse,qa,ka)

def toeplitz(win, shift):
    x=jnp.broadcast_to(win,(128,256))
    return pltpu.roll(x,shift,1,stride=1,stride_axis=0)[:,0:128]

def eye128():
    return lax.broadcasted_iota(jnp.int32,(128,128),0)==lax.broadcasted_iota(jnp.int32,(128,128),1)

def self_fwd(q,k,v,rev,qa,ka):
    Lq,W=q.shape; H=W//HD; nb=Lq//128
    def kern(q_ref,k_ref,v_ref,rev_ref,qa_ref,ka_ref,o_ref,of_ref,lse_ref,qaug,kaug,kdiag,vs,os,tz):
        h=pl.program_id(0)
        for hh in range(H):
            @pl.when(h==hh)
            def _():
                sl=slice(hh*HD,(hh+1)*HD)
                qaug[:,0:HD]=q_ref[:,sl]*BF(0.125); qaug[:,HD:]=qa_ref[...]
                kaug[:,0:HD]=k_ref[:,sl]; kaug[:,HD:]=ka_ref[...]
                kdiag[:,0:HD]=k_ref[:,sl]; kdiag[:,HD:]=jnp.zeros((Lq,HD),BF)
                vs[...]=v_ref[:,sl]
        @pl.when(h==0)
        def _():
            lse_ref[...]=jnp.zeros((Lq,128),F32)
        for d in range(nb):
            tz[d]=toeplitz(rev_ref[pl.ds(h,1),(nb-1-d)*128:(nb+1-d)*128],129)
        eye=eye128()
        lane=lax.broadcasted_iota(jnp.int32,(128,128),1)
        for q0 in range(0,Lq,256):
            qn=min(256,Lq-q0); kend=q0+qn
            s=nt(qaug[q0:q0+qn,:],kaug[0:kend,:])
            for a in range(qn//128):
                qt=q0//128+a
                r0=q0+a*128
                rows=slice(r0,r0+128)
                sd=nt(qaug[rows,:],kdiag[rows,:])
                tiles=[]
                for b in range(qt+1):
                    t=s[a*128:(a+1)*128,b*128:(b+1)*128]
                    if b==qt: t=jnp.where(eye,sd,t)
                    tiles.append(t+tz[qt-b])
                m=tiles[0]
                for t in tiles[1:]: m=jnp.maximum(m,t)
                m=jnp.max(m,axis=1,keepdims=True)
                ps=[jnp.exp(t-m) for t in tiles]
                l=ps[0]
                for t in ps[1:]: l=l+t
                l=jnp.sum(l,axis=1,keepdims=True)
                pb=jnp.concatenate([t.astype(BF) for t in ps],axis=1)
                os[h,rows,:]=nn(pb,vs[0:(qt+1)*128,:])/l
                lse_ref[rows,:]=jnp.where(lane==h,m+jnp.log(l),lse_ref[rows,:])
        @pl.when(h==H-1)
        def _():
            oo=jnp.concatenate([os[t] for t in range(H)],axis=1)
            o_ref[...]=oo.astype(BF)
            of_ref[...]=oo
    full=lambda s: pl.BlockSpec(s,lambda h:(0,)*len(s))
    return pl.pallas_call(kern,grid=(H,),
        out_shape=(jax.ShapeDtypeStruct((Lq,W),BF),jax.ShapeDtypeStruct((Lq,W),F32),jax.ShapeDtypeStruct((Lq,128),F32)),
        in_specs=[full((Lq,W)),full((Lq,W)),full((Lq,W)),full(rev.shape),full((Lq,HD)),full((Lq,HD))],
        out_specs=(full((Lq,W)),full((Lq,W)),full((Lq,128))),
        scratch_shapes=[pltpu.VMEM((Lq,2*HD),BF)]*3+[pltpu.VMEM((Lq,HD),BF),pltpu.VMEM((H,Lq,HD),F32),pltpu.VMEM((nb,128,128),F32)],
        compiler_params=pltpu.CompilerParams(vmem_limit_bytes=48*2**20),name="self_fwd")(q,k,v,rev,qa,ka)

def self_bwd(q,k,v,do,of,lse,fwd,qa,ka):
    Lq,W=q.shape; H=W//HD; nb=Lq//128
    def kern(q_ref,k_ref,v_ref,do_ref,of_ref,lse_ref,fwd_ref,qa_ref,ka_ref,dq_ref,dk_ref,dv_ref,gb_ref,qaug,kaug,kdiag,vaug,doaug,dkacc,dvacc,dqs,dks,dvs,tz,ga):
        h=pl.program_id(0)
        for hh in range(H):
            @pl.when(h==hh)
            def _():
                sl=slice(hh*HD,(hh+1)*HD)
                lane=lax.broadcasted_iota(jnp.int32,(Lq,HD),1)
                kaug[:,0:HD]=k_ref[:,sl]
                ones=(lane>=3)&(lane<6)
                kaug[:,HD:]=jnp.where(ones,BF(1),ka_ref[...])
                kdiag[:,0:HD]=k_ref[:,sl]
                kdiag[:,HD:]=jnp.where(ones,BF(1),BF(0)).astype(BF)
                vaug[:,0:HD]=v_ref[:,sl]
                vaug[:,HD:]=jnp.where(lane<3,BF(1),BF(0)).astype(BF)
                a,b,c=split3(-lse_ref[:,hh:hh+1])
                qaug[:,0:HD]=q_ref[:,sl]*BF(0.125)
                qaug[:,HD:]=jnp.where(lane==3,a,jnp.where(lane==4,b,jnp.where(lane==5,c,qa_ref[...])))
                dd=do_ref[:,sl]
                delta=jnp.sum(dd.astype(F32)*of_ref[:,sl],axis=1,keepdims=True)
                a,b,c=split3(-delta)
                doaug[:,0:HD]=dd
                doaug[:,HD:]=jnp.where(lane==0,a,jnp.where(lane==1,b,jnp.where(lane==2,c,BF(0))))
        dkacc[...]=jnp.zeros_like(dkacc)
        dvacc[...]=jnp.zeros_like(dvacc)
        ga[...]=jnp.zeros_like(ga)
        for d in range(nb):
            tz[d]=toeplitz(fwd_ref[pl.ds(h,1),d*128:(d+2)*128],128)
        eye=eye128()
        for q0 in range(0,Lq,256):
            qn=min(256,Lq-q0); kend=q0+qn
            qg=qaug[q0:kend,:]; dg=doaug[q0:kend,:]
            s=nt(kaug[0:kend,:],qg)
            g=nt(vaug[0:kend,:],dg)
            pcols=[]; dcols=[]
            for a in range(qn//128):
                qt=q0//128+a
                rows=slice(q0+a*128,q0+(a+1)*128)
                sd=nt(kdiag[rows,:],qaug[rows,:])
                pt=[]; dt=[]
                for b in range(kend//128):
                    d=qt-b
                    if d<0:
                        pt.append(jnp.zeros((128,128),BF)); dt.append(jnp.zeros((128,128),BF)); continue
                    t=s[b*128:(b+1)*128,a*128:(a+1)*128]
                    if d==0: t=jnp.where(eye,sd,t)
                    p=jnp.exp(t+tz[d])
                    ds=(p*g[b*128:(b+1)*128,a*128:(a+1)*128]).astype(BF)
                    ga[d]+=ds.astype(F32)
                    pt.append(p.astype(BF)); dt.append(ds)
                pcols.append(jnp.concatenate(pt,axis=0)); dcols.append(jnp.concatenate(dt,axis=0))
            P=jnp.concatenate(pcols,axis=1); DS=jnp.concatenate(dcols,axis=1)
            dvacc[0:kend,:]+=nn(P,dg[:,0:HD])
            dkacc[0:kend,:]+=nn(DS,qg[:,0:HD])
            dqs[h,q0:kend,:]=(tn(DS,kaug[0:kend,0:HD])*0.125).astype(BF)
        dks[h]=dkacc[...].astype(BF)
        dvs[h]=dvacc[...].astype(BF)
        flip=(lax.broadcasted_iota(jnp.int32,(128,128),0)+lax.broadcasted_iota(jnp.int32,(128,128),1)==127).astype(F32)
        for d in range(nb):
            y=lax.dot_general(flip,ga[d],(((1,),(0,)),((),())),preferred_element_type=F32,precision=lax.Precision.HIGHEST)
            x=pltpu.roll(jnp.concatenate([y,jnp.zeros((128,128),F32)],axis=1),1,1,stride=1,stride_axis=0)
            gb_ref[pl.ds(h,1),d*256:(d+1)*256]=jnp.sum(x,axis=0,keepdims=True)
        @pl.when(h==H-1)
        def _():
            dq_ref[...]=jnp.concatenate([dqs[t] for t in range(H)],axis=1)
            dk_ref[...]=jnp.concatenate([dks[t] for t in range(H)],axis=1)
            dv_ref[...]=jnp.concatenate([dvs[t] for t in range(H)],axis=1)
    full=lambda s: pl.BlockSpec(s,lambda h:(0,)*len(s))
    return pl.pallas_call(kern,grid=(H,),
        out_shape=(jax.ShapeDtypeStruct((Lq,W),BF),)*3+(jax.ShapeDtypeStruct((H,nb*256),F32),),
        in_specs=[full((Lq,W))]*5+[full((Lq,128)),full(fwd.shape),full((Lq,HD)),full((Lq,HD))],
        out_specs=(full((Lq,W)),)*3+(full((H,nb*256)),),
        scratch_shapes=[pltpu.VMEM((Lq,2*HD),BF)]*5+[pltpu.VMEM((Lq,HD),F32)]*2+[pltpu.VMEM((H,Lq,HD),BF)]*3+[pltpu.VMEM((nb,128,128),F32)]*2,
        compiler_params=pltpu.CompilerParams(vmem_limit_bytes=48*2**20),name="self_bwd")(q,k,v,do,of,lse,fwd,qa,ka)

def fold_bias(gb,Lq):
    H=gb.shape[0]; nb=Lq//128
    x=gb.reshape(H,nb,2,128)
    low=x[:,:,0].reshape(H,Lq); high=x[:,:,1].reshape(H,Lq)
    return high+jnp.concatenate([low[:,128:],jnp.zeros((H,128),gb.dtype)],axis=1)


def normalize(values, scaling):
    return values * lax.rsqrt(jnp.mean(values * values, -1, keepdims=True) + NORM_EPS) * scaling


def gated(gate_values, up_values):
    return jax.nn.gelu(gate_values, approximate=True) * up_values


def factored_start(gradient, rowwise):
    square = gradient * gradient
    rowwise_new = BETA_TWO * rowwise + (1.0 - BETA_TWO) * jnp.mean(square, 2).T
    return (rowwise_new, jnp.sum(square, 0), jnp.sum(rowwise_new, 1))


def factored_finish(gradient, moment, rowwise_new, colwise, weight, column_sum, row_sum, total_rows):
    colwise_new = BETA_TWO * colwise + (1.0 - BETA_TWO) * (column_sum / total_rows)
    moment_new = BETA_ONE * moment + (1.0 - BETA_ONE) * gradient
    second = rowwise_new.T[:, :, None] * colwise_new[None] / (row_sum / total_rows)[None, :, None]
    stepped = (
        moment_new / (1.0 - BETA_ONE**STEP) / (jnp.sqrt(second / (1.0 - BETA_TWO**STEP)) + ADAM_EPS)
    )
    updated = weight - MATRIX_RATE * (stepped + WEIGHT_DECAY * weight)
    return (moment_new, colwise_new, updated)


def adaptive(gradient, moment, second, weight):
    moment_new = BETA_ONE * moment + (1.0 - BETA_ONE) * gradient
    second_new = BETA_TWO * second + (1.0 - BETA_TWO) * gradient * gradient
    stepped = (
        moment_new
        / (1.0 - BETA_ONE**STEP)
        / (jnp.sqrt(second_new / (1.0 - BETA_TWO**STEP)) + ADAM_EPS)
    )
    return (moment_new, second_new, weight - VECTOR_RATE * stepped)


def make_shards(n, rows):
    devices = n * rows
    both = ("rows", "seq")
    hpd = -(-HEADS // n)
    wd = hpd * HD
    wide = n * wd

    def widen(values):
        extra = wide - values.shape[-1]
        return values if extra == 0 else jnp.pad(values, [(0, 0)] * (values.ndim - 1) + [(0, extra)])

    def to_seq(values):
        return lax.all_to_all(values, "seq", 0, 1, tiled=True)

    def along_seq(values):
        if n % 2:
            return lax.all_gather(values, "seq", axis=0, tiled=True)
        shard = lax.axis_index("seq")
        length = values.shape[0]
        whole = jnp.zeros((n * length,) + values.shape[1:], values.dtype)
        for step in range(0, n, 2):
            block = values
            if step:
                block = lax.ppermute(values, "seq", [(i, (i + step) % n) for i in range(n)])
            beside = lax.ppermute(block, "seq", [(i, i ^ 1) for i in range(n)])
            for part, owner in ((block, shard), (beside, shard ^ 1)):
                place = lax.rem(owner + n - step, n) * length
                whole = lax.dynamic_update_slice_in_dim(whole, part, place, 0)
        return whole

    def own_columns(weight):
        count, j = weight.shape[:2]
        parts = jnp.moveaxis(widen(weight).reshape(count, j, n, wd), 2, 0).reshape(1, n, count, j * wd)
        parts = jnp.broadcast_to(parts, (rows,) + parts.shape[1:]).reshape(devices, count, j * wd)
        return lax.all_to_all(parts, both, 0, 0, tiled=True).reshape(devices * count, j, wd)

    def by_heads(weight):
        count, j = weight.shape[:2]
        return jnp.moveaxis(widen(weight).reshape(count, j, n, wd), 2, 1).reshape(count, n * j * wd)

    def sum_columns(gradient):
        total, width = gradient.shape
        count, j = total // devices, width // wd
        got = lax.all_to_all(gradient.astype(BF).reshape(devices, count, width), both, 0, 0, tiled=True)
        got = jnp.sum(got.reshape(rows, n, count, j, wd).astype(F32), 0)
        return jnp.moveaxis(got, 0, 2).reshape(count, j, wide)[:, :, :D]

    def sum_rows(gradient):
        count, width = D // devices, gradient.shape[1]
        if wide == D and wd == rows * count:
            got = lax.all_to_all(
                gradient.astype(BF).reshape(rows, count, width), "rows", 0, 0, tiled=True
            )
            got = jnp.sum(got.astype(F32), 0)
            places = [(r * n + s, s * rows + r) for r in range(rows) for s in range(n)]
            return lax.ppermute(got, both, places)
        whole = lax.dynamic_update_slice_in_dim(
            jnp.zeros((wide, width), BF), gradient.astype(BF), lax.axis_index("seq") * wd, 0
        )[:D]
        return lax.psum_scatter(whole, both, scatter_dimension=0, tiled=True).astype(F32)

    def shards(
        decoder_input,
        encoder_output,
        cotangent,
        decoder_segment,
        decoder_padding,
        encoder_segment,
        encoder_padding,
        distance_bucket,
        attention_weight,
        attention_moment,
        attention_rowwise,
        attention_colwise,
        expand_weight,
        expand_moment,
        expand_rowwise,
        expand_colwise,
        contract_weight,
        contract_moment,
        contract_rowwise,
        contract_colwise,
        norm_gain,
        gain_moment,
        gain_second,
        relative_table,
        table_moment,
        table_second,
    ):
        shard = lax.axis_index("seq")
        length = decoder_segment.shape[1]
        attention_low = attention_weight.astype(BF)
        first_columns = own_columns(attention_low[:, 0:3]).reshape(D, 3 * wd)
        row_input = along_seq(decoder_input[0])
        attention_full = lax.all_gather(
            jnp.concatenate(
                (
                    attention_low[:, 3],
                    attention_low[:, 7],
                    by_heads(attention_low[:, 4:5]),
                    by_heads(attention_low[:, 5:7]),
                    by_heads(attention_low[:, 0:3]),
                ),
                1,
            ),
            both, axis=0, tiled=True,
        )
        row_encoder = along_seq(encoder_output[0])
        expand_full = lax.all_gather(
            expand_weight.astype(BF).reshape(-1, 2 * FF), both, axis=0, tiled=True
        )
        contract_full = lax.all_gather(contract_weight.astype(BF), both, axis=0, tiled=True)
        edges = (0, D, 2 * D, 2 * D + wide, 2 * D + 3 * wide, 2 * D + 6 * wide)
        self_out_weight, cross_out_weight, cross_query_weight, cross_pair_weight, first_weight = (
            attention_full[:, low:high] for low, high in zip(edges[:-1], edges[1:])
        )
        cross_query_columns = lax.dynamic_slice_in_dim(cross_query_weight, shard * wd, wd, 1)
        cross_columns = lax.dynamic_slice_in_dim(cross_pair_weight, shard * 2 * wd, 2 * wd, 1)

        def own_rows(matrix):
            padded = jnp.pad(matrix, ((0, wide - D), (0, 0))) if wide > D else matrix
            return lax.dynamic_slice_in_dim(padded, shard * wd, wd, 0)

        document = jnp.arange(HD, dtype=jnp.int32)[None, :]
        decoder_document = decoder_segment[0][:, None] == document
        query_side = decoder_document.astype(BF)
        self_side = jnp.where(
            (document < 3) & ~(decoder_document & (decoder_padding[0][:, None] == 1)), NEG, 0.0
        ).astype(BF)
        cross_side = jnp.where(
            (document < 3)
            & ~((encoder_segment[0][:, None] == document) & (encoder_padding[0][:, None] == 1)),
            NEG,
            0.0,
        ).astype(BF)
        onehot = (
            distance_bucket[:, None] == jnp.arange(BUCKETS, dtype=jnp.int32)[None, :]
        ).astype(F32)
        table_own = lax.dynamic_slice_in_dim(
            jnp.pad(relative_table, ((0, 0), (0, n * hpd - HEADS))), shard * hpd, hpd, 1
        )
        bias = jnp.einsum("db,bh->hd", onehot, table_own, precision=HIGHEST)
        beyond = jnp.full((hpd, 128), NEG, F32)
        bias_forward = jnp.concatenate((beyond, bias), 1)
        bias_backward = jnp.concatenate((bias[:, ::-1], beyond), 1)

        def dot(left, right):
            return jnp.dot(left, right, preferred_element_type=F32)

        def dot_back(left, right):
            return lax.dot_general(left, right, (((1,), (1,)), ((), ())), preferred_element_type=F32)

        def outer(left, right):
            return lax.dot_general(left, right, (((0,), (0,)), ((), ())), preferred_element_type=F32)

        row_norm = normalize(row_input.astype(F32), norm_gain[0]).astype(BF)
        self_proj = dot(row_norm, first_columns).astype(BF)
        query, key, value = (
            self_proj[:, 0:wd],
            self_proj[:, wd : 2 * wd],
            self_proj[:, 2 * wd : 3 * wd],
        )
        self_heads, self_exact, self_lse = self_fwd(
            query, key, value, bias_backward, query_side, self_side
        )
        inputs = decoder_input[0].astype(F32)
        self_out = to_seq(self_heads)[:, :D]
        after_self = inputs + dot(self_out, self_out_weight)
        cross_norm = normalize(after_self, norm_gain[1]).astype(BF)
        row_cross_norm = along_seq(cross_norm)
        cross_query = dot(row_cross_norm, cross_query_columns).astype(BF)
        cross_pair = dot(row_encoder, cross_columns).astype(BF)
        cross_key, cross_value = cross_pair[:, 0:wd], cross_pair[:, wd : 2 * wd]
        cross_heads, cross_exact, cross_lse = cross_fwd(
            cross_query, cross_key, cross_value, query_side, cross_side
        )
        cross_out = to_seq(cross_heads)[:, :D]
        after_cross = after_self + dot(cross_out, cross_out_weight)
        feed_norm = normalize(after_cross, norm_gain[2]).astype(BF)
        hidden_pair = dot(feed_norm, expand_full)
        gate_values, up_values = hidden_pair[:, 0:FF], hidden_pair[:, FF:]
        feed_branch = cotangent[0]
        grad_result = feed_branch.astype(F32)
        grad_hidden = dot_back(feed_branch, contract_full)
        hidden_wide, gated_back = jax.vjp(gated, gate_values, up_values)
        hidden = hidden_wide.astype(BF)
        layer_output = (after_cross + dot(hidden, contract_full)).astype(BF)
        grad_gate, grad_up = gated_back(grad_hidden)
        grad_pair = jnp.concatenate((grad_gate.astype(BF), grad_up.astype(BF)), 1)
        unused_norm, norm_back = jax.vjp(normalize, after_cross, norm_gain[2])
        feed_part, feed_gain = norm_back(dot_back(grad_pair, expand_full))
        grad_after_cross = grad_result + feed_part
        cross_branch = grad_after_cross.astype(BF)
        row_cross_branch = along_seq(cross_branch)
        cross_grad = dot_back(row_cross_branch, own_rows(cross_out_weight)).astype(BF)
        cross_out_sum = sum_rows(outer(cross_heads, row_cross_branch))
        contract_sum = lax.psum_scatter(
            outer(hidden, feed_branch).astype(BF), both, scatter_dimension=0, tiled=True
        ).astype(F32)
        expand_sum = lax.psum_scatter(
            outer(feed_norm, grad_pair).astype(BF), both, scatter_dimension=0, tiled=True
        ).astype(F32).reshape(-1, 2, FF)
        cross_qgrad, cross_kgrad, cross_vgrad = cross_bwd(
            cross_query, cross_key, cross_value, cross_grad, cross_exact, cross_lse, query_side, cross_side
        )
        grad_cross_query = to_seq(cross_qgrad)
        unused_norm, norm_back = jax.vjp(normalize, after_self, norm_gain[1])
        cross_part, cross_gain = norm_back(dot_back(grad_cross_query, cross_query_weight))
        grad_after_self = grad_after_cross + cross_part
        self_branch = grad_after_self.astype(BF)
        row_self_branch = along_seq(self_branch)
        self_grad = dot_back(row_self_branch, own_rows(self_out_weight)).astype(BF)
        self_out_sum = sum_rows(outer(self_heads, row_self_branch))
        cross_grads = jnp.concatenate((cross_kgrad, cross_vgrad), 1)
        cross_sum = sum_columns(
            jnp.concatenate(
                (outer(row_cross_norm, cross_qgrad), outer(row_encoder, cross_grads)), 1
            )
        )
        encoder_gradient = dot_back(
            to_seq(cross_grads), cross_pair_weight
        )
        self_qgrad, self_kgrad, self_vgrad, pair_bias = self_bwd(
            query, key, value, self_grad, self_exact, self_lse, bias_forward, query_side, self_side
        )
        grad_bias = fold_bias(pair_bias, length)
        table_own_grad = jnp.einsum("hd,db->bh", grad_bias, onehot, precision=HIGHEST)
        table_local = lax.dynamic_update_slice_in_dim(
            jnp.zeros((BUCKETS, n * hpd), F32), table_own_grad, shard * hpd, 1
        )[:, :HEADS]
        self_grads = jnp.concatenate((self_qgrad, self_kgrad, self_vgrad), 1)
        self_sum = sum_columns(outer(row_norm, self_grads))
        unused_norm, norm_back = jax.vjp(normalize, inputs, norm_gain[0])
        self_part, self_gain = norm_back(
            dot_back(to_seq(self_grads), first_weight)
        )
        input_gradient = grad_after_self + self_part

        attention_sum = jnp.concatenate(
            (self_sum, self_out_sum[:, None], cross_sum, cross_out_sum[:, None]), 1
        )
        attention_rows, attention_columns, attention_rowsum = factored_start(
            attention_sum, attention_rowwise
        )
        expand_rows, expand_columns, expand_rowsum = factored_start(expand_sum, expand_rowwise)
        contract_rows, contract_columns, contract_rowsum = factored_start(
            contract_sum[:, None, :], contract_rowwise[None, :]
        )
        gain_local = jnp.stack((self_gain, cross_gain, feed_gain), 0)
        (
            attention_total,
            expand_total,
            contract_total,
            attention_rowtotal,
            expand_rowtotal,
            contract_rowtotal,
            gain_gradient,
            table_gradient,
        ) = lax.psum(
            (
                attention_columns,
                expand_columns,
                contract_columns,
                attention_rowsum,
                expand_rowsum,
                contract_rowsum,
                gain_local,
                table_local,
            ),
            both,
        )
        attention_new = factored_finish(
            attention_sum,
            attention_moment,
            attention_rows,
            attention_colwise,
            attention_weight,
            attention_total,
            attention_rowtotal,
            D,
        )
        expand_new = factored_finish(
            expand_sum,
            expand_moment,
            expand_rows,
            expand_colwise,
            expand_weight,
            expand_total,
            expand_rowtotal,
            D,
        )
        contract_new = factored_finish(
            contract_sum[:, None, :],
            contract_moment[:, None, :],
            contract_rows,
            contract_colwise[None, :],
            contract_weight[:, None, :],
            contract_total,
            contract_rowtotal,
            FF,
        )
        gain_new = adaptive(gain_gradient, gain_moment, gain_second, norm_gain)
        table_new = adaptive(table_gradient, table_moment, table_second, relative_table)
        return (
            layer_output[None],
            input_gradient[None],
            encoder_gradient[None],
            attention_sum,
            attention_new[0],
            attention_rows,
            attention_new[1],
            attention_new[2],
            expand_sum,
            expand_new[0],
            expand_rows,
            expand_new[1],
            expand_new[2],
            contract_sum,
            contract_new[0][:, 0],
            contract_rows[0],
            contract_new[1][0],
            contract_new[2][:, 0],
            gain_gradient,
            gain_new[0],
            gain_new[1],
            gain_new[2],
            table_gradient,
            table_new[0],
            table_new[1],
            table_new[2],
        )

    return shards


def solution(mesh):
    placed = (
        P("rows", "seq", None),
        P("rows", "seq", None),
        P("rows", "seq", None),
        P("rows", None),
        P("rows", None),
        P("rows", None),
        P("rows", None),
        P(),
        P(("rows", "seq"), None, None),
        P(("rows", "seq"), None, None),
        P(None, ("rows", "seq")),
        P(),
        P(("rows", "seq"), None, None),
        P(("rows", "seq"), None, None),
        P(None, ("rows", "seq")),
        P(),
        P(("rows", "seq"), None),
        P(("rows", "seq"), None),
        P(("rows", "seq")),
        P(),
        P(),
        P(),
        P(),
        P(),
        P(),
        P(),
    )
    return jax.shard_map(
        make_shards(mesh.shape["seq"], mesh.shape["rows"]),
        mesh=mesh,
        in_specs=placed,
        out_specs=(
            P("rows", "seq", None),
            P("rows", "seq", None),
            P("rows", "seq", None),
            P(("rows", "seq"), None, None),
            P(("rows", "seq"), None, None),
            P(None, ("rows", "seq")),
            P(),
            P(("rows", "seq"), None, None),
            P(("rows", "seq"), None, None),
            P(("rows", "seq"), None, None),
            P(None, ("rows", "seq")),
            P(),
            P(("rows", "seq"), None, None),
            P(("rows", "seq"), None),
            P(("rows", "seq"), None),
            P(("rows", "seq")),
            P(),
            P(("rows", "seq"), None),
            P(),
            P(),
            P(),
            P(),
            P(),
            P(),
            P(),
            P(),
        ),
        check_vma=False,
    )
```

time: 2120 us -> 628 us (0.30)
  waiting for transfers between devices: 726 us -> 161 us
  local copies, waits for them, and re-layouts: 635 us -> 83.9 us
  matrix products: 567 us -> 86.5 us
  Pallas kernels: 0 us -> 135 us
  other arithmetic: 110 us -> 31.9 us
  starting transfers between devices: 0.79 us -> 55.5 us
    reduce_scatter x7 -> x2, waiting for transfers between devices: 641 us -> 0.02 us  [the longest x1 0.02 us: shards(): lax.psum_scatter(outer(feed_norm, grad_pair).astype(BF), both, scatter_di...]
    dot_general x191 -> x23, matrix products: 567 us -> 86.5 us  [the longest x7 29.5 us: outer(): lax.dot_general(left, right, (((0,), (0,)), ((), ())), preferred_element_...]
    dynamic_update_slice x48 -> x18, local copies, waits for them, and re-layouts: 469 us -> 23.4 us  [the longest x17 22.1 us: along_seq(): whole = lax.dynamic_update_slice_in_dim(whole, part, place, 0)]
    pallas_call x0 -> x4, Pallas kernels: none -> 135 us  [the longest x1 68.6 us: cross_bwd(): pl.pallas_call(kern, grid=(H, nq), out_shape=(jax.ShapeDtypeStruct((Lq, W...]
    ppermute x0 -> x17, waiting for transfers between devices: none -> 73 us  [the longest x5 72.9 us: along_seq(): block = lax.ppermute(values, 'seq', [(i, (i + step) % n) for i in range(n)])]
    unnamed x191 -> x181, local copies, waits for them, and re-layouts: 80.3 us -> 20.1 us
    convert_element_type x25 -> x5, other arithmetic: 61.7 us -> 4.57 us  [the longest x1 2.51 us: shards(): cross_side = jnp.where((document < 3) & ~((encoder_segment[0][:, None] ==...]
    all_to_all x0 -> x9, waiting for transfers between devices: none -> 43.9 us  [the longest x4 20.5 us: to_seq(): return lax.all_to_all(values, 'seq', 0, 1, tiled=True)]
  transfers between devices with their start and end apart: 14 -> 31, of which waited for: 7 -> 13; matrix products, arithmetic and copies ran while one was open for 21% -> 26% of each run, Pallas kernels for 0% -> 22%
where the time goes in v1:
time: 628 us; the launch traced here: 623 us
  waiting for transfers between devices  161 us (26%)
  Pallas kernels  135 us (21%)
  matrix products  86.5 us (14%)
  local copies, waits for them, and re-layouts  83.9 us (13%)
  starting transfers between devices  55.5 us (9%)
  blocking collectives  53 us (8%)
  other arithmetic  31.9 us (5%)
  between operations  16.3 us (3%)
    ppermute x5, waiting for transfers between devices, along_seq(): block = lax.ppermute(values, 'seq', [(i, (i + step) % n) for i in range(n)])  72.9 us
    pallas_call x1, Pallas kernels, cross_bwd(): pl.pallas_call(kern, grid=(H, nq), out_shape=(jax.ShapeDtypeStruct((Lq, W...  68.6 us
    all_gather x1, waiting for transfers between devices, shards(): lax.all_gather(contract_weight.astype(BF), both, axis=0, tiled=True)  44.2 us
    psum x1, blocking collectives, shards(): lax.psum((attention_columns, expand_columns, contract_columns, attention_...  39.8 us
    pallas_call x1, Pallas kernels, cross_fwd(): pl.pallas_call(kern, grid=(Lq // qb,), out_shape=(jax.ShapeDtypeStruct((L...  31.2 us
    dot_general x7, matrix products, outer(): lax.dot_general(left, right, (((0,), (0,)), ((), ())), preferred_element_...  29.5 us
    dot_general x7, matrix products, dot_back(): lax.dot_general(left, right, (((1,), (1,)), ((), ())), preferred_element_...  28.7 us
    dot_general x7, matrix products, dot(): return jnp.dot(left, right, preferred_element_type=F32)  26.6 us
  transfers between devices with their start and end apart: 31, of which 13 were waited for; matrix products, arithmetic and copies ran while one was open for 26% of the time, Pallas kernels for 22%

profile of v1, /device:TPU:0, one launch (start us, length us, event | category | flops | bytes accessed | tf_op | source)
XLA Modules:
  0.0 623.4 jit_solution(13089699473889411487)
XLA Ops:
  16.1 6.2 all-to-all-start
  29.8 50.1 %collective-permute-done.1 = bf16[352,768]{1,0:T(8,128)(2,1)} collective-permute-done((bf16[352,768]{1,0:T(8,128)(2,1)S(1)}, bf16[352,768]{1,0:T(8,128)(2,1)}, u32[]{:S(2)}, u32[]{:S(2)}) %collective-permute-start.1) | collective-permute-done | bytes 540704 | tf_op jit(solution)/shard_map/ppermute | solution.py:352
  89.9 14.1 %self_fwd.1 = (bf16[1408,192]{1,0:T(8,128)(2,1)S(1)}, f32[1408,192]{1,0:T(8,128)S(1)}, f32[1408,128]{1,0:T(8,128)S(1)}) custom-call(bf16[1408,192]{1,0:T(8,128)(2,1)S(1)} %get-tuple-element.215.q_ref, bf16[1408,192]{1,0:T(8,128)(2,1)S(1)} %get-tuple-element.214.k_ref, bf16[1408,192]{1,0:T(8,128)(2,1)S(1)} %get-tuple-element.213.v_ref, ...), custom_call_target="tpu_custom_call" | custom-call | tf_op jit(solution)/shard_map/self_fwd/pallas_call | solution.py:203
  109.1 4.2 all-to-all-start.1
  136.2 5.0 collective-permute-done.4
  144.8 31.2 %cross_fwd.1 = (bf16[1408,192]{1,0:T(8,128)(2,1)}, f32[1408,192]{1,0:T(8,128)}, f32[1408,128]{1,0:T(8,128)}) custom-call(bf16[1408,192]{1,0:T(8,128)(2,1)} %convolution_convert_fusion.4.q_ref, bf16[4096,192]{1,0:T(8,128)(2,1)} %get-tuple-element.212.k_ref, bf16[4096,192]{1,0:T(8,128)(2,1)} %get-tuple-element.211.v_ref, bf16[1408,64]{1,0:T(8,128)(2,1)} %copy-done, ...), custom_call_target="tpu_custom_call" | custom-call | tf_op jit(solution)/shard_map/cross_fwd/pallas_call | solution.py:72
  178.2 13.2 %all_to_all.120 = bf16[4,352,192]{1,2,0:T(8,128)(2,1)S(1)} all-to-all(bf16[4,352,192]{1,2,0:T(8,128)(2,1)} %copy.141), channel_id=1, replica_groups=mesh['rows'=8,'seq'=4] {'seq'}, dimensions={0} | all-to-all | bytes 1081344 | tf_op jit(solution)/shard_map/all_to_all | solution.py:341
  194.6 8.2 %fusion.61 = f32[352,4096]{1,0:T(8,128)} fusion(bf16[768,4096]{1,0:T(8,128)(2,1)} %all-gather.6.cloned.1.call-done, f32[352,768]{1,0:T(8,128)} %get-tuple-element.220, f32[768]{0:T(1024)S(1)} %get-tuple-element.168, f32[352]{0:T(512)S(1)} %fusion.56), kind=kOutput, calls=%fused_computation.182 | convolution fusion | flops 2215403520 | bytes 13144448 | tf_op jit(solution)/shard_map/dot_general | solution.py:476
  202.8 44.2 %all-gather.8.cloned.1.call-done = bf16[2048,768]{1,0:T(8,128)(2,1)} async-done(((bf16[64,768]{1,0:T(8,128)(2,1)}), bf16[2048,768]{1,0:T(8,128)(2,1)}) %all-gather.8.cloned.1.call-update) | async-done | bytes 3145744 | tf_op jit(solution)/shard_map/all_gather | solution.py:440
  247.1 7.0 %fusion.11 = (bf16[352,2048]{1,0:T(8,128)(2,1)S(1)}, bf16[352,2048]{1,0:T(8,128)(2,1)S(1)}, bf16[352,2048]{1,0:T(8,128)(2,1)S(1)}) fusion(f32[352,4096]{1,0:T(8,128)} %fusion.61, bf16[2048,768]{1,0:T(8,128)(2,1)} %all-gather.8.cloned.1.call-done, bf16[1,352,768]{2,1,0:T(8,128)(2,1)} %param.28), kind=kOutput, calls=%fused_computation.20 | convolution fusion | flops 1126039552 | bytes 13778944 | tf_op jit(solution)/shard_map/dot_general | solution.py:479
  262.0 13.3 %collective-permute-done.10 = bf16[352,768]{1,0:T(8,128)(2,1)} collective-permute-done((bf16[352,768]{1,0:T(8,128)(2,1)}, bf16[352,768]{1,0:T(8,128)(2,1)}, u32[]{:S(2)}, u32[]{:S(2)}) %collective-permute-start.10) | collective-permute-done | bytes 540704 | tf_op jit(solution)/shard_map/ppermute | solution.py:352
  290.2 68.6 %cross_bwd.1 = (bf16[1408,192]{1,0:T(8,128)(2,1)}, bf16[4096,192]{1,0:T(8,128)(2,1)}, bf16[4096,192]{1,0:T(8,128)(2,1)}) custom-call(bf16[1408,192]{1,0:T(8,128)(2,1)} %convolution_convert_fusion.4.q_ref, bf16[4096,192]{1,0:T(8,128)(2,1)} %get-tuple-element.212.k_ref, bf16[4096,192]{1,0:T(8,128)(2,1)} %get-tuple-element.211.v_ref, ...), custom_call_target="tpu_custom_call" | custom-call | tf_op jit(solution)/shard_map/cross_bwd/pallas_call | solution.py:140
  360.9 4.6 all-to-all-start.3
  372.4 6.8 %convolution_convert_fusion.8 = bf16[768,384]{1,0:T(8,128)(2,1)S(1)} fusion(bf16[4096,768]{1,0:T(8,128)(2,1)} %constant_dynamic-update-slice_fusion.10, bf16[4096,384]{1,0:T(8,128)(2,1)S(1)} %pad_maximum_fusion), kind=kOutput, calls=%fused_computation.46 | convolution fusion | flops 2416214016 | bytes 10027008 | tf_op jit(solution)/shard_map/dot_general | solution.py:482
  382.0 4.2 all-to-all-start.9
  396.5 4.4 all-to-all-start.8
  400.9 8.3 %convolution_convert_fusion = bf16[768,4096]{1,0:T(8,128)(2,1)} fusion(bf16[352,2048]{1,0:T(8,128)(2,1)} %copy-done.78, bf16[352,2048]{1,0:T(8,128)(2,1)} %copy-done.77, f32[352,768]{1,0:T(8,128)} %get-tuple-element.220, f32[768]{0:T(1024)S(1)} %get-tuple-element.168, f32[352]{0:T(512)S(1)} %fusion.56), kind=kOutput, calls=%fused_computation | convolution fusion | flops 2224316416 | bytes 10260864 | tf_op jit(solution)/shard_map/dot_general | solution.py:482
  409.5 4.4 collective-permute-done.13
  420.6 5.1 all-to-all-done.8
  425.7 3.7 all-to-all-start.7
  429.4 4.7 copy.146
  434.1 5.1 all-to-all-done.7
  439.9 4.9 all-to-all-start.5
  451.0 21.2 %self_bwd.1 = (bf16[1408,192]{1,0:T(8,128)(2,1)S(1)}, bf16[1408,192]{1,0:T(8,128)(2,1)S(1)}, bf16[1408,192]{1,0:T(8,128)(2,1)S(1)}, f32[3,2816]{1,0:T(4,128)S(1)}) custom-call(bf16[1408,192]{1,0:T(8,128)(2,1)S(1)} %get-tuple-element.215.q_ref, bf16[1408,192]{1,0:T(8,128)(2,1)S(1)} %get-tuple-element.214.k_ref, ...), custom_call_target="tpu_custom_call" | custom-call | tf_op jit(solution)/shard_map/self_bwd/pallas_call | solution.py:279
  476.6 16.4 %all-to-all-done.5 = bf16[4,1024,384]{1,2,0:T(8,128)(2,1)} async-done(((bf16[4,1024,384]{1,2,0:T(8,128)(2,1)}), bf16[4,1024,384]{1,2,0:T(8,128)(2,1)}, u32[]{:S(2)}, u32[]{:S(2)}) %all-to-all-start.5) | async-done | bytes 3145760 | tf_op jit(solution)/shard_map/all_to_all | solution.py:341
  493.0 4.6 all-to-all-start.4
  497.6 4.5 fusion.17
  506.2 3.9 convolution_convert_fusion.7
  522.6 6.5 %all-to-all-start.6 = ((bf16[32,24,576]{2,1,0:T(8,128)(2,1)}), bf16[32,24,576]{2,1,0:T(8,128)(2,1)}, u32[]{:S(2)}, u32[]{:S(2)}) async-start(bf16[32,24,576]{2,1,0:T(8,128)(2,1)} %bitcast.138), calls=%async_computation.6 | async-start | bytes 1966080 | tf_op jit(solution)/shard_map/all_to_all | solution.py:372
  529.2 7.1 %convolution_bitcast_fusion = f32[1,1024,768]{2,1,0:T(8,128)} fusion(bf16[1024,1536]{0,1:T(8,128)(2,1)} %bitcast.28, bf16[768,6144]{1,0:T(8,128)(2,1)} %all-gather.4.cloned.1.call-done), kind=kOutput, calls=%fused_computation.38 | convolution fusion | flops 2415919104 | bytes 8650752 | tf_op jit(solution)/shard_map/dot_general | solution.py:479
  544.0 12.4 %all-to-all-done.6 = bf16[32,24,576]{2,1,0:T(8,128)(2,1)} async-done(((bf16[32,24,576]{2,1,0:T(8,128)(2,1)}), bf16[32,24,576]{2,1,0:T(8,128)(2,1)}, u32[]{:S(2)}, u32[]{:S(2)}) %all-to-all-start.6) | async-done | bytes 884768 | tf_op jit(solution)/shard_map/all_to_all | solution.py:372
  566.7 39.8 %all-reduce.3 = (f32[8,768]{1,0:T(8,128)S(1)}, f32[8]{0:T(128)S(1)}, f32[2,2048]{1,0:T(2,128)S(1)}, f32[2]{0:T(128)S(1)}, f32[1,768]{1,0:T(1,128)S(1)}, /*index=...) all-reduce(f32[8,768]{1,0:T(8,128)S(1)} %get-tuple-element.162, ...), channel_id=1, replica_groups=mesh['rows'=8,'seq'=4] {'rows','seq'}, use_global_device_ids=true, to_apply=%region_13.14 | all-reduce | flops 13707 | bytes 109656 | tf_op jit(solution)/shard_map/psum | solution.py:587
  (366 shorter events, 169.3 us)
Async XLA Ops:
  7.2 116.0 %all-gather.4.cloned.1.call-start = ((), (), s32[]{:S(2)}) async-start(), calls=%async_computation.12 | async-start | bytes 9732096 | tf_op jit(solution)/shard_map/all_gather | solution.py:423
  10.3 184.4 %all-gather.6.cloned.1.call-start = ((), (), s32[]{:S(2)}) async-start(), calls=%async_computation.13 | async-start | bytes 6488064 | tf_op jit(solution)/shard_map/all_gather | solution.py:437
  11.3 102.4 %collective-permute-start.6 = (bf16[1024,768]{1,0:T(8,128)(2,1)}, bf16[1024,768]{1,0:T(8,128)(2,1)}, u32[]{:S(2)}, u32[]{:S(2)}) collective-permute-start(bf16[1024,768]{1,0:T(8,128)(2,1)} %bitcast.12), channel_id=1, source_target_pairs={{0,1},{1,0},{2,3},{3,2},{4,5},{5,4},{6,7},{7,6},{8,9},{9,8},{10,11... | collective-permute-start | bytes 4718600 | tf_op jit(solution)/shard_map/ppermute | solution.py:353
  11.8 73.3 %collective-permute-start.7 = (bf16[1024,768]{1,0:T(8,128)(2,1)}, bf16[1024,768]{1,0:T(8,128)(2,1)}, u32[]{:S(2)}, u32[]{:S(2)}) collective-permute-start(bf16[1024,768]{1,0:T(8,128)(2,1)} %bitcast.12), channel_id=1, source_target_pairs={{0,2},{1,3},{2,0},{3,1},{4,6},{5,7},{6,4},{7,5},{8,10},{9,11},{10,... | collective-permute-start | bytes 4718600 | tf_op jit(solution)/shard_map/ppermute | solution.py:352
  14.4 67.6 %collective-permute-start = (bf16[352,768]{1,0:T(8,128)(2,1)S(1)}, bf16[352,768]{1,0:T(8,128)(2,1)}, u32[]{:S(2)}, u32[]{:S(2)}) collective-permute-start(bf16[352,768]{1,0:T(8,128)(2,1)S(1)} %bitcast.136), channel_id=1, source_target_pairs={{0,1},{1,0},{2,3},{3,2},{4,5},{5,4},{6,7},{7,6},{8,9},{9,8},{10,11... | collective-permute-start | bytes 1622024 | tf_op jit(solution)/shard_map/ppermute | solution.py:353
  14.5 65.4 %collective-permute-start.1 = (bf16[352,768]{1,0:T(8,128)(2,1)S(1)}, bf16[352,768]{1,0:T(8,128)(2,1)}, u32[]{:S(2)}, u32[]{:S(2)}) collective-permute-start(bf16[352,768]{1,0:T(8,128)(2,1)S(1)} %bitcast.137), channel_id=1, source_target_pairs={{0,2},{1,3},{2,0},{3,1},{4,6},{5,7},{6,4},{7,5},{8,10},{9,11},{10,... | collective-permute-start | bytes 1622024 | tf_op jit(solution)/shard_map/ppermute | solution.py:352
  16.1 70.0 %all-to-all-start = ((bf16[32,24,576]{2,1,0:T(8,128)(2,1)}), bf16[32,24,576]{2,1,0:T(8,128)(2,1)}, u32[]{:S(2)}, u32[]{:S(2)}) async-start(bf16[32,24,576]{2,1,0:T(8,128)(2,1)} %bitcast.2), calls=%async_computation | async-start | bytes 1966080 | tf_op jit(solution)/shard_map/all_to_all | solution.py:363
  22.4 224.7 %all-gather.8.cloned.1.call-start = ((), (), s32[]{:S(2)}) async-start(), calls=%async_computation.14 | async-start | bytes 3244032 | tf_op jit(solution)/shard_map/all_gather | solution.py:440
  29.3 476.9 %copy-start.55 = (f32[768]{0:T(1024)}, f32[768]{0:T(1024)S(1)}, u32[]{:S(2)}) copy-start(f32[768]{0:T(1024)S(1)} %get-tuple-element.170) | copy-start | bytes 9220
  79.9 5.1 collective-permute-start.2
  85.1 34.0 %collective-permute-start.8 = (bf16[1024,768]{1,0:T(8,128)(2,1)}, bf16[1024,768]{1,0:T(8,128)(2,1)}, u32[]{:S(2)}, u32[]{:S(2)}) collective-permute-start(bf16[1024,768]{1,0:T(8,128)(2,1)} %collective-permute-done.7), channel_id=1, source_target_pairs={{0,1},{1,0},{2,3},{3,2},{4,5},{5,4},{6,7},{7,6},{8,9},{9,8},{10,11... | collective-permute-start | bytes 4718600 | tf_op jit(solution)/shard_map/ppermute | solution.py:353
  109.1 14.1 %all-to-all-start.1 = ((bf16[4,352,192]{1,2,0:T(8,128)(2,1)}), bf16[4,352,192]{1,2,0:T(8,128)(2,1)}, u32[]{:S(2)}, u32[]{:S(2)}) async-start(bf16[4,352,192]{1,2,0:T(8,128)(2,1)} %copy.136), calls=%async_computation.1 | async-start | bytes 1179648 | tf_op jit(solution)/shard_map/all_to_all | solution.py:341
  113.3 427.9 %reduce-scatter.5.cloned.1.call-start = ((), (), s32[]{:S(2)}) async-start(), calls=%async_computation.16 | async-start | bytes 3244032 | tf_op jit(solution)/shard_map/reduce_scatter | solution.py:525
  126.4 16.4 %collective-permute-start.3 = (bf16[352,768]{1,0:T(8,128)(2,1)S(1)}, bf16[352,768]{1,0:T(8,128)(2,1)S(1)}, u32[]{:S(2)}, u32[]{:S(2)}) collective-permute-start(bf16[352,768]{1,0:T(8,128)(2,1)S(1)} %get-tuple-element.204), channel_id=1, source_target_pairs={{0,1},{1,0},{2,3},{3,2},{4,5},{5,4},{6,7},{7,6},{8,9},{9,8},{10,11... | collective-permute-start | bytes 1622024 | tf_op jit(solution)/shard_map/ppermute | solution.py:353
  126.4 14.7 %collective-permute-start.4 = (bf16[352,768]{1,0:T(8,128)(2,1)S(1)}, bf16[352,768]{1,0:T(8,128)(2,1)S(1)}, u32[]{:S(2)}, u32[]{:S(2)}) collective-permute-start(bf16[352,768]{1,0:T(8,128)(2,1)S(1)} %get-tuple-element.204), channel_id=1, source_target_pairs={{0,2},{1,3},{2,0},{3,1},{4,6},{5,7},{6,4},{7,5},{8,10},{9,11},{10,... | collective-permute-start | bytes 1622024 | tf_op jit(solution)/shard_map/ppermute | solution.py:352
  141.1 1.9 collective-permute-start.5
  260.6 14.8 %collective-permute-start.10 = (bf16[352,768]{1,0:T(8,128)(2,1)}, bf16[352,768]{1,0:T(8,128)(2,1)}, u32[]{:S(2)}, u32[]{:S(2)}) collective-permute-start(bf16[352,768]{1,0:T(8,128)(2,1)} %get-tuple-element.202), channel_id=1, source_target_pairs={{0,2},{1,3},{2,0},{3,1},{4,6},{5,7},{6,4},{7,5},{8,10},{9,11},{10,... | collective-permute-start | bytes 1622024 | tf_op jit(solution)/shard_map/ppermute | solution.py:352
  262.0 16.9 %collective-permute-start.9 = (bf16[352,768]{1,0:T(8,128)(2,1)}, bf16[352,768]{1,0:T(8,128)(2,1)}, u32[]{:S(2)}, u32[]{:S(2)}) collective-permute-start(bf16[352,768]{1,0:T(8,128)(2,1)} %get-tuple-element.202), channel_id=1, source_target_pairs={{0,1},{1,0},{2,3},{3,2},{4,5},{5,4},{6,7},{7,6},{8,9},{9,8},{10,11... | collective-permute-start | bytes 1622024 | tf_op jit(solution)/shard_map/ppermute | solution.py:353
  275.4 7.4 %collective-permute-start.11 = (bf16[352,768]{1,0:T(8,128)(2,1)}, bf16[352,768]{1,0:T(8,128)(2,1)}, u32[]{:S(2)}, u32[]{:S(2)}) collective-permute-start(bf16[352,768]{1,0:T(8,128)(2,1)} %collective-permute-done.10), channel_id=1, source_target_pairs={{0,1},{1,0},{2,3},{3,2},{4,5},{5,4},{6,7},{7,6},{8,9},{9,8},{10,11... | collective-permute-start | bytes 1622024 | tf_op jit(solution)/shard_map/ppermute | solution.py:353
  360.9 21.1 %all-to-all-start.3 = ((bf16[4,352,192]{1,2,0:T(8,128)(2,1)}), bf16[4,352,192]{1,2,0:T(8,128)(2,1)}, u32[]{:S(2)}, u32[]{:S(2)}) async-start(bf16[4,352,192]{1,2,0:T(8,128)(2,1)} %copy.143), calls=%async_computation.3 | async-start | bytes 1179648 | tf_op jit(solution)/shard_map/all_to_all | solution.py:341
  382.0 14.4 %all-to-all-start.9 = ((bf16[8,24,768]{2,1,0:T(8,128)(2,1)}), bf16[8,24,768]{2,1,0:T(8,128)(2,1)S(1)}, u32[]{:S(2)}, u32[]{:S(2)}) async-start(bf16[8,24,768]{2,1,0:T(8,128)(2,1)} %bitcast.151), calls=%async_computation.9 | async-start | bytes 589824 | tf_op jit(solution)/shard_map/all_to_all | solution.py:379
  393.7 20.3 %collective-permute-start.13 = (bf16[352,768]{1,0:T(8,128)(2,1)}, bf16[352,768]{1,0:T(8,128)(2,1)}, u32[]{:S(2)}, u32[]{:S(2)}) collective-permute-start(bf16[352,768]{1,0:T(8,128)(2,1)} %get-tuple-element.199), channel_id=1, source_target_pairs={{0,2},{1,3},{2,0},{3,1},{4,6},{5,7},{6,4},{7,5},{8,10},{9,11},{10,... | collective-permute-start | bytes 1622024 | tf_op jit(solution)/shard_map/ppermute | solution.py:352
  396.5 29.2 %all-to-all-start.8 = ((bf16[32,24,576]{2,1,0:T(8,128)(2,1)}), bf16[32,24,576]{2,1,0:T(8,128)(2,1)}, u32[]{:S(2)}, u32[]{:S(2)}) async-start(bf16[32,24,576]{2,1,0:T(8,128)(2,1)} %pad_maximum_fusion.5), calls=%async_computation.8 | async-start | bytes 1966080 | tf_op jit(solution)/shard_map/all_to_all | solution.py:372
  400.9 163.1 %reduce-scatter.3.cloned.1.call-start = ((), (), s32[]{:S(2)}) async-start(), calls=%async_computation.15 | async-start | bytes 6488064 | tf_op jit(solution)/shard_map/reduce_scatter | solution.py:528
  409.2 4.7 collective-permute-start.12
  413.9 2.7 collective-permute-start.14
  425.7 13.5 %all-to-all-start.7 = ((bf16[8,24,768]{2,1,0:T(8,128)(2,1)}), bf16[8,24,768]{2,1,0:T(8,128)(2,1)S(1)}, u32[]{:S(2)}, u32[]{:S(2)}) async-start(bf16[8,24,768]{2,1,0:T(8,128)(2,1)} %bitcast.152), calls=%async_computation.7 | async-start | bytes 589824 | tf_op jit(solution)/shard_map/all_to_all | solution.py:379
  439.9 53.1 %all-to-all-start.5 = ((bf16[4,1024,384]{1,2,0:T(8,128)(2,1)}), bf16[4,1024,384]{1,2,0:T(8,128)(2,1)}, u32[]{:S(2)}, u32[]{:S(2)}) async-start(bf16[4,1024,384]{1,2,0:T(8,128)(2,1)} %copy.146), calls=%async_computation.5 | async-start | bytes 6291456 | tf_op jit(solution)/shard_map/all_to_all | solution.py:341
  493.0 29.6 %all-to-all-start.4 = ((bf16[4,352,576]{1,2,0:T(8,128)(2,1)}), bf16[4,352,576]{1,2,0:T(8,128)(2,1)}, u32[]{:S(2)}, u32[]{:S(2)}) async-start(bf16[4,352,576]{1,2,0:T(8,128)(2,1)} %copy.145), calls=%async_computation.4 | async-start | bytes 3538944 | tf_op jit(solution)/shard_map/all_to_all | solution.py:341
  503.9 58.8 %collective-permute-start.16 = (f32[24,768]{1,0:T(8,128)}, f32[24,768]{1,0:T(8,128)}, u32[]{:S(2)}, u32[]{:S(2)}) collective-permute-start(f32[24,768]{1,0:T(8,128)} %convert_reduce_fusion), channel_id=1, source_target_pairs={{0,0},{1,8},{2,16},{3,24},{4,1},{5,9},{6,17},{7,25},{8,2},{9,10},{... | collective-permute-start | bytes 221192 | tf_op jit(solution)/shard_map/ppermute | solution.py:384
  519.3 43.4 %collective-permute-start.15 = (f32[24,768]{1,0:T(8,128)S(1)}, f32[24,768]{1,0:T(8,128)S(1)}, u32[]{:S(2)}, u32[]{:S(2)}) collective-permute-start(f32[24,768]{1,0:T(8,128)S(1)} %convert_reduce_fusion.1), channel_id=1, source_target_pairs={{0,0},{1,8},{2,16},{3,24},{4,1},{5,9},{6,17},{7,25},{8,2},{9,10},{... | collective-permute-start | bytes 221192 | tf_op jit(solution)/shard_map/ppermute | solution.py:384
  522.6 33.8 %all-to-all-start.6 = ((bf16[32,24,576]{2,1,0:T(8,128)(2,1)}), bf16[32,24,576]{2,1,0:T(8,128)(2,1)}, u32[]{:S(2)}, u32[]{:S(2)}) async-start(bf16[32,24,576]{2,1,0:T(8,128)(2,1)} %bitcast.138), calls=%async_computation.6 | async-start | bytes 1966080 | tf_op jit(solution)/shard_map/all_to_all | solution.py:372
  (85 other events, 787.6 us)
Sparse Core Ops, SparseCore 0:
  11.5 102.1 all-gather.3
  117.1 68.9 all-gather.5
  189.6 57.4 all-gather.7
  279.0 100.4 reduce-scatter.4
  409.3 131.2 reduce-scatter.2

commit v2 on v1

--- a/solution.py
+++ b/solution.py
@@ -27,16 +27,16 @@
 def nn(a,b): return lax.dot_general(a,b,(((1,),(0,)),((),())),preferred_element_type=F32)
 def tn(a,b): return lax.dot_general(a,b,(((0,),(0,)),((),())),preferred_element_type=F32)
 
-def cross_fwd(q,k,v,qa,ka,qb=352,kc=1024):
-    Lq,W=q.shape; Lk=k.shape[0]; H=W//HD
+def cross_fwd(q,kv,qa,ka,qb=352,kc=1024):
+    Lq,W=q.shape; Lk=kv.shape[0]; H=W//HD
     nk=Lk//kc
-    def kern(q_ref,k_ref,v_ref,qa_ref,ka_ref,o_ref,of_ref,lse_ref,kaug,vs,s_s,m_s,l_s,acc):
+    def kern(q_ref,kv_ref,qa_ref,ka_ref,o_ref,of_ref,lse_ref,kaug,vs,s_s,m_s,l_s,acc):
         @pl.when(pl.program_id(0)==0)
         def _():
             for h in range(H):
-                kaug[h,:,0:HD]=k_ref[:,h*HD:(h+1)*HD]
+                kaug[h,:,0:HD]=kv_ref[:,2*h*HD:(2*h+1)*HD]
                 kaug[h,:,HD:2*HD]=ka_ref[...]
-                vs[h]=v_ref[:,h*HD:(h+1)*HD]
+                vs[h]=kv_ref[:,(2*h+1)*HD:(2*h+2)*HD]
         lane=lax.broadcasted_iota(jnp.int32,(qb,128),1)
         lses=jnp.zeros((qb,128),F32)
         outs=[]
@@ -71,29 +71,50 @@
     row=lambda w: pl.BlockSpec((qb,w),lambda i:(i,0))
     return pl.pallas_call(kern,grid=(Lq//qb,),
         out_shape=(jax.ShapeDtypeStruct((Lq,W),BF),jax.ShapeDtypeStruct((Lq,W),F32),jax.ShapeDtypeStruct((Lq,128),F32)),
-        in_specs=[row(W),full((Lk,W)),full((Lk,W)),row(HD),full((Lk,HD))],
+        in_specs=[row(W),full((Lk,2*W)),row(HD),full((Lk,HD))],
         out_specs=(row(W),row(W),row(128)),
         scratch_shapes=[pltpu.VMEM((H,Lk,2*HD),BF),pltpu.VMEM((H,Lk,HD),BF),pltpu.VMEM((qb,Lk),F32),pltpu.VMEM((qb,128),F32),pltpu.VMEM((qb,128),F32),pltpu.VMEM((qb,HD),F32)],
-        compiler_params=pltpu.CompilerParams(vmem_limit_bytes=56*2**20),name="cross_fwd")(q,k,v,qa,ka)
+        compiler_params=pltpu.CompilerParams(vmem_limit_bytes=56*2**20),cost_estimate=cost(31.0),name="cross_fwd")(q,kv,qa,ka)
 
 def split3(x):
     a=x.astype(BF); r=x-a.astype(F32)
     b=r.astype(BF); c=(r-b.astype(F32)).astype(BF)
     return a,b,c
 
-def cross_bwd(q,k,v,do,of,lse,qa,ka,qb=256,kc=1024):
-    Lq,W=q.shape; Lk=k.shape[0]; H=W//HD
+def cross_bwd(q,kv,do,of,lse,qa,ka,n,qb=256,kc=1024):
+    Lq,W=q.shape; Lk=kv.shape[0]; H=W//HD
     nq=-(-Lq//qb); Lp=nq*qb; nk=Lk//kc
-    def kern(q_ref,k_ref,v_ref,do_ref,of_ref,lse_ref,qa_ref,ka_ref,dq_ref,dk_ref,dv_ref,kaug,vaug,qaug,doaug,dkacc,dvacc,dqs,dks,dvs):
+    def kern(q_ref,kv_ref,do_ref,of_ref,lse_ref,qa_ref,ka_ref,dq_ref,home_ref,dqw,last_ref,*rest):
+        dkv_refs=rest[:n]
+        (kaug,vaug,qaug,doaug,dkacc,dvacc,dqs,dkvs,q_out,q_in,kv_out,kv_in,own)=rest[n:]
         h=pl.program_id(0); i=pl.program_id(1)
+        r,s=lax.axis_index("rows"),lax.axis_index("seq")
+        def home(p,hh):
+            rows=slice(p*(Lk//n),(p+1)*(Lk//n))
+            peer=s^p
+            return pltpu.make_async_remote_copy(src_ref=dkvs.at[hh,rows],dst_ref=home_ref.at[s,hh],send_sem=kv_out.at[p,hh],
+                recv_sem=kv_in.at[p,hh],device_id=(r,peer),device_id_type=MESH)
+        def keep(hh):
+            return pltpu.make_async_copy(dkvs.at[hh,0:Lk//n],home_ref.at[s,hh],own.at[hh])
+        def turn(p):
+            return pltpu.make_async_remote_copy(src_ref=dqw.at[s^p],dst_ref=dq_ref.at[s],send_sem=q_out.at[p],
+                recv_sem=q_in.at[p],device_id=(r,s^p),device_id_type=MESH)
+        def stay():
+            return pltpu.make_async_copy(dqw.at[s],dq_ref.at[s],own.at[H])
+        @pl.when((h==0)&(i==0))
+        def _():
+            barrier=pltpu.get_barrier_semaphore()
+            for p in range(1,n):
+                pl.semaphore_signal(barrier,inc=1,device_id=(r,s^p),device_id_type=MESH)
+            pl.semaphore_wait(barrier,n-1)
         for hh in range(H):
             @pl.when((h==hh)&(i==0))
             def _():
                 sl=slice(hh*HD,(hh+1)*HD)
-                kaug[:,0:HD]=k_ref[:,sl]
+                kaug[:,0:HD]=kv_ref[:,2*hh*HD:(2*hh+1)*HD]
                 lane=lax.broadcasted_iota(jnp.int32,(Lk,HD),1)
                 kaug[:,HD:2*HD]=jnp.where((lane>=3)&(lane<6),BF(1),ka_ref[...])
-                vaug[:,0:HD]=v_ref[:,sl]
+                vaug[:,0:HD]=kv_ref[:,(2*hh+1)*HD:(2*hh+2)*HD]
                 vaug[:,HD:2*HD]=jnp.where(lane<3,BF(1),BF(0)).astype(BF)
                 lq=lax.broadcasted_iota(jnp.int32,(Lq,HD),1)
                 a,b,c=split3(-lse_ref[:,hh:hh+1])
@@ -127,23 +148,39 @@
             return dq+tn(ds,kk[:,0:HD])
         for c in range(nk): dq=step(c,dq)
         dqs[h,pl.ds(off,qb),:]=(dq*0.125).astype(BF)
-        @pl.when(i==nq-1)
-        def _():
-            dks[h]=dkacc[...].astype(BF)
-            dvs[h]=dvacc[...].astype(BF)
+        for hh in range(H):
+            @pl.when((i==nq-1)&(h==hh))
+            def _():
+                dkvs[hh,:,0:HD]=dkacc[...].astype(BF)
+                dkvs[hh,:,HD:]=dvacc[...].astype(BF)
+                if hh==H-1:
+                    for b in range(n):
+                        dqw[b]=jnp.concatenate([dqs[t,b*(Lq//n):(b+1)*(Lq//n),:] for t in range(H)],axis=1)
+                    for p in range(1,n): turn(p).start()
+                    stay().start()
+                else:
+                    for p in range(1,n): home(p,hh).start()
+                    keep(hh).start()
         @pl.when((i==nq-1)&(h==H-1))
         def _():
-            dq_ref[...]=jnp.concatenate([dqs[t,0:Lq,:] for t in range(H)],axis=1)
-            dk_ref[...]=jnp.concatenate([dks[t] for t in range(H)],axis=1)
-            dv_ref[...]=jnp.concatenate([dvs[t] for t in range(H)],axis=1)
+            for b,dkv_ref in enumerate(dkv_refs):
+                part=slice(b*(Lk//n),(b+1)*(Lk//n))
+                for t in range(H): dkv_ref[:,2*t*HD:2*(t+1)*HD]=dkvs[t,part,:]
+                last_ref[b]=dkvs[H-1,part,:]
+            for p in range(1,n): turn(p).wait()
+            stay().wait()
+            for hh in range(H-1):
+                for p in range(1,n): home(p,hh).wait()
+                keep(hh).wait()
     full=lambda s: pl.BlockSpec(s,lambda h,i:(0,)*len(s))
     return pl.pallas_call(kern,grid=(H,nq),
-        out_shape=(jax.ShapeDtypeStruct((Lq,W),BF),jax.ShapeDtypeStruct((Lk,W),BF),jax.ShapeDtypeStruct((Lk,W),BF)),
-        in_specs=[full((Lq,W)),full((Lk,W)),full((Lk,W)),full((Lq,W)),full((Lq,W)),full((Lq,128)),full((Lq,HD)),full((Lk,HD))],
-        out_specs=(full((Lq,W)),full((Lk,W)),full((Lk,W))),
+        out_shape=(jax.ShapeDtypeStruct((n,Lq//n,W),BF),jax.ShapeDtypeStruct((n,H-1,Lk//n,2*HD),BF),jax.ShapeDtypeStruct((n,Lq//n,W),BF),jax.ShapeDtypeStruct((n,Lk//n,2*HD),BF))+(jax.ShapeDtypeStruct((Lk//n,2*W),BF),)*n,
+        in_specs=[full((Lq,W)),full((Lk,2*W)),full((Lq,W)),full((Lq,W)),full((Lq,128)),full((Lq,HD)),full((Lk,HD))],
+        out_specs=(ANY,ANY,full((n,Lq//n,W)),full((n,Lk//n,2*HD)))+(full((Lk//n,2*W)),)*n,
         scratch_shapes=[pltpu.VMEM((Lk,2*HD),BF),pltpu.VMEM((Lk,2*HD),BF),pltpu.VMEM((Lp,2*HD),BF),pltpu.VMEM((Lp,2*HD),BF),
-            pltpu.VMEM((Lk,HD),F32),pltpu.VMEM((Lk,HD),F32),pltpu.VMEM((H,Lp,HD),BF),pltpu.VMEM((H,Lk,HD),BF),pltpu.VMEM((H,Lk,HD),BF)],
-        compiler_params=pltpu.CompilerParams(vmem_limit_bytes=60*2**20),name="cross_bwd")(q,k,v,do,of,lse,qa,ka)
+            pltpu.VMEM((Lk,HD),F32),pltpu.VMEM((Lk,HD),F32),pltpu.VMEM((H,Lp,HD),BF),pltpu.VMEM((H,Lk,2*HD),BF)]
+            +[pltpu.SemaphoreType.DMA((n,))]*2+[pltpu.SemaphoreType.DMA((n,H))]*2+[pltpu.SemaphoreType.DMA((H+1,))],
+        compiler_params=pltpu.CompilerParams(vmem_limit_bytes=60*2**20,collective_id=10,has_side_effects=True),cost_estimate=cost(68.0),name="cross_bwd")(q,kv,do,of,lse,qa,ka)
 
 def toeplitz(win, shift):
     x=jnp.broadcast_to(win,(128,256))
@@ -152,18 +189,18 @@
 def eye128():
     return lax.broadcasted_iota(jnp.int32,(128,128),0)==lax.broadcasted_iota(jnp.int32,(128,128),1)
 
-def self_fwd(q,k,v,rev,qa,ka):
-    Lq,W=q.shape; H=W//HD; nb=Lq//128
-    def kern(q_ref,k_ref,v_ref,rev_ref,qa_ref,ka_ref,o_ref,of_ref,lse_ref,qaug,kaug,kdiag,vs,os,tz):
+def self_fwd(qkv,rev,qa,ka):
+    Lq,W=qkv.shape[0],qkv.shape[1]//3; H=W//HD; nb=Lq//128
+    def kern(qkv_ref,rev_ref,qa_ref,ka_ref,o_ref,of_ref,lse_ref,qaug,kaug,kdiag,vs,os,tz):
         h=pl.program_id(0)
         for hh in range(H):
             @pl.when(h==hh)
             def _():
                 sl=slice(hh*HD,(hh+1)*HD)
-                qaug[:,0:HD]=q_ref[:,sl]*BF(0.125); qaug[:,HD:]=qa_ref[...]
-                kaug[:,0:HD]=k_ref[:,sl]; kaug[:,HD:]=ka_ref[...]
-                kdiag[:,0:HD]=k_ref[:,sl]; kdiag[:,HD:]=jnp.zeros((Lq,HD),BF)
-                vs[...]=v_ref[:,sl]
+                qaug[:,0:HD]=qkv_ref[:,sl]*BF(0.125); qaug[:,HD:]=qa_ref[...]
+                kaug[:,0:HD]=qkv_ref[:,W+hh*HD:W+(hh+1)*HD]; kaug[:,HD:]=ka_ref[...]
+                kdiag[:,0:HD]=qkv_ref[:,W+hh*HD:W+(hh+1)*HD]; kdiag[:,HD:]=jnp.zeros((Lq,HD),BF)
+                vs[...]=qkv_ref[:,2*W+hh*HD:2*W+(hh+1)*HD]
         @pl.when(h==0)
         def _():
             lse_ref[...]=jnp.zeros((Lq,128),F32)
@@ -202,29 +239,288 @@
     full=lambda s: pl.BlockSpec(s,lambda h:(0,)*len(s))
     return pl.pallas_call(kern,grid=(H,),
         out_shape=(jax.ShapeDtypeStruct((Lq,W),BF),jax.ShapeDtypeStruct((Lq,W),F32),jax.ShapeDtypeStruct((Lq,128),F32)),
-        in_specs=[full((Lq,W)),full((Lq,W)),full((Lq,W)),full(rev.shape),full((Lq,HD)),full((Lq,HD))],
+        in_specs=[full((Lq,3*W)),full(rev.shape),full((Lq,HD)),full((Lq,HD))],
         out_specs=(full((Lq,W)),full((Lq,W)),full((Lq,128))),
         scratch_shapes=[pltpu.VMEM((Lq,2*HD),BF)]*3+[pltpu.VMEM((Lq,HD),BF),pltpu.VMEM((H,Lq,HD),F32),pltpu.VMEM((nb,128,128),F32)],
-        compiler_params=pltpu.CompilerParams(vmem_limit_bytes=48*2**20),name="self_fwd")(q,k,v,rev,qa,ka)
-
-def self_bwd(q,k,v,do,of,lse,fwd,qa,ka):
-    Lq,W=q.shape; H=W//HD; nb=Lq//128
-    def kern(q_ref,k_ref,v_ref,do_ref,of_ref,lse_ref,fwd_ref,qa_ref,ka_ref,dq_ref,dk_ref,dv_ref,gb_ref,qaug,kaug,kdiag,vaug,doaug,dkacc,dvacc,dqs,dks,dvs,tz,ga):
+        compiler_params=pltpu.CompilerParams(vmem_limit_bytes=48*2**20),cost_estimate=cost(15.0),name="self_fwd")(qkv,rev,qa,ka)
+
+MESH = pl.DeviceIdType.MESH
+ANY = pl.BlockSpec(memory_space=pl.ANY)
+VM = pl.BlockSpec(memory_space=pltpu.VMEM)
+
+
+def cost(micros):
+    return pl.CostEstimate(flops=int(micros * 1.0e9), bytes_accessed=int(micros * 3.0e6), transcendentals=0)
+
+
+def greet_all(count, n):
+    r, s = lax.axis_index("rows"), lax.axis_index("seq")
+    barrier = pltpu.get_barrier_semaphore()
+
+    def greet(step, carry):
+        j = lax.rem((s if count == n else r * n + s) + step, count)
+        device = (r, j) if count == n else (lax.div(j, n), lax.rem(j, n))
+        pl.semaphore_signal(barrier, inc=1, device_id=device, device_id_type=MESH)
+        return carry
+
+    lax.fori_loop(1, count, greet, 0)
+    pl.semaphore_wait(barrier, count - 1)
+
+
+class Exchange:
+    def __init__(self, plans, n, rows):
+        self.kinds = [kind for kind, x in plans]
+        self.count = len(plans)
+        self.n, self.rows = n, rows
+        shapes = [(n * rows,) + x.shape[1:] if kind == "own" else x.shape for kind, x in plans]
+        self.shapes = tuple(jax.ShapeDtypeStruct(shape, x.dtype) for shape, (kind, x) in zip(shapes, plans))
+        self.scratch = [pltpu.SemaphoreType.DMA((shape[0],)) for shape in shapes for side in range(2)]
+        self.scratch += [pltpu.SemaphoreType.DMA((self.count,))]
+
+    def each(self, sent, got, sems, act):
+        n, rows = self.n, self.rows
+        r, s = lax.axis_index("rows"), lax.axis_index("seq")
+        me = r * n + s
+        for p, kind in enumerate(self.kinds):
+            x, y, out_sem, in_sem, own = sent[p], got[p], sems[2 * p], sems[2 * p + 1], sems[-1].at[p]
+
+            def remote(block, slot, device, leave, arrive, x=x, y=y, out_sem=out_sem, in_sem=in_sem):
+                return pltpu.make_async_remote_copy(
+                    src_ref=x.at[block], dst_ref=y.at[slot], send_sem=out_sem.at[leave], recv_sem=in_sem.at[arrive],
+                    device_id=device, device_id_type=MESH,
+                )
+
+            if kind == "rows":
+                def send(j, carry, act=act, x=x, y=y, own=own, remote=remote):
+                    target = s * rows + j
+                    away = remote(j, r, (lax.div(target, n), lax.rem(target, n)), j, r)
+
+                    @pl.when(target != me)
+                    def _():
+                        act(away, True)
+
+                    @pl.when(target == me)
+                    def _():
+                        act(pltpu.make_async_copy(x.at[j], y.at[r], own), None)
+
+                    return carry
+
+                def take(q, carry, act=act, remote=remote):
+                    @pl.when((q != r) | (lax.div(me, rows) != s))
+                    def _():
+                        act(remote(0, q, (r, s), 0, q), False)
+
+                    return carry
+
+                lax.fori_loop(0, rows, send, 0)
+                lax.fori_loop(0, rows, take, 0)
+                continue
+            if kind == "xor":
+                act(pltpu.make_async_copy(x.at[0], y.at[s], own), None)
+                for p in range(1, n):
+                    away = remote(p, s, (r, s ^ p), p, p)
+                    act(away, True)
+                    act(away, False)
+                continue
+            length, here = (n, s) if kind == "seq" else (n * rows, me)
+            act(pltpu.make_async_copy(x.at[s if kind == "own" else here], y.at[here], own), None)
+
+            def both_ways(step, carry, act=act, length=length, here=here, kind=kind, remote=remote):
+                j = lax.rem(here + step, length)
+                device = (r, j) if kind == "seq" else (lax.div(j, n), lax.rem(j, n))
+                away = remote(lax.rem(j, n) if kind == "own" else j, here, device, step, step)
+                act(away, True)
+                act(away, False)
+                return carry
+
+            lax.fori_loop(1, length, both_ways, 0)
+
+    def start(self, sent, got, sems, greet=True):
+        near = all(kind == "seq" for kind in self.kinds)
+        if greet:
+            greet_all(self.n if near else self.n * self.rows, self.n)
+        self.each(sent, got, sems, lambda copy, away: copy.start() if away is not False else None)
+
+    def wait(self, sent, got, sems):
+        def act(copy, away):
+            if away is None:
+                copy.wait()
+            elif away:
+                copy.wait_send()
+            else:
+                copy.wait_recv()
+
+        self.each(sent, got, sems, act)
+
+
+class Job:
+    def __init__(self, inputs=(), outs=(), body=None):
+        self.inputs, self.outs, self.body = list(inputs), tuple(outs), body
+        self.scratch = [pltpu.VMEM(x.shape, x.dtype) for x in self.inputs]
+        self.scratch += [pltpu.SemaphoreType.DMA((len(self.inputs),))] if self.inputs else []
+
+    def split(self, refs, before, between, after):
+        i, o = len(self.inputs), len(self.outs)
+        head, refs = refs[:before], refs[before:]
+        ins, refs = refs[:i], refs[i:]
+        middle, refs = refs[:between], refs[between:]
+        outs, refs = refs[:o], refs[o:]
+        return head + middle + refs[:after], ins, outs, refs[after:]
+
+    def run(self, ins, outs, scratch):
+        if not self.inputs:
+            return
+        held, sem = scratch[:-1], scratch[-1]
+        copies = [pltpu.make_async_copy(x, y, sem.at[k]) for k, (x, y) in enumerate(zip(ins, held))]
+        for copy in copies:
+            copy.start()
+        for copy in copies:
+            copy.wait()
+        self.body(held, outs)
+
+
+def exchange(plans, n, rows, collective_id, job=None):
+    ride, job = Exchange(plans, n, rows), job or Job()
+
+    def kern(*refs):
+        refs, ins, outs, scratch = job.split(refs, ride.count, ride.count, len(ride.scratch))
+        sent, got, sems = refs[: ride.count], refs[ride.count : 2 * ride.count], refs[2 * ride.count :]
+        ride.start(sent, got, sems)
+        job.run(ins, outs, scratch)
+        ride.wait(sent, got, sems)
+
+    return pl.pallas_call(
+        kern,
+        out_shape=ride.shapes + job.outs,
+        in_specs=[ANY] * (ride.count + len(job.inputs)),
+        out_specs=(ANY,) * ride.count + (VM,) * len(job.outs),
+        scratch_shapes=ride.scratch + job.scratch,
+        compiler_params=pltpu.CompilerParams(
+            collective_id=collective_id, has_side_effects=True, vmem_limit_bytes=56 * 2**20
+        ),
+        cost_estimate=cost(20.0),name="exchange",
+    )(*[x for kind, x in plans], *job.inputs)
+
+
+def gather_seq(values, n, rows, collective_id, plans=(), job=None):
+    ride, job = Exchange(plans, n, rows), job or Job()
+    sems_used = ride.scratch if ride.count else []
+
+    def kern(*refs):
+        refs, ins, outs, scratch = job.split(refs, 1 + ride.count, 1 + ride.count, 5 + len(sems_used))
+        x_ref, sent, o_ref = refs[0], refs[1 : 1 + ride.count], refs[1 + ride.count]
+        got, rest = refs[2 + ride.count : 2 + 2 * ride.count], refs[2 + 2 * ride.count :]
+        own, out_sem, in_sem, side_out, side_in = rest[:5]
+        sems = rest[5:]
+        r, s = lax.axis_index("rows"), lax.axis_index("seq")
+        beside = s + 1 - 2 * lax.rem(s, 2)
+        if ride.count:
+            greet_all(n * rows, n)
+        else:
+            barrier = pltpu.get_barrier_semaphore()
+            for step in range(2, n, 2):
+                pl.semaphore_signal(barrier, inc=1, device_id=(r, lax.rem(s + step, n)), device_id_type=MESH)
+            pl.semaphore_signal(barrier, inc=1, device_id=(r, beside), device_id_type=MESH)
+            pl.semaphore_wait(barrier, n // 2)
+        far = [
+            pltpu.make_async_remote_copy(
+                src_ref=x_ref, dst_ref=o_ref.at[s], send_sem=out_sem.at[k], recv_sem=in_sem.at[k],
+                device_id=(r, lax.rem(s + 2 * k, n)), device_id_type=MESH,
+            )
+            for k in range(1, n // 2)
+        ]
+        for copy in far:
+            copy.start()
+
+        def across(k):
+            slot = lax.rem(s + n - 2 * k, n)
+            return pltpu.make_async_remote_copy(
+                src_ref=x_ref if k == 0 else o_ref.at[slot], dst_ref=o_ref.at[slot],
+                send_sem=side_out.at[k], recv_sem=side_in.at[k], device_id=(r, beside), device_id_type=MESH,
+            )
+
+        near = [across(k) for k in range(n // 2)]
+        near[0].start()
+        local = pltpu.make_async_copy(x_ref, o_ref.at[s], own)
+        local.start()
+        if ride.count:
+            ride.start(sent, got, sems, greet=False)
+        for k, copy in enumerate(far):
+            job.run(ins, outs, scratch) if k == 0 else None
+            copy.wait_recv()
+            near[k + 1].start()
+        for copy in near:
+            copy.wait()
+        for copy in far:
+            copy.wait_send()
+        local.wait()
+        if ride.count:
+            ride.wait(sent, got, sems)
+
+    length, features = values.shape
+    whole, *got = pl.pallas_call(
+        kern,
+        out_shape=(jax.ShapeDtypeStruct((n, length, features), values.dtype),) + ride.shapes + job.outs,
+        in_specs=[ANY] * (1 + ride.count + len(job.inputs)),
+        out_specs=(ANY,) * (1 + ride.count) + (VM,) * len(job.outs),
+        scratch_shapes=[pltpu.SemaphoreType.DMA] + [pltpu.SemaphoreType.DMA((n // 2,))] * 4
+        + sems_used + job.scratch,
+        compiler_params=pltpu.CompilerParams(
+            collective_id=collective_id, has_side_effects=True, vmem_limit_bytes=56 * 2**20
+        ),
+        cost_estimate=cost(20.0),
+        name="gather_seq",
+    )(values, *[x for kind, x in plans], *job.inputs)
+    whole = whole.reshape(n * length, features)
+    return (whole, *got) if got else whole
+
+
+def project_blocks(blocks, weight):
+    length, width = blocks[0].shape[0], weight.shape[1]
+    count = len(blocks)
+
+    def kern(*refs):
+        weight_ref, o_ref = refs[count], refs[count + 1]
+        for k in range(count):
+            o_ref[k * length : (k + 1) * length, :] = nn(refs[k][...], weight_ref[...]).astype(BF)
+
+    return pl.pallas_call(
+        kern,
+        out_shape=jax.ShapeDtypeStruct((count * length, width), BF),
+        in_specs=[VM] * (count + 1),
+        out_specs=VM,
+        compiler_params=pltpu.CompilerParams(vmem_limit_bytes=40 * 2**20),
+        cost_estimate=cost(8.0),
+        name="project_blocks",
+    )(*blocks, weight)
+
+
+def self_bwd(qkv,do,of,lse,fwd,qa,ka,plans,n,rows):
+    Lq,W=qkv.shape[0],qkv.shape[1]//3; H=W//HD; nb=Lq//128
+    ride=Exchange(plans,n,rows)
+    def kern(qkv_ref,do_ref,of_ref,lse_ref,fwd_ref,qa_ref,ka_ref,*rest):
+        sent,rest=rest[:ride.count],rest[ride.count:]
+        grad_ref,gb_ref=rest[:2]
+        got,rest=rest[2:2+ride.count],rest[2+ride.count:]
+        (qaug,kaug,kdiag,vaug,doaug,dkacc,dvacc,dqs,dks,dvs,tz,ga),sems=rest[:12],rest[12:]
         h=pl.program_id(0)
+        @pl.when(h==0)
+        def _():
+            ride.start(sent,got,sems)
         for hh in range(H):
             @pl.when(h==hh)
             def _():
                 sl=slice(hh*HD,(hh+1)*HD)
                 lane=lax.broadcasted_iota(jnp.int32,(Lq,HD),1)
-                kaug[:,0:HD]=k_ref[:,sl]
+                kaug[:,0:HD]=qkv_ref[:,W+hh*HD:W+(hh+1)*HD]
                 ones=(lane>=3)&(lane<6)
                 kaug[:,HD:]=jnp.where(ones,BF(1),ka_ref[...])
-                kdiag[:,0:HD]=k_ref[:,sl]
+                kdiag[:,0:HD]=qkv_ref[:,W+hh*HD:W+(hh+1)*HD]
                 kdiag[:,HD:]=jnp.where(ones,BF(1),BF(0)).astype(BF)
-                vaug[:,0:HD]=v_ref[:,sl]
+                vaug[:,0:HD]=qkv_ref[:,2*W+hh*HD:2*W+(hh+1)*HD]
                 vaug[:,HD:]=jnp.where(lane<3,BF(1),BF(0)).astype(BF)
                 a,b,c=split3(-lse_ref[:,hh:hh+1])
-                qaug[:,0:HD]=q_ref[:,sl]*BF(0.125)
+                qaug[:,0:HD]=qkv_ref[:,sl]*BF(0.125)
                 qaug[:,HD:]=jnp.where(lane==3,a,jnp.where(lane==4,b,jnp.where(lane==5,c,qa_ref[...])))
                 dd=do_ref[:,sl]
                 delta=jnp.sum(dd.astype(F32)*of_ref[:,sl],axis=1,keepdims=True)
@@ -272,22 +568,131 @@
             gb_ref[pl.ds(h,1),d*256:(d+1)*256]=jnp.sum(x,axis=0,keepdims=True)
         @pl.when(h==H-1)
         def _():
-            dq_ref[...]=jnp.concatenate([dqs[t] for t in range(H)],axis=1)
-            dk_ref[...]=jnp.concatenate([dks[t] for t in range(H)],axis=1)
-            dv_ref[...]=jnp.concatenate([dvs[t] for t in range(H)],axis=1)
+            grad_ref[...]=jnp.concatenate([x[t] for x in (dqs,dks,dvs) for t in range(H)],axis=1)
+            ride.wait(sent,got,sems)
     full=lambda s: pl.BlockSpec(s,lambda h:(0,)*len(s))
     return pl.pallas_call(kern,grid=(H,),
-        out_shape=(jax.ShapeDtypeStruct((Lq,W),BF),)*3+(jax.ShapeDtypeStruct((H,nb*256),F32),),
-        in_specs=[full((Lq,W))]*5+[full((Lq,128)),full(fwd.shape),full((Lq,HD)),full((Lq,HD))],
-        out_specs=(full((Lq,W)),)*3+(full((H,nb*256)),),
-        scratch_shapes=[pltpu.VMEM((Lq,2*HD),BF)]*5+[pltpu.VMEM((Lq,HD),F32)]*2+[pltpu.VMEM((H,Lq,HD),BF)]*3+[pltpu.VMEM((nb,128,128),F32)]*2,
-        compiler_params=pltpu.CompilerParams(vmem_limit_bytes=48*2**20),name="self_bwd")(q,k,v,do,of,lse,fwd,qa,ka)
+        out_shape=(jax.ShapeDtypeStruct((Lq,3*W),BF),jax.ShapeDtypeStruct((H,nb*256),F32))+ride.shapes,
+        in_specs=[full((Lq,3*W))]+[full((Lq,W))]*2+[full((Lq,128)),full(fwd.shape),full((Lq,HD)),full((Lq,HD))]+[ANY]*ride.count,
+        out_specs=(full((Lq,3*W)),full((H,nb*256)))+(ANY,)*ride.count,
+        scratch_shapes=[pltpu.VMEM((Lq,2*HD),BF)]*5+[pltpu.VMEM((Lq,HD),F32)]*2+[pltpu.VMEM((H,Lq,HD),BF)]*3+[pltpu.VMEM((nb,128,128),F32)]*2+ride.scratch,
+        compiler_params=pltpu.CompilerParams(vmem_limit_bytes=48*2**20,collective_id=2,has_side_effects=True),cost_estimate=cost(35.0),name="self_bwd")(
+            qkv,do,of,lse,fwd,qa,ka,*[x for kind,x in plans])
 
 def fold_bias(gb,Lq):
     H=gb.shape[0]; nb=Lq//128
     x=gb.reshape(H,nb,2,128)
     low=x[:,:,0].reshape(H,Lq); high=x[:,:,1].reshape(H,Lq)
     return high+jnp.concatenate([low[:,128:],jnp.zeros((H,128),gb.dtype)],axis=1)
+
+
+MESH = pl.DeviceIdType.MESH
+
+
+def sum_parts(first, cross, self_out, cross_out, n, wd):
+    devices, count, wide = first.shape
+    total = self_out.shape[0]
+
+    def kern(first_ref, cross_ref, self_out_ref, cross_out_ref, sum_ref, col_ref, mean_ref):
+        lane = lax.broadcasted_iota(jnp.int32, (count, 128), 1)
+        means = jnp.zeros((count, 128), F32)
+        sums = [None] * 8
+        for ref, matrices in ((first_ref, (0, 1, 2)), (cross_ref, (4, 5, 6))):
+            parts = []
+            for s in range(n):
+                part = ref[s].astype(F32)
+                for r in range(1, devices // n):
+                    part = part + ref[r * n + s].astype(F32)
+                parts.append(part)
+            for k, j in enumerate(matrices):
+                if j > 4:
+                    low = range(wd + (k - 1) * HD, 3 * wd, 2 * HD)
+                    pieces = [part[:, c : c + HD] for part in parts for c in low]
+                else:
+                    pieces = [part[:, k * wd : (k + 1) * wd] for part in parts]
+                sums[j] = jnp.concatenate(pieces, 1)[:, :D]
+        for j, ref in ((3, self_out_ref), (7, cross_out_ref)):
+            sums[j] = ref[0].astype(F32)
+            for r in range(1, total):
+                sums[j] = sums[j] + ref[r].astype(F32)
+        for j in range(8):
+            square = sums[j] * sums[j]
+            sum_ref[j] = sums[j]
+            col_ref[j : j + 1, :] = jnp.sum(square, 0, keepdims=True)
+            means = jnp.where(lane == j, jnp.mean(square, 1, keepdims=True), means)
+        mean_ref[...] = means
+
+    return pl.pallas_call(
+        kern,
+        out_shape=(
+            jax.ShapeDtypeStruct((8, count, D), F32),
+            jax.ShapeDtypeStruct((8, D), F32),
+            jax.ShapeDtypeStruct((count, 128), F32),
+        ),
+        in_specs=[VM] * 4,
+        out_specs=(VM,) * 3,
+        compiler_params=pltpu.CompilerParams(vmem_limit_bytes=32 * 2**20),
+        cost_estimate=cost(4.0),name="sum_parts",
+    )(first, cross, self_out, cross_out)
+
+
+def sum_everywhere(values, n, rows):
+    count = n * rows
+
+    def kern(x_ref, o_ref, got, mine, out_sem, in_sem, out_sem2, in_sem2):
+        me = lax.axis_index("rows") * n + lax.axis_index("seq")
+
+        def place(step):
+            j = lax.rem(me + step, count)
+            return j, (lax.div(j, n), lax.rem(j, n))
+
+        greet_all(count, n)
+
+        def piece(step):
+            j, device = place(step)
+            return pltpu.make_async_remote_copy(
+                src_ref=x_ref.at[j], dst_ref=got.at[step], send_sem=out_sem.at[step], recv_sem=in_sem.at[step],
+                device_id=device, device_id_type=MESH,
+            )
+
+        def total(step):
+            return pltpu.make_async_remote_copy(
+                src_ref=mine, dst_ref=o_ref.at[me], send_sem=out_sem2.at[step], recv_sem=in_sem2.at[step],
+                device_id=place(step)[1], device_id_type=MESH,
+            )
+
+        def start_piece(step, carry):
+            piece(step).start()
+            return carry
+
+        def add_piece(step, carry):
+            piece(step).wait()
+            return carry + got[step]
+
+        def start_total(step, carry):
+            total(step).start()
+            return carry
+
+        def wait_total(step, carry):
+            total(step).wait()
+            return carry
+
+        lax.fori_loop(1, count, start_piece, 0)
+        mine[...] = lax.fori_loop(1, count, add_piece, x_ref[me])
+        lax.fori_loop(1, count, start_total, 0)
+        o_ref[me] = mine[...]
+        lax.fori_loop(1, count, wait_total, 0)
+
+    return pl.pallas_call(
+        kern,
+        out_shape=jax.ShapeDtypeStruct(values.shape, F32),
+        in_specs=[VM],
+        out_specs=VM,
+        scratch_shapes=[pltpu.VMEM(values.shape, F32), pltpu.VMEM(values.shape[1:], F32)]
+        + [pltpu.SemaphoreType.DMA((count,))] * 4,
+        compiler_params=pltpu.CompilerParams(collective_id=1, has_side_effects=True),
+        cost_estimate=cost(16.0),name="sum_everywhere",
+    )(values)
 
 
 def normalize(values, scaling):
@@ -337,55 +742,26 @@
         extra = wide - values.shape[-1]
         return values if extra == 0 else jnp.pad(values, [(0, 0)] * (values.ndim - 1) + [(0, extra)])
 
-    def to_seq(values):
-        return lax.all_to_all(values, "seq", 0, 1, tiled=True)
-
-    def along_seq(values):
-        if n % 2:
-            return lax.all_gather(values, "seq", axis=0, tiled=True)
-        shard = lax.axis_index("seq")
-        length = values.shape[0]
-        whole = jnp.zeros((n * length,) + values.shape[1:], values.dtype)
+    def blocks_along_seq(values, gate):
+        blocks = []
         for step in range(0, n, 2):
             block = values
             if step:
-                block = lax.ppermute(values, "seq", [(i, (i + step) % n) for i in range(n)])
-            beside = lax.ppermute(block, "seq", [(i, i ^ 1) for i in range(n)])
-            for part, owner in ((block, shard), (beside, shard ^ 1)):
-                place = lax.rem(owner + n - step, n) * length
-                whole = lax.dynamic_update_slice_in_dim(whole, part, place, 0)
-        return whole
-
-    def own_columns(weight):
-        count, j = weight.shape[:2]
-        parts = jnp.moveaxis(widen(weight).reshape(count, j, n, wd), 2, 0).reshape(1, n, count, j * wd)
-        parts = jnp.broadcast_to(parts, (rows,) + parts.shape[1:]).reshape(devices, count, j * wd)
-        return lax.all_to_all(parts, both, 0, 0, tiled=True).reshape(devices * count, j, wd)
+                block = lax.ppermute(values, "seq", [(i, i ^ step) for i in range(n)])
+                block = lax.optimization_barrier((block, gate))[0]
+            blocks += [block, lax.ppermute(block, "seq", [(i, i ^ 1) for i in range(n)])]
+        return blocks
 
     def by_heads(weight):
         count, j = weight.shape[:2]
-        return jnp.moveaxis(widen(weight).reshape(count, j, n, wd), 2, 1).reshape(count, n * j * wd)
-
-    def sum_columns(gradient):
-        total, width = gradient.shape
-        count, j = total // devices, width // wd
-        got = lax.all_to_all(gradient.astype(BF).reshape(devices, count, width), both, 0, 0, tiled=True)
-        got = jnp.sum(got.reshape(rows, n, count, j, wd).astype(F32), 0)
-        return jnp.moveaxis(got, 0, 2).reshape(count, j, wide)[:, :, :D]
-
-    def sum_rows(gradient):
-        count, width = D // devices, gradient.shape[1]
-        if wide == D and wd == rows * count:
-            got = lax.all_to_all(
-                gradient.astype(BF).reshape(rows, count, width), "rows", 0, 0, tiled=True
-            )
-            got = jnp.sum(got.astype(F32), 0)
-            places = [(r * n + s, s * rows + r) for r in range(rows) for s in range(n)]
-            return lax.ppermute(got, both, places)
-        whole = lax.dynamic_update_slice_in_dim(
-            jnp.zeros((wide, width), BF), gradient.astype(BF), lax.axis_index("seq") * wd, 0
-        )[:D]
-        return lax.psum_scatter(whole, both, scatter_dimension=0, tiled=True).astype(F32)
+        return jnp.moveaxis(widen(weight).reshape(count, j, n * hpd, HD), 2, 1).reshape(count, wide * j)
+
+    def to_seq(values, collective_id):
+        (parts,) = exchange([("seq", values.reshape(n, -1, values.shape[1]))], n, rows, collective_id)
+        return side_by_side(parts)[:, :D]
+
+    def side_by_side(parts):
+        return jnp.moveaxis(parts, 0, 1).reshape(parts.shape[1], -1)
 
     def shards(
         decoder_input,
@@ -418,8 +794,12 @@
         shard = lax.axis_index("seq")
         length = decoder_segment.shape[1]
         attention_low = attention_weight.astype(BF)
-        first_columns = own_columns(attention_low[:, 0:3]).reshape(D, 3 * wd)
-        row_input = along_seq(decoder_input[0])
+        count = expand_weight.shape[0]
+        first_parts = jnp.moveaxis(widen(attention_low[:, 0:3]).reshape(count, 3, n, wd), 2, 0)
+        row_input, first_columns = gather_seq(
+            decoder_input[0], n, rows, 3, [("own", first_parts.reshape(n, count, 3 * wd))]
+        )
+        first_columns = first_columns.reshape(D, 3 * wd)
         attention_full = lax.all_gather(
             jnp.concatenate(
                 (
@@ -427,19 +807,36 @@
                     attention_low[:, 7],
                     by_heads(attention_low[:, 4:5]),
                     by_heads(attention_low[:, 5:7]),
-                    by_heads(attention_low[:, 0:3]),
                 ),
                 1,
             ),
             both, axis=0, tiled=True,
         )
-        row_encoder = along_seq(encoder_output[0])
-        expand_full = lax.all_gather(
-            expand_weight.astype(BF).reshape(-1, 2 * FF), both, axis=0, tiled=True
-        )
-        contract_full = lax.all_gather(contract_weight.astype(BF), both, axis=0, tiled=True)
-        edges = (0, D, 2 * D, 2 * D + wide, 2 * D + 3 * wide, 2 * D + 6 * wide)
-        self_out_weight, cross_out_weight, cross_query_weight, cross_pair_weight, first_weight = (
+        deep = -(-contract_weight.shape[0] // count)
+        spare = deep * count - contract_weight.shape[0]
+        contract_low = jnp.pad(contract_weight.astype(BF), ((0, spare), (0, 0)))
+        feed_full = lax.all_gather(
+            jnp.concatenate(
+                (
+                    expand_weight.astype(BF).reshape(count, 2 * FF),
+                    jnp.moveaxis(contract_low.reshape(deep, count, D), 0, 1).reshape(count, deep * D),
+                ),
+                1,
+            ),
+            both, axis=0, tiled=True,
+        )
+        expand_full = feed_full[:, 0 : 2 * FF]
+        contract_full = jnp.concatenate(
+            [
+                feed_full[:, 2 * FF + g * D : 2 * FF + (g + 1) * D].reshape(devices, count, D)[
+                    :, : contract_weight.shape[0] - g * count
+                ]
+                for g in range(deep)
+            ],
+            1,
+        ).reshape(FF, D)
+        edges = (0, D, 2 * D, 2 * D + wide, 2 * D + 3 * wide)
+        self_out_weight, cross_out_weight, cross_query_weight, cross_pair_weight = (
             attention_full[:, low:high] for low, high in zip(edges[:-1], edges[1:])
         )
         cross_query_columns = lax.dynamic_slice_in_dim(cross_query_weight, shard * wd, wd, 1)
@@ -455,11 +852,12 @@
         self_side = jnp.where(
             (document < 3) & ~(decoder_document & (decoder_padding[0][:, None] == 1)), NEG, 0.0
         ).astype(BF)
+        real_document = jnp.where(encoder_padding[0] == 1, encoder_segment[0], -1).reshape(n, -1)
+        real_document = jnp.concatenate(
+            [lax.dynamic_slice_in_dim(real_document, shard ^ p, 1, 0)[0] for p in range(n)]
+        )
         cross_side = jnp.where(
-            (document < 3)
-            & ~((encoder_segment[0][:, None] == document) & (encoder_padding[0][:, None] == 1)),
-            NEG,
-            0.0,
+            (document < 3) & (real_document[:, None] != document), NEG, 0.0
         ).astype(BF)
         onehot = (
             distance_bucket[:, None] == jnp.arange(BUCKETS, dtype=jnp.int32)[None, :]
@@ -483,26 +881,23 @@
 
         row_norm = normalize(row_input.astype(F32), norm_gain[0]).astype(BF)
         self_proj = dot(row_norm, first_columns).astype(BF)
-        query, key, value = (
-            self_proj[:, 0:wd],
-            self_proj[:, wd : 2 * wd],
-            self_proj[:, 2 * wd : 3 * wd],
-        )
         self_heads, self_exact, self_lse = self_fwd(
-            query, key, value, bias_backward, query_side, self_side
+            self_proj, bias_backward, query_side, self_side
         )
         inputs = decoder_input[0].astype(F32)
-        self_out = to_seq(self_heads)[:, :D]
+        self_out = to_seq(self_heads, 8)
         after_self = inputs + dot(self_out, self_out_weight)
+        encoder_blocks = blocks_along_seq(
+            lax.optimization_barrier((encoder_output[0], row_input))[0], after_self
+        )
         cross_norm = normalize(after_self, norm_gain[1]).astype(BF)
-        row_cross_norm = along_seq(cross_norm)
+        row_cross_norm = gather_seq(cross_norm, n, rows, 4)
         cross_query = dot(row_cross_norm, cross_query_columns).astype(BF)
-        cross_pair = dot(row_encoder, cross_columns).astype(BF)
-        cross_key, cross_value = cross_pair[:, 0:wd], cross_pair[:, wd : 2 * wd]
+        cross_pair = project_blocks(encoder_blocks, cross_columns)
         cross_heads, cross_exact, cross_lse = cross_fwd(
-            cross_query, cross_key, cross_value, query_side, cross_side
-        )
-        cross_out = to_seq(cross_heads)[:, :D]
+            cross_query, cross_pair, query_side, cross_side
+        )
+        cross_out = to_seq(cross_heads, 9)
         after_cross = after_self + dot(cross_out, cross_out_weight)
         feed_norm = normalize(after_cross, norm_gain[2]).astype(BF)
         hidden_pair = dot(feed_norm, expand_full)
@@ -519,62 +914,158 @@
         feed_part, feed_gain = norm_back(dot_back(grad_pair, expand_full))
         grad_after_cross = grad_result + feed_part
         cross_branch = grad_after_cross.astype(BF)
-        row_cross_branch = along_seq(cross_branch)
+        down_rows = deep * count - spare
+
+        def feed_gradients(ins, outs):
+            norm_ref, pair_ref, hidden_ref, branch_ref = ins
+            (o_ref,) = outs
+            for c in range(0, 2 * FF, 512):
+                part = tn(norm_ref[...], pair_ref[:, c : c + 512])
+                o_ref[:, :, c : c + 512] = part.reshape(devices, count, 512).astype(BF)
+            group = devices * 1024 // FF
+            for c in range(0, FF, 1024):
+                part = tn(hidden_ref[:, c : c + 1024], branch_ref[...]).reshape(group, down_rows, D)
+                first = c // 1024 * group
+                for g in range(deep):
+                    piece = part[:, g * count : (g + 1) * count]
+                    if piece.shape[1] < count:
+                        low = jnp.zeros((group, count - piece.shape[1], D), F32)
+                        piece = jnp.concatenate((piece, low), 1)
+                    o_ref[first : first + group, :, 2 * FF + g * D : 2 * FF + (g + 1) * D] = piece.astype(BF)
+
+        if count % 8 == 0:
+            row_cross_branch, feed_local = gather_seq(
+                cross_branch, n, rows, 5,
+                job=Job(
+                    (feed_norm, grad_pair, hidden, feed_branch),
+                    (jax.ShapeDtypeStruct((devices, count, 2 * FF + deep * D), BF),),
+                    feed_gradients,
+                ),
+            )
+            feed_local = feed_local.reshape(D, -1)
+        else:
+            row_cross_branch = gather_seq(cross_branch, n, rows, 5)
+            contract_local = outer(hidden, feed_branch).astype(BF).reshape(devices, -1, D)
+            contract_local = jnp.pad(contract_local, ((0, 0), (0, spare), (0, 0)))
+            feed_local = jnp.concatenate(
+                [outer(feed_norm, grad_pair).astype(BF)]
+                + [contract_local[:, g * count : (g + 1) * count].reshape(D, D) for g in range(deep)],
+                1,
+            )
+        feed_sum = lax.psum_scatter(feed_local, both, scatter_dimension=0, tiled=True).astype(F32)
         cross_grad = dot_back(row_cross_branch, own_rows(cross_out_weight)).astype(BF)
-        cross_out_sum = sum_rows(outer(cross_heads, row_cross_branch))
-        contract_sum = lax.psum_scatter(
-            outer(hidden, feed_branch).astype(BF), both, scatter_dimension=0, tiled=True
-        ).astype(F32)
-        expand_sum = lax.psum_scatter(
-            outer(feed_norm, grad_pair).astype(BF), both, scatter_dimension=0, tiled=True
-        ).astype(F32).reshape(-1, 2, FF)
-        cross_qgrad, cross_kgrad, cross_vgrad = cross_bwd(
-            cross_query, cross_key, cross_value, cross_grad, cross_exact, cross_lse, query_side, cross_side
-        )
-        grad_cross_query = to_seq(cross_qgrad)
+        expand_sum = feed_sum[:, 0 : 2 * FF].reshape(count, 2, FF)
+        contract_sum = jnp.concatenate(
+            [feed_sum[:, 2 * FF + g * D : 2 * FF + (g + 1) * D] for g in range(deep)], 0
+        )[: deep * count - spare]
+        cross_qparts, cross_home, cross_qgrad, cross_last, *cross_grads = cross_bwd(
+            cross_query, cross_pair, cross_grad, cross_exact, cross_lse, query_side, cross_side, n
+        )
+        grad_cross_query = side_by_side(cross_qparts)[:, :D]
         unused_norm, norm_back = jax.vjp(normalize, after_self, norm_gain[1])
-        cross_part, cross_gain = norm_back(dot_back(grad_cross_query, cross_query_weight))
+        cross_part, cross_gain = norm_back(dot_back(grad_cross_query, cross_query_weight[:, :D]))
         grad_after_self = grad_after_cross + cross_part
         self_branch = grad_after_self.astype(BF)
-        row_self_branch = along_seq(self_branch)
+        def cross_gradients(ins, outs):
+            norm_ref, query_ref, heads_ref, branch_ref = ins[:4]
+            o_ref, out_ref = outs
+            o_ref[:, 0:wd] = tn(norm_ref[...], query_ref[...]).astype(BF)
+            pair = tn(ins[4][...], ins[4 + n][...])
+            for p in range(1, n):
+                pair = pair + tn(ins[4 + p][...], ins[4 + n + p][...])
+            o_ref[:, wd : 3 * wd] = pair.astype(BF)
+            out_ref[...] = tn(heads_ref[...], branch_ref[...]).astype(BF)
+
+        row_self_branch, cross_local, cross_out_local = gather_seq(
+            self_branch, n, rows, 6,
+            job=Job(
+                (row_cross_norm, cross_qgrad.reshape(-1, wd), cross_heads, row_cross_branch)
+                + tuple(encoder_blocks) + tuple(cross_grads),
+                (jax.ShapeDtypeStruct((D, 3 * wd), BF), jax.ShapeDtypeStruct((wd, D), BF)),
+                cross_gradients,
+            ),
+        )
         self_grad = dot_back(row_self_branch, own_rows(self_out_weight)).astype(BF)
-        self_out_sum = sum_rows(outer(self_heads, row_self_branch))
-        cross_grads = jnp.concatenate((cross_kgrad, cross_vgrad), 1)
-        cross_sum = sum_columns(
-            jnp.concatenate(
-                (outer(row_cross_norm, cross_qgrad), outer(row_encoder, cross_grads)), 1
-            )
-        )
-        encoder_gradient = dot_back(
-            to_seq(cross_grads), cross_pair_weight
-        )
-        self_qgrad, self_kgrad, self_vgrad, pair_bias = self_bwd(
-            query, key, value, self_grad, self_exact, self_lse, bias_forward, query_side, self_side
-        )
+        self_out_local = outer(self_heads, row_self_branch).astype(BF)
+        matched = wide == D and wd == rows * count
+        plans = [
+            ("all", cross_local.reshape(devices, count, 3 * wd)),
+            ("xor", cross_last),
+        ]
+        rows_local = (self_out_local, cross_out_local)
+        if matched:
+            plans += [("rows", x.reshape(rows, count, D)) for x in rows_local]
+        self_grads, pair_bias, cross_parts, cross_last_home, *rows_parts = self_bwd(
+            self_proj, self_grad, self_exact, self_lse, bias_forward, query_side, self_side, plans, n, rows
+        )
+        if not matched:
+            padded = lax.dynamic_update_slice_in_dim(
+                jnp.zeros((wide, 2 * D), BF), jnp.concatenate(rows_local, 1), shard * wd, 0
+            )[:D]
+            whole = lax.psum_scatter(padded, both, scatter_dimension=0, tiled=True)[None]
+            rows_parts = [whole[:, :, :D], whole[:, :, D:]]
         grad_bias = fold_bias(pair_bias, length)
         table_own_grad = jnp.einsum("hd,db->bh", grad_bias, onehot, precision=HIGHEST)
         table_local = lax.dynamic_update_slice_in_dim(
             jnp.zeros((BUCKETS, n * hpd), F32), table_own_grad, shard * hpd, 1
         )[:, :HEADS]
-        self_grads = jnp.concatenate((self_qgrad, self_kgrad, self_vgrad), 1)
-        self_sum = sum_columns(outer(row_norm, self_grads))
+        self_back = dot_back(self_grads, first_columns).astype(BF)
+        def encoder_job(ins, outs):
+            home_ref, last_ref, weight_ref = ins
+            total = None
+            for t in range(n):
+                for h in range(hpd):
+                    grads = last_ref[t] if h == hpd - 1 else home_ref[t, h]
+                    low = (t * hpd + h) * 2 * HD
+                    part = nt(grads, weight_ref[:, low : low + 2 * HD])
+                    total = part if total is None else total + part
+            outs[0][...] = total
+
+        self_back_parts, self_parts, encoder_gradient = exchange(
+            [
+                ("seq", self_back.reshape(n, -1, D)),
+                ("all", outer(row_norm, self_grads).astype(BF).reshape(devices, count, 3 * wd)),
+            ],
+            n, rows, 7,
+            job=Job(
+                (cross_home, cross_last_home, cross_pair_weight),
+                (jax.ShapeDtypeStruct(encoder_output.shape[1:], F32),),
+                encoder_job,
+            ),
+        )
         unused_norm, norm_back = jax.vjp(normalize, inputs, norm_gain[0])
-        self_part, self_gain = norm_back(
-            dot_back(to_seq(self_grads), first_weight)
-        )
+        self_part, self_gain = norm_back(jnp.sum(self_back_parts.astype(F32), 0))
         input_gradient = grad_after_self + self_part
 
-        attention_sum = jnp.concatenate(
-            (self_sum, self_out_sum[:, None], cross_sum, cross_out_sum[:, None]), 1
-        )
-        attention_rows, attention_columns, attention_rowsum = factored_start(
-            attention_sum, attention_rowwise
-        )
+        attention_parts, attention_columns, attention_means = sum_parts(
+            self_parts, cross_parts, *rows_parts, n, wd
+        )
+        attention_sum = jnp.moveaxis(attention_parts, 0, 1)
+        attention_rows = BETA_TWO * attention_rowwise + (1.0 - BETA_TWO) * attention_means[:, 0:8].T
+        attention_rowsum = jnp.sum(attention_rows, 1)
         expand_rows, expand_columns, expand_rowsum = factored_start(expand_sum, expand_rowwise)
         contract_rows, contract_columns, contract_rowsum = factored_start(
             contract_sum[:, None, :], contract_rowwise[None, :]
         )
         gain_local = jnp.stack((self_gain, cross_gain, feed_gain), 0)
+        pieces = (
+            attention_columns,
+            expand_columns,
+            contract_columns,
+            attention_rowsum,
+            expand_rowsum,
+            contract_rowsum,
+            gain_local,
+            table_local,
+        )
+        flat = jnp.concatenate([piece.reshape(-1) for piece in pieces])
+        size = devices * 8 * 128 * -(-flat.shape[0] // (devices * 8 * 128))
+        flat = jnp.pad(flat, (0, size - flat.shape[0])).reshape(devices, -1, 128)
+        flat = sum_everywhere(flat, n, rows).reshape(-1)
+        sums, start = [], 0
+        for piece in pieces:
+            sums.append(flat[start : start + piece.size].reshape(piece.shape))
+            start += piece.size
         (
             attention_total,
             expand_total,
@@ -584,19 +1075,7 @@
             contract_rowtotal,
             gain_gradient,
             table_gradient,
-        ) = lax.psum(
-            (
-                attention_columns,
-                expand_columns,
-                contract_columns,
-                attention_rowsum,
-                expand_rowsum,
-                contract_rowsum,
-                gain_local,
-                table_local,
-            ),
-            both,
-        )
+        ) = sums
         attention_new = factored_finish(
             attention_sum,
             attention_moment,

time: 628 us -> 546 us (0.87)
  Pallas kernels: 135 us -> 392 us
  waiting for transfers between devices: 161 us -> 0.08 us
  blocking collectives: 53 us -> 0 us
  starting transfers between devices: 55.5 us -> 3.22 us
  matrix products: 86.5 us -> 44.4 us
  local copies, waits for them, and re-layouts: 83.9 us -> 47.7 us
    pallas_call x2 -> x12, Pallas kernels: 89.8 us -> 347 us  [the longest x4 94.4 us: gather_seq(): pl.pallas_call(kern, out_shape=(jax.ShapeDtypeStruct((n, length, features...]
    ppermute x17 -> x3, waiting for transfers between devices: 73 us -> 0.01 us  [the longest x2 0.01 us: blocks_along_seq(): lax.ppermute(block, 'seq', [(i, i ^ 1) for i in range(n)])]
    all_gather x2 -> x1, waiting for transfers between devices: 44.2 us -> 0.01 us  [shards(): lax.all_gather(jnp.concatenate((expand_weight.astype(BF).reshape(count, 2...]
    all_to_all x9 -> x0, waiting for transfers between devices: 43.9 us -> none  [the longest x4 20.5 us: to_seq(): return lax.all_to_all(values, 'seq', 0, 1, tiled=True)]
    all_to_all x9 -> x0, starting transfers between devices: 43.2 us -> none  [the longest x4 18.2 us: to_seq(): return lax.all_to_all(values, 'seq', 0, 1, tiled=True)]
    psum x1 -> x0, blocking collectives: 39.8 us -> none  [shards(): lax.psum((attention_columns, expand_columns, contract_columns, attention_...]
    dot_general x7 -> x2, matrix products: 29.5 us -> 5.69 us  [outer(): lax.dot_general(left, right, (((0,), (0,)), ((), ())), preferred_element_...]
    dynamic_update_slice x17 -> x0, local copies, waits for them, and re-layouts: 22.1 us -> none  [along_seq(): whole = lax.dynamic_update_slice_in_dim(whole, part, place, 0)]
  transfers between devices with their start and end apart: 31 -> 6, of which waited for: 13 -> 0; matrix products, arithmetic and copies ran while one was open for 26% -> 12% of each run, Pallas kernels for 22% -> 66%
where the time goes in v2:
time: 546 us; the launch traced here: 536 us
  Pallas kernels  392 us (72%)
  local copies, waits for them, and re-layouts  47.7 us (9%)
  matrix products  44.4 us (8%)
  other arithmetic  31.6 us (6%)
  between operations  16.3 us (3%)
    pallas_call x4, Pallas kernels, gather_seq(): pl.pallas_call(kern, out_shape=(jax.ShapeDtypeStruct((n, length, features...  94.4 us
    pallas_call x3, Pallas kernels, exchange(): pl.pallas_call(kern, out_shape=ride.shapes + job.outs, in_specs=[ANY] * (...  85.9 us
    pallas_call x1, Pallas kernels, cross_bwd(): pl.pallas_call(kern, grid=(H, nq), out_shape=(jax.ShapeDtypeStruct((n, Lq...  80.3 us
    pallas_call x1, Pallas kernels, self_bwd(): pl.pallas_call(kern, grid=(H,), out_shape=(jax.ShapeDtypeStruct((Lq, 3 *...  61.2 us
    pallas_call x1, Pallas kernels, cross_fwd(): pl.pallas_call(kern, grid=(Lq // qb,), out_shape=(jax.ShapeDtypeStruct((L...  31.1 us
    unnamed x178, local copies, waits for them, and re-layouts  21 us
    dot_general x6, matrix products, dot_back(): lax.dot_general(left, right, (((1,), (1,)), ((), ())), preferred_element_...  20.6 us
    pallas_call x1, Pallas kernels, sum_everywhere(): pl.pallas_call(kern, out_shape=jax.ShapeDtypeStruct(values.shape, F32), i...  18.6 us
  transfers between devices with their start and end apart: 6, of which 0 were waited for; matrix products, arithmetic and copies ran while one was open for 12% of the time, Pallas kernels for 66%

profile of v2, /device:TPU:0, one launch (start us, length us, event | category | flops | bytes accessed | tf_op | source)
XLA Modules:
  0.0 535.5 jit_solution(14767598310098353895)
XLA Ops:
  12.2 32.8 %gather_seq.4 = (bf16[4,352,768]{2,1,0:T(8,128)(2,1)}, bf16[32,24,576]{2,1,0:T(8,128)(2,1)}) custom-call(bf16[352,768]{1,0:T(8,128)(2,1)} %bitcast.126, bf16[4,24,576]{2,1,0:T(8,128)(2,1)} %reshape.345.refs_1_), custom_call_target="tpu_custom_call" | custom-call | flops 20000000000 | bytes 60000000 | tf_op jit(solution)/shard_map/gather_seq/pallas_call | solution.py:461
  49.8 2.4 fusion.4
  56.7 14.4 %self_fwd.1 = (bf16[1408,192]{1,0:T(8,128)(2,1)S(1)}, f32[1408,192]{1,0:T(8,128)S(1)}, f32[1408,128]{1,0:T(8,128)S(1)}) custom-call(bf16[1408,576]{1,0:T(8,128)(2,1)S(1)} %convolution_convert_fusion.1.qkv_ref, f32[3,1536]{1,0:T(4,128)S(1)} %concatenate.30.rev_ref, bf16[1408,64]{1,0:T(8,128)(2,1)S(1)} %fusion.30.qa_ref, ...), custom_call_target="tpu_custom_call" | custom-call | flops 15000000512 | bytes 45000000 | tf_op jit(solution)/shard_map/self_fwd/pallas_call | solution.py:240
  73.2 31.6 %exchange.3 = bf16[4,352,192]{2,1,0:T(8,128)(2,1)} custom-call(bf16[4,352,192]{2,1,0:T(8,128)(2,1)} %bitcast.121), custom_call_target="tpu_custom_call" | custom-call | flops 20000000000 | bytes 60000000 | tf_op jit(solution)/shard_map/exchange/pallas_call | solution.py:392
  108.9 3.0 select_convert_fusion.ka_ref
  112.0 2.3 multiply_reduce_fusion.5
  121.9 18.8 %gather_seq.5 = bf16[4,352,768]{2,1,0:T(8,128)(2,1)} custom-call(bf16[352,768]{1,0:T(8,128)(2,1)} %multiply_convert_fusion.7.refs_0_), custom_call_target="tpu_custom_call" | custom-call | flops 20000000000 | bytes 60000000 | tf_op jit(solution)/shard_map/gather_seq/pallas_call | solution.py:461
  140.7 3.5 convolution_convert_fusion.2.q_ref
  144.2 5.9 %project_blocks.1.kv_ref = bf16[4096,384]{1,0:T(8,128)(2,1)S(1)} custom-call(bf16[1024,768]{1,0:T(8,128)(2,1)S(1)} %bitcast.119, bf16[1024,768]{1,0:T(8,128)(2,1)} %collective-permute-done.refs_1_.refs_6_, bf16[1024,768]{1,0:T(8,128)(2,1)} %collective-permute-done.1.refs_2_.refs_7_, bf16[1024,768]{1,0:T(8,128)(2,1)S(1)} %collective-permute-done.2.refs_3_.refs_8_, ...), custom_call_target="tpu_custom_call" | custom-call | flops 8000000000 | bytes 24000000 | tf_op jit(solution)/shard_map/project_blocks/pallas_call | solution.py:487
  151.7 31.1 %cross_fwd.1 = (bf16[1408,192]{1,0:T(8,128)(2,1)}, f32[1408,192]{1,0:T(8,128)}, f32[1408,128]{1,0:T(8,128)}) custom-call(bf16[1408,192]{1,0:T(8,128)(2,1)} %convolution_convert_fusion.2.q_ref, bf16[4096,384]{1,0:T(8,128)(2,1)} %copy-done.11, bf16[1408,64]{1,0:T(8,128)(2,1)} %copy-done, bf16[4096,64]{1,0:T(8,128)(2,1)} %select_convert_fusion.ka_ref), custom_call_target="tpu_custom_call" | custom-call | flops 31000000512 | bytes 93000000 | tf_op jit(solution)/shard_map/cross_fwd/pallas_call | solution.py:72
  182.8 9.4 %exchange.4 = bf16[4,352,192]{2,1,0:T(8,128)(2,1)} custom-call(bf16[4,352,192]{2,1,0:T(8,128)(2,1)} %bitcast.173), custom_call_target="tpu_custom_call" | custom-call | flops 20000000000 | bytes 60000000 | tf_op jit(solution)/shard_map/exchange/pallas_call | solution.py:392
  192.2 2.2 copy.138
  197.7 2.4 fusion.70
  202.9 2.4 fusion.2
  205.3 4.2 fusion.13
  211.2 3.1 multiply_reduce_fusion
  216.4 22.8 %gather_seq.6 = (bf16[4,352,768]{2,1,0:T(8,128)(2,1)}, bf16[32,24,6400]{2,1,0:T(8,128)(2,1)}) custom-call(bf16[352,768]{1,0:T(8,128)(2,1)} %fusion.61.refs_0_, bf16[352,768]{1,0:T(8,128)(2,1)} %multiply_convert_fusion.6.refs_1_, bf16[352,4096]{1,0:T(8,128)(2,1)} %pad_maximum_fusion.1.refs_2_, bf16[352,2048]{1,0:T(8,128)(2,1)} %get-tuple-element.242.refs_3_, ...), custom_call_target="tpu_custom_call" | custom-call | flops 20000000000 | bytes 60000000 | tf_op jit(solution)/shard_map/gather_seq/pallas_call | solution.py:461
  239.2 3.3 convolution_convert_fusion.4
  242.5 2.2 copy.140.do_ref
  244.8 80.3 %cross_bwd.1 = (bf16[4,352,192]{2,1,0:T(8,128)(2,1)}, bf16[4,2,1024,128]{3,2,1,0:T(8,128)(2,1)}, bf16[4,352,192]{2,1,0:T(8,128)(2,1)}, bf16[4,1024,128]{2,1,0:T(...) custom-call(bf16[1408,192]{1,0:T(8,128)(2,1)} %convolution_convert_f, ...), custom_call_target="tpu_custom_call" | custom-call | flops 67999997952 | bytes 204000000 | tf_op jit(solution)/shard_map/cross_bwd/pallas_call | solution.py:176
  325.0 2.3 copy.141
  327.3 2.5 multiply_reduce_fusion.1
  331.6 20.0 %gather_seq.7 = (bf16[4,352,768]{2,1,0:T(8,128)(2,1)}, bf16[768,576]{1,0:T(8,128)(2,1)}, bf16[192,768]{1,0:T(8,128)(2,1)}) custom-call(bf16[352,768]{1,0:T(8,128)(2,1)} %get-tuple-element.232.refs_0_, bf16[1408,768]{1,0:T(8,128)(2,1)} %bitcast.165, bf16[1408,192]{1,0:T(8,128)(2,1)} %bitcast.174, bf16[1408,192]{1,0:T(8,128)(2,1)} %get-tuple-element.66.refs_3_, ...), custom_call_target="tpu_custom_call" | custom-call | flops 20000000000 | bytes 60000000 | tf_op jit(solution)/shard_map/gather_seq/pallas_call | solution.py:461
  351.7 2.6 convolution_convert_fusion.3
  354.6 2.4 convolution_convert_fusion.5
  357.1 61.2 %self_bwd.1 = (bf16[1408,576]{1,0:T(8,128)(2,1)}, f32[3,2816]{1,0:T(4,128)S(1)}, bf16[32,24,576]{2,1,0:T(8,128)(2,1)S(1)}, bf16[4,1024,128]{2,1,0:T(8,128)(2,1)}...) custom-call(bf16[1408,576]{1,0:T(8,128)(2,1)} %copy-done.10, bf16[1408,192]{1,0:T(8,128)(2,1)S(1)} %copy.142.do_ref, ...), custom_call_target="tpu_custom_call" | custom-call | flops 35000000512 | bytes 105000000 | tf_op jit(solution)/shard_map/self_bwd/pallas_call | solution.py:574
  418.3 3.3 fusion.18
  422.9 5.0 convolution_convert_fusion
  427.9 44.9 %exchange.5 = (bf16[4,352,768]{2,1,0:T(8,128)(2,1)}, bf16[32,24,576]{2,1,0:T(8,128)(2,1)}, f32[1024,768]{1,0:T(8,128)}) custom-call(bf16[4,352,768]{2,1,0:T(8,128)(2,1)} %bitcast.170, bf16[32,24,576]{2,1,0:T(8,128)(2,1)} %bitcast.136, bf16[4,2,1024,128]{3,2,1,0:T(8,128)(2,1)} %get-tuple-element.83.refs_2_, bf16[4,1024,128]{2,1,0:T(8,128)(2,1)} %get-tuple-element.84.refs_3_, ...), custom_call_target="tpu_custom_call" | custom-call | flops 20000000000 | bytes 60000000 | tf_op jit(solution)/shard_map/exchange/pallas_call | solution.py:392
  482.6 4.0 fusion.20
  491.7 18.6 %sum_everywhere.1 = f32[32,8,128]{2,1,0:T(8,128)} custom-call(f32[32,8,128]{2,1,0:T(8,128)} %pad_bitcast_fusion.x_ref), custom_call_target="tpu_custom_call" | custom-call | flops 16000000000 | bytes 48000000 | tf_op jit(solution)/shard_map/sum_everywhere/pallas_call | solution.py:686
  524.8 3.8 copy.185
  (297 shorter events, 70.9 us)
Async XLA Ops:
  7.2 104.7 %all-gather.3.cloned.1.call-start = ((), (), s32[]{:S(2)}) async-start(), calls=%async_computation.1 | async-start | bytes 6082560 | tf_op jit(solution)/shard_map/all_gather | solution.py:803
  9.8 187.9 %all-gather.5.cloned.1.call-start = ((), (), s32[]{:S(2)}) async-start(), calls=%async_computation.2 | async-start | bytes 10137600 | tf_op jit(solution)/shard_map/all_gather | solution.py:818
  11.0 475.6 %reduce-scatter.2.cloned.1.call-start = ((), (), s32[]{:S(2)}) async-start(), calls=%async_computation.3 | async-start | bytes 10137600 | tf_op jit(solution)/shard_map/reduce_scatter | solution.py:955
  12.2 32.8 %copy-start.4 = (bf16[1,1024,768]{2,1,0:T(8,128)(2,1)S(1)}, bf16[1,1024,768]{2,1,0:T(8,128)(2,1)}, u32[]{:S(2)}) copy-start(bf16[1,1024,768]{2,1,0:T(8,128)(2,1)} %param.27) | copy-start | bytes 4718596
  12.2 34.9 %copy-start.79 = (s32[1408]{0:T(1024)S(1)}, s32[1408]{0:T(1024)}, u32[]{:S(2)}) copy-start(s32[1408]{0:T(1024)} %param.33) | copy-start | bytes 16900
  12.2 37.1 %copy-start.70 = (s32[1,1408]{1,0:T(1,128)S(1)}, s32[1,1408]{1,0:T(1,128)}, u32[]{:S(2)}) copy-start(s32[1,1408]{1,0:T(1,128)} %param.29) | copy-start | bytes 16900
  12.2 37.1 %copy-start.59 = (s32[1,4096]{1,0:T(1,128)S(1)}, s32[1,4096]{1,0:T(1,128)}, u32[]{:S(2)}) copy-start(s32[1,4096]{1,0:T(1,128)} %param.31) | copy-start | bytes 49156
  12.2 37.1 %copy-start.60 = (s32[1,4096]{1,0:T(1,128)S(1)}, s32[1,4096]{1,0:T(1,128)}, u32[]{:S(2)}) copy-start(s32[1,4096]{1,0:T(1,128)} %param.32) | copy-start | bytes 49156
  12.2 37.3 %copy-start.71 = (s32[1,1408]{1,0:T(1,128)S(1)}, s32[1,1408]{1,0:T(1,128)}, u32[]{:S(2)}) copy-start(s32[1,1408]{1,0:T(1,128)} %param.30) | copy-start | bytes 16900
  12.2 37.3 %copy-start.47 = (f32[3,768]{1,0:T(4,128)S(1)}, f32[3,768]{1,0:T(4,128)}, u32[]{:S(2)}) copy-start(f32[3,768]{1,0:T(4,128)} %param.46) | copy-start | bytes 27652
  12.2 37.3 %copy-start.19 = (bf16[1,352,768]{2,1,0:T(8,128)(2,1)S(1)}, bf16[1,352,768]{2,1,0:T(8,128)(2,1)}, u32[]{:S(2)}) copy-start(bf16[1,352,768]{2,1,0:T(8,128)(2,1)} %param.26) | copy-start | bytes 1622020
  45.0 99.1 %collective-permute-start = (bf16[1024,768]{1,0:T(8,128)(2,1)S(1)}, bf16[1024,768]{1,0:T(8,128)(2,1)}, u32[]{:S(2)}, u32[]{:S(2)}) collective-permute-start(bf16[1024,768]{1,0:T(8,128)(2,1)S(1)} %bitcast.117), channel_id=1, source_target_pairs={{0,1},{1,0},{2,3},{3,2},{4,5},{5,4},{6,7},{7,6},{8,9},{9,8},{10,11... | collective-permute-start | bytes 4718600 | tf_op jit(solution)/shard_map/ppermute | solution.py:752
  45.5 68.8 %collective-permute-start.1 = (bf16[1024,768]{1,0:T(8,128)(2,1)S(1)}, bf16[1024,768]{1,0:T(8,128)(2,1)}, u32[]{:S(2)}, u32[]{:S(2)}) collective-permute-start(bf16[1024,768]{1,0:T(8,128)(2,1)S(1)} %bitcast.118), channel_id=1, source_target_pairs={{0,2},{1,3},{2,0},{3,1},{4,6},{5,7},{6,4},{7,5},{8,10},{9,11},{10,... | collective-permute-start | bytes 4718600 | tf_op jit(solution)/shard_map/ppermute | solution.py:750
  49.6 67.9 %copy-start.49 = (f32[768]{0:T(1024)}, f32[768]{0:T(1024)S(1)}, u32[]{:S(2)}) copy-start(f32[768]{0:T(1024)S(1)} %get-tuple-element.211) | copy-start | bytes 9220
  49.8 58.5 %copy-start.56 = (f32[352]{0:T(512)}, f32[352]{0:T(512)S(1)}, u32[]{:S(2)}) copy-start(f32[352]{0:T(512)S(1)} %fusion.25) | copy-start | bytes 4228
  55.3 15.8 %copy-start.10 = (bf16[1408,576]{1,0:T(8,128)(2,1)}, bf16[1408,576]{1,0:T(8,128)(2,1)S(1)}, u32[]{:S(2)}) copy-start(bf16[1408,576]{1,0:T(8,128)(2,1)S(1)} %convolution_convert_fusion.1.qkv_ref) | copy-start | bytes 4866052
  55.6 15.5 %copy-start = (bf16[1408,64]{1,0:T(8,128)(2,1)}, bf16[1408,64]{1,0:T(8,128)(2,1)S(1)}, u32[]{:S(2)}) copy-start(bf16[1408,64]{1,0:T(8,128)(2,1)S(1)} %fusion.30.qa_ref) | copy-start | bytes 540676
  73.2 34.5 %copy-start.74 = (f32[8,24]{1,0:T(8,128)S(1)}, f32[8,24]{1,0:T(8,128)}, u32[]{:S(2)}) copy-start(f32[8,24]{1,0:T(8,128)} %param.36) | copy-start | bytes 2308
  114.3 29.8 %collective-permute-start.2 = (bf16[1024,768]{1,0:T(8,128)(2,1)}, bf16[1024,768]{1,0:T(8,128)(2,1)S(1)}, u32[]{:S(2)}, u32[]{:S(2)}) collective-permute-start(bf16[1024,768]{1,0:T(8,128)(2,1)} %collective-permute-done.1.refs_2_.refs_7_), channel_id=1, source_target_pairs={{0,1},{1,0},{2,3},{3,2},{4,5},{5,4},{6,7},{7,6},{8,9},{9,8},{10,11... | collective-permute-start | bytes 4718600 | tf_op jit(solution)/shard_map/ppermute | solution.py:752
  196.6 133.3 %copy-start.14 = (f32[352,768]{1,0:T(8,128)}, f32[352,768]{1,0:T(8,128)S(1)}, u32[]{:S(2)}) copy-start(f32[352,768]{1,0:T(8,128)S(1)} %get-tuple-element.256) | copy-start | bytes 3244036
  244.7 82.6 %copy-start.50 = (f32[768]{0:T(1024)S(1)}, f32[768]{0:T(1024)}, u32[]{:S(2)}) copy-start(f32[768]{0:T(1024)} %copy-done.49) | copy-start | bytes 9220
  244.7 82.6 %copy-start.54 = (f32[352]{0:T(512)S(1)}, f32[352]{0:T(512)}, u32[]{:S(2)}) copy-start(f32[352]{0:T(512)} %copy-done.53) | copy-start | bytes 4228
  357.0 61.2 %copy-start.17 = (bf16[4,352,768]{2,1,0:T(8,128)(2,1)S(1)}, bf16[4,352,768]{2,1,0:T(8,128)(2,1)}, u32[]{:S(2)}) copy-start(bf16[4,352,768]{2,1,0:T(8,128)(2,1)} %get-tuple-element.61) | copy-start | bytes 6488068
  357.1 61.2 %copy-start.44 = (f32[768]{0:T(1024)S(1)}, f32[768]{0:T(1024)}, u32[]{:S(2)}) copy-start(f32[768]{0:T(1024)} %copy-done.43) | copy-start | bytes 9220
  357.1 61.2 %copy-start.67 = (f32[1408]{0:T(1024)S(1)}, f32[1408]{0:T(1024)}, u32[]{:S(2)}) copy-start(f32[1408]{0:T(1024)} %rsqrt.47) | copy-start | bytes 16900
  489.0 32.7 %copy-start.25 = (f32[24,2,2048]{2,1,0:T(2,128)}, f32[24,2,2048]{2,1,0:T(2,128)S(1)}, u32[]{:S(2)}) copy-start(f32[24,2,2048]{2,1,0:T(2,128)S(1)} %reshape.373) | copy-start | bytes 1179652
  489.5 29.3 %copy-start.75 = (f32[2,24]{1,0:T(2,128)}, f32[2,24]{1,0:T(2,128)S(1)}, u32[]{:S(2)}) copy-start(f32[2,24]{1,0:T(2,128)S(1)} %get-tuple-element.295) | copy-start | bytes 580
  489.7 34.2 %copy-start.36 = (f32[64,768]{1,0:T(8,128)}, f32[64,768]{1,0:T(8,128)S(1)}, u32[]{:S(2)}) copy-start(f32[64,768]{1,0:T(8,128)S(1)} %get-tuple-element.298) | copy-start | bytes 589828
  490.3 33.5 %copy-start.76 = (f32[64]{0:T(128)}, f32[64]{0:T(128)S(1)}, u32[]{:S(2)}) copy-start(f32[64]{0:T(128)S(1)} %get-tuple-element.300) | copy-start | bytes 772
  491.7 24.3 %copy-start.52 = (f32[8,768]{1,0:T(8,128)S(1)}, f32[8,768]{1,0:T(8,128)}, u32[]{:S(2)}) copy-start(f32[8,768]{1,0:T(8,128)} %param.37) | copy-start | bytes 73732
  491.7 24.3 %copy-start.28 = (f32[24,8,768]{2,1,0:T(8,128)S(1)}, f32[24,8,768]{2,1,0:T(8,128)}, u32[]{:S(2)}) copy-start(f32[24,8,768]{2,1,0:T(8,128)} %param.34) | copy-start | bytes 1769476
  491.7 24.3 %copy-start.37 = (f32[24,8,768]{2,1,0:T(8,128)S(1)}, f32[24,8,768]{2,1,0:T(8,128)}, u32[]{:S(2)}) copy-start(f32[24,8,768]{2,1,0:T(8,128)} %param.35) | copy-start | bytes 1769476
  (57 other events, 203.0 us)
Sparse Core Ops, SparseCore 0:
  11.5 95.8 all-gather.2
  110.9 82.4 all-gather.4
  244.8 164.3 reduce-scatter.1

commit v3 on v2

--- a/solution.py
+++ b/solution.py
@@ -81,34 +81,34 @@
     b=r.astype(BF); c=(r-b.astype(F32)).astype(BF)
     return a,b,c
 
-def cross_bwd(q,kv,do,of,lse,qa,ka,n,qb=256,kc=1024):
-    Lq,W=q.shape; Lk=kv.shape[0]; H=W//HD
-    nq=-(-Lq//qb); Lp=nq*qb; nk=Lk//kc
-    def kern(q_ref,kv_ref,do_ref,of_ref,lse_ref,qa_ref,ka_ref,dq_ref,home_ref,dqw,last_ref,*rest):
+def cross_bwd(q,kv,do,of,lse,qa,ka,plans,n,rows,qb=256):
+    Lq,W=q.shape; Lk=kv.shape[0]; H=W//HD; kc=Lk//n
+    ride=Exchange(plans,n,rows); riders=ride.scratch if plans else []
+    def kern(q_ref,kv_ref,do_ref,of_ref,lse_ref,qa_ref,ka_ref,*rest):
+        sent,rest=rest[:ride.count],rest[ride.count:]
+        dq_ref,home_ref,dqw=rest[:3]
+        got,rest=rest[3:3+ride.count],rest[3+ride.count:]
+        rest,sems=rest[:len(rest)-len(riders)],rest[len(rest)-len(riders):]
         dkv_refs=rest[:n]
-        (kaug,vaug,qaug,doaug,dkacc,dvacc,dqs,dkvs,q_out,q_in,kv_out,kv_in,own)=rest[n:]
-        h=pl.program_id(0); i=pl.program_id(1)
+        kaug,vaug,qaug,doaug,ps,dss,dqacc,kt,dqs,dkvs,q_out,q_in,kv_out,kv_in,own=rest[n:]
+        h=pl.program_id(0); c=pl.program_id(1)
         r,s=lax.axis_index("rows"),lax.axis_index("seq")
-        def home(p,hh):
-            rows=slice(p*(Lk//n),(p+1)*(Lk//n))
-            peer=s^p
-            return pltpu.make_async_remote_copy(src_ref=dkvs.at[hh,rows],dst_ref=home_ref.at[s,hh],send_sem=kv_out.at[p,hh],
-                recv_sem=kv_in.at[p,hh],device_id=(r,peer),device_id_type=MESH)
-        def keep(hh):
-            return pltpu.make_async_copy(dkvs.at[hh,0:Lk//n],home_ref.at[s,hh],own.at[hh])
+        def home(p):
+            return pltpu.make_async_remote_copy(src_ref=dkvs.at[h,p*kc:(p+1)*kc],dst_ref=home_ref.at[s,h],send_sem=kv_out.at[p,h],
+                recv_sem=kv_in.at[p,h],device_id=(r,s^p),device_id_type=MESH)
+        def keep():
+            return pltpu.make_async_copy(dkvs.at[h,0:kc],home_ref.at[s,h],own.at[h])
         def turn(p):
             return pltpu.make_async_remote_copy(src_ref=dqw.at[s^p],dst_ref=dq_ref.at[s],send_sem=q_out.at[p],
                 recv_sem=q_in.at[p],device_id=(r,s^p),device_id_type=MESH)
         def stay():
             return pltpu.make_async_copy(dqw.at[s],dq_ref.at[s],own.at[H])
-        @pl.when((h==0)&(i==0))
+        @pl.when((h==0)&(c==0))
         def _():
-            barrier=pltpu.get_barrier_semaphore()
-            for p in range(1,n):
-                pl.semaphore_signal(barrier,inc=1,device_id=(r,s^p),device_id_type=MESH)
-            pl.semaphore_wait(barrier,n-1)
+            greet_all(n*rows if plans else n,n)
+            if plans: ride.start(sent,got,sems,greet=False)
         for hh in range(H):
-            @pl.when((h==hh)&(i==0))
+            @pl.when((h==hh)&(c==0))
             def _():
                 sl=slice(hh*HD,(hh+1)*HD)
                 kaug[:,0:HD]=kv_ref[:,2*hh*HD:(2*hh+1)*HD]
@@ -117,74 +117,67 @@
                 vaug[:,0:HD]=kv_ref[:,(2*hh+1)*HD:(2*hh+2)*HD]
                 vaug[:,HD:2*HD]=jnp.where(lane<3,BF(1),BF(0)).astype(BF)
                 lq=lax.broadcasted_iota(jnp.int32,(Lq,HD),1)
-                a,b,c=split3(-lse_ref[:,hh:hh+1])
-                aug=jnp.where(lq==3,a,jnp.where(lq==4,b,jnp.where(lq==5,c,qa_ref[...])))
+                x,y,z=split3(-lse_ref[:,hh:hh+1])
                 qaug[0:Lq,0:HD]=q_ref[:,sl]*BF(0.125)
-                qaug[0:Lq,HD:2*HD]=aug
+                qaug[0:Lq,HD:2*HD]=jnp.where(lq==3,x,jnp.where(lq==4,y,jnp.where(lq==5,z,qa_ref[...])))
                 dd=do_ref[:,sl]
                 delta=jnp.sum(dd.astype(F32)*of_ref[:,sl],axis=1,keepdims=True)
-                a,b,c=split3(-delta)
-                aug=jnp.where(lq==0,a,jnp.where(lq==1,b,jnp.where(lq==2,c,BF(0))))
+                x,y,z=split3(-delta)
                 doaug[0:Lq,0:HD]=dd
-                doaug[0:Lq,HD:2*HD]=aug
-                if Lp>Lq:
-                    qaug[Lq:Lp,:]=jnp.zeros((Lp-Lq,2*HD),BF)
-                    doaug[Lq:Lp,:]=jnp.zeros((Lp-Lq,2*HD),BF)
-                dkacc[...]=jnp.zeros_like(dkacc)
-                dvacc[...]=jnp.zeros_like(dvacc)
-        off=pl.multiple_of(i*qb,qb)
-        qg=qaug[pl.ds(off,qb),:]
-        dg=doaug[pl.ds(off,qb),:]
-        qp=qg[:,0:HD]; dp_=dg[:,0:HD]
-        dq=jnp.zeros((qb,HD),F32)
-        def step(c,dq):
-            o=pl.multiple_of(c*kc,kc)
-            kk=kaug[pl.ds(o,kc),:]
-            p=jnp.exp(nt(kk,qg))
-            g=nt(vaug[pl.ds(o,kc),:],dg)
-            ds=(p*g).astype(BF)
-            dvacc[pl.ds(o,kc),:]+=nn(p.astype(BF),dp_)
-            dkacc[pl.ds(o,kc),:]+=nn(ds,qp)
-            return dq+tn(ds,kk[:,0:HD])
-        for c in range(nk): dq=step(c,dq)
-        dqs[h,pl.ds(off,qb),:]=(dq*0.125).astype(BF)
-        for hh in range(H):
-            @pl.when((i==nq-1)&(h==hh))
+                doaug[0:Lq,HD:2*HD]=jnp.where(lq==0,x,jnp.where(lq==1,y,jnp.where(lq==2,z,BF(0))))
+                dqacc[...]=jnp.zeros_like(dqacc)
+                for b in range(n):
+                    kt[b]=kv_ref[b*kc:(b+1)*kc,2*hh*HD:(2*hh+1)*HD].astype(F32).T.astype(BF)
+        off=pl.multiple_of((n-1-c)*kc,kc)
+        kk=kaug[pl.ds(off,kc),:]
+        vv=vaug[pl.ds(off,kc),:]
+        for i in range(0,Lq,qb):
+            part=slice(i,min(i+qb,Lq))
+            p=jnp.exp(nt(kk,qaug[part,:]))
+            g=nt(vv,doaug[part,:])
+            ps[:,part]=p.astype(BF)
+            dss[:,part]=(p*g).astype(BF)
+        dkvs[h,pl.ds(off,kc),0:HD]=nn(dss[...],qaug[:,0:HD]).astype(BF)
+        dkvs[h,pl.ds(off,kc),HD:2*HD]=nn(ps[...],doaug[:,0:HD]).astype(BF)
+        dqacc[...]+=nn(kt[n-1-c],dss[...])
+        for p in range(1,n):
+            @pl.when(c==n-1-p)
             def _():
-                dkvs[hh,:,0:HD]=dkacc[...].astype(BF)
-                dkvs[hh,:,HD:]=dvacc[...].astype(BF)
-                if hh==H-1:
-                    for b in range(n):
-                        dqw[b]=jnp.concatenate([dqs[t,b*(Lq//n):(b+1)*(Lq//n),:] for t in range(H)],axis=1)
-                    for p in range(1,n): turn(p).start()
-                    stay().start()
-                else:
-                    for p in range(1,n): home(p,hh).start()
-                    keep(hh).start()
-        @pl.when((i==nq-1)&(h==H-1))
+                home(p).start()
+        @pl.when(c==n-1)
         def _():
+            keep().start()
+            dqs[h]=(dqacc[...].T*0.125).astype(BF)
+        @pl.when((c==n-1)&(h==H-1))
+        def _():
+            for b in range(n):
+                dqw[b]=jnp.concatenate([dqs[t,b*(Lq//n):(b+1)*(Lq//n),:] for t in range(H)],axis=1)
+            for p in range(1,n): turn(p).start()
+            stay().start()
             for b,dkv_ref in enumerate(dkv_refs):
-                part=slice(b*(Lk//n),(b+1)*(Lk//n))
-                for t in range(H): dkv_ref[:,2*t*HD:2*(t+1)*HD]=dkvs[t,part,:]
-                last_ref[b]=dkvs[H-1,part,:]
+                for t in range(H): dkv_ref[:,2*t*HD:2*(t+1)*HD]=dkvs[t,b*kc:(b+1)*kc,:]
             for p in range(1,n): turn(p).wait()
             stay().wait()
-            for hh in range(H-1):
-                for p in range(1,n): home(p,hh).wait()
-                keep(hh).wait()
-    full=lambda s: pl.BlockSpec(s,lambda h,i:(0,)*len(s))
-    return pl.pallas_call(kern,grid=(H,nq),
-        out_shape=(jax.ShapeDtypeStruct((n,Lq//n,W),BF),jax.ShapeDtypeStruct((n,H-1,Lk//n,2*HD),BF),jax.ShapeDtypeStruct((n,Lq//n,W),BF),jax.ShapeDtypeStruct((n,Lk//n,2*HD),BF))+(jax.ShapeDtypeStruct((Lk//n,2*W),BF),)*n,
-        in_specs=[full((Lq,W)),full((Lk,2*W)),full((Lq,W)),full((Lq,W)),full((Lq,128)),full((Lq,HD)),full((Lk,HD))],
-        out_specs=(ANY,ANY,full((n,Lq//n,W)),full((n,Lk//n,2*HD)))+(full((Lk//n,2*W)),)*n,
-        scratch_shapes=[pltpu.VMEM((Lk,2*HD),BF),pltpu.VMEM((Lk,2*HD),BF),pltpu.VMEM((Lp,2*HD),BF),pltpu.VMEM((Lp,2*HD),BF),
-            pltpu.VMEM((Lk,HD),F32),pltpu.VMEM((Lk,HD),F32),pltpu.VMEM((H,Lp,HD),BF),pltpu.VMEM((H,Lk,2*HD),BF)]
-            +[pltpu.SemaphoreType.DMA((n,))]*2+[pltpu.SemaphoreType.DMA((n,H))]*2+[pltpu.SemaphoreType.DMA((H+1,))],
-        compiler_params=pltpu.CompilerParams(vmem_limit_bytes=60*2**20,collective_id=10,has_side_effects=True),cost_estimate=cost(68.0),name="cross_bwd")(q,kv,do,of,lse,qa,ka)
-
-def toeplitz(win, shift):
-    x=jnp.broadcast_to(win,(128,256))
-    return pltpu.roll(x,shift,1,stride=1,stride_axis=0)[:,0:128]
+            if plans: ride.wait(sent,got,sems)
+        @pl.when(c==n-1)
+        def _():
+            for p in range(1,n): home(p).wait()
+            keep().wait()
+    full=lambda s: pl.BlockSpec(s,lambda h,c:(0,)*len(s))
+    return pl.pallas_call(kern,grid=(H,n),
+        out_shape=(jax.ShapeDtypeStruct((n,Lq//n,W),BF),jax.ShapeDtypeStruct((n,H,kc,2*HD),BF),jax.ShapeDtypeStruct((n,Lq//n,W),BF))+ride.shapes+(jax.ShapeDtypeStruct((kc,2*W),BF),)*n,
+        in_specs=[full((Lq,W)),full((Lk,2*W)),full((Lq,W)),full((Lq,W)),full((Lq,128)),full((Lq,HD)),full((Lk,HD))]+[ANY]*ride.count,
+        out_specs=(ANY,ANY,full((n,Lq//n,W)))+(ANY,)*ride.count+(full((kc,2*W)),)*n,
+        scratch_shapes=[pltpu.VMEM((Lk,2*HD),BF),pltpu.VMEM((Lk,2*HD),BF),pltpu.VMEM((Lq,2*HD),BF),pltpu.VMEM((Lq,2*HD),BF),
+            pltpu.VMEM((kc,Lq),BF),pltpu.VMEM((kc,Lq),BF),pltpu.VMEM((HD,Lq),F32),pltpu.VMEM((n,HD,kc),BF),pltpu.VMEM((H,Lq,HD),BF),pltpu.VMEM((H,Lk,2*HD),BF)]
+            +[pltpu.SemaphoreType.DMA((n,))]*2+[pltpu.SemaphoreType.DMA((n,H))]*2+[pltpu.SemaphoreType.DMA((H+1,))]+riders,
+        compiler_params=pltpu.CompilerParams(vmem_limit_bytes=60*2**20,collective_id=10,has_side_effects=True),cost_estimate=cost(68.0),name="cross_bwd")(q,kv,do,of,lse,qa,ka,*[x for kind,x in plans])
+
+def toeplitz(line, shift):
+    return pltpu.roll(jnp.broadcast_to(line,(128,line.shape[1])),shift,1,stride=1,stride_axis=0)
+
+def toeplitz_rows(x):
+    return pltpu.roll(x,1,1,stride=1,stride_axis=0)
 
 def eye128():
     return lax.broadcasted_iota(jnp.int32,(128,128),0)==lax.broadcasted_iota(jnp.int32,(128,128),1)
@@ -204,8 +197,9 @@
         @pl.when(h==0)
         def _():
             lse_ref[...]=jnp.zeros((Lq,128),F32)
+        bands=toeplitz(rev_ref[pl.ds(h,1),:],(nb+1)*128-127)
         for d in range(nb):
-            tz[d]=toeplitz(rev_ref[pl.ds(h,1),(nb-1-d)*128:(nb+1-d)*128],129)
+            tz[d]=bands[:,(nb-1-d)*128:(nb-d)*128]
         eye=eye128()
         lane=lax.broadcasted_iota(jnp.int32,(128,128),1)
         for q0 in range(0,Lq,256):
@@ -530,8 +524,9 @@
         dkacc[...]=jnp.zeros_like(dkacc)
         dvacc[...]=jnp.zeros_like(dvacc)
         ga[...]=jnp.zeros_like(ga)
+        bands=toeplitz(fwd_ref[pl.ds(h,1),:],nb*128)
         for d in range(nb):
-            tz[d]=toeplitz(fwd_ref[pl.ds(h,1),d*128:(d+2)*128],128)
+            tz[d]=bands[:,d*128:(d+1)*128]
         eye=eye128()
         for q0 in range(0,Lq,256):
             qn=min(256,Lq-q0); kend=q0+qn
@@ -562,28 +557,22 @@
         dks[h]=dkacc[...].astype(BF)
         dvs[h]=dvacc[...].astype(BF)
         flip=(lax.broadcasted_iota(jnp.int32,(128,128),0)+lax.broadcasted_iota(jnp.int32,(128,128),1)==127).astype(F32)
-        for d in range(nb):
-            y=lax.dot_general(flip,ga[d],(((1,),(0,)),((),())),preferred_element_type=F32,precision=lax.Precision.HIGHEST)
-            x=pltpu.roll(jnp.concatenate([y,jnp.zeros((128,128),F32)],axis=1),1,1,stride=1,stride_axis=0)
-            gb_ref[pl.ds(h,1),d*256:(d+1)*256]=jnp.sum(x,axis=0,keepdims=True)
+        y=jnp.concatenate([ga[d] for d in range(nb)],axis=1)
+        y=lax.dot_general(flip,y,(((1,),(0,)),((),())),preferred_element_type=F32,precision=lax.Precision.HIGHEST)
+        y=toeplitz_rows(jnp.concatenate([y,jnp.zeros((128,128),F32)],axis=1))
+        gb_ref[pl.ds(h,1),:]=jnp.sum(y,axis=0,keepdims=True)
         @pl.when(h==H-1)
         def _():
             grad_ref[...]=jnp.concatenate([x[t] for x in (dqs,dks,dvs) for t in range(H)],axis=1)
             ride.wait(sent,got,sems)
     full=lambda s: pl.BlockSpec(s,lambda h:(0,)*len(s))
     return pl.pallas_call(kern,grid=(H,),
-        out_shape=(jax.ShapeDtypeStruct((Lq,3*W),BF),jax.ShapeDtypeStruct((H,nb*256),F32))+ride.shapes,
+        out_shape=(jax.ShapeDtypeStruct((Lq,3*W),BF),jax.ShapeDtypeStruct((H,(nb+1)*128),F32))+ride.shapes,
         in_specs=[full((Lq,3*W))]+[full((Lq,W))]*2+[full((Lq,128)),full(fwd.shape),full((Lq,HD)),full((Lq,HD))]+[ANY]*ride.count,
-        out_specs=(full((Lq,3*W)),full((H,nb*256)))+(ANY,)*ride.count,
+        out_specs=(full((Lq,3*W)),full((H,(nb+1)*128)))+(ANY,)*ride.count,
         scratch_shapes=[pltpu.VMEM((Lq,2*HD),BF)]*5+[pltpu.VMEM((Lq,HD),F32)]*2+[pltpu.VMEM((H,Lq,HD),BF)]*3+[pltpu.VMEM((nb,128,128),F32)]*2+ride.scratch,
-        compiler_params=pltpu.CompilerParams(vmem_limit_bytes=48*2**20,collective_id=2,has_side_effects=True),cost_estimate=cost(35.0),name="self_bwd")(
+        compiler_params=pltpu.CompilerParams(vmem_limit_bytes=48*2**20,collective_id=11,has_side_effects=True),cost_estimate=cost(35.0),name="self_bwd")(
             qkv,do,of,lse,fwd,qa,ka,*[x for kind,x in plans])
-
-def fold_bias(gb,Lq):
-    H=gb.shape[0]; nb=Lq//128
-    x=gb.reshape(H,nb,2,128)
-    low=x[:,:,0].reshape(H,Lq); high=x[:,:,1].reshape(H,Lq)
-    return high+jnp.concatenate([low[:,128:],jnp.zeros((H,128),gb.dtype)],axis=1)
 
 
 MESH = pl.DeviceIdType.MESH
@@ -636,28 +625,44 @@
     )(first, cross, self_out, cross_out)
 
 
-def sum_everywhere(values, n, rows):
+def sum_everywhere(arrays, n, rows):
     count = n * rows
-
-    def kern(x_ref, o_ref, got, mine, out_sem, in_sem, out_sem2, in_sem2):
+    wide_tiles, tiles = FF // 128, D // 128
+    table_at, sums_at = tiles + wide_tiles, tiles + wide_tiles + BUCKETS // 8
+    assert sums_at < count
+
+    def kern(att, exp, con, att_rows, exp_rows, con_rows, gain, table, *rest):
+        outs, (x, o, got, mine, out_sem, in_sem, out_sem2, in_sem2) = rest[:6], rest[6:]
         me = lax.axis_index("rows") * n + lax.axis_index("seq")
 
         def place(step):
             j = lax.rem(me + step, count)
             return j, (lax.div(j, n), lax.rem(j, n))
 
+        x[...] = jnp.zeros(x.shape, F32)
+        for t in range(tiles):
+            x[t] = att[:, t * 128 : (t + 1) * 128]
+            x[tiles + t, 2:5, :] = gain[:, t * 128 : (t + 1) * 128]
+            x[tiles + t, 5:6, :] = con[:, t * 128 : (t + 1) * 128]
+        for t in range(wide_tiles):
+            x[tiles + t, 0:2, :] = exp[:, t * 128 : (t + 1) * 128]
+        for t in range(BUCKETS // 8):
+            x[table_at + t, :, 0:HEADS] = table[t * 8 : (t + 1) * 8, :]
+        x[sums_at, :, 0:1] = jnp.sum(att_rows[...], 1, keepdims=True)
+        x[sums_at, 0:2, 1:2] = jnp.sum(exp_rows[...], 1, keepdims=True)
+        x[sums_at, 0:1, 2:3] = jnp.sum(con_rows[...], 1, keepdims=True)
         greet_all(count, n)
 
         def piece(step):
             j, device = place(step)
             return pltpu.make_async_remote_copy(
-                src_ref=x_ref.at[j], dst_ref=got.at[step], send_sem=out_sem.at[step], recv_sem=in_sem.at[step],
+                src_ref=x.at[j], dst_ref=got.at[step], send_sem=out_sem.at[step], recv_sem=in_sem.at[step],
                 device_id=device, device_id_type=MESH,
             )
 
         def total(step):
             return pltpu.make_async_remote_copy(
-                src_ref=mine, dst_ref=o_ref.at[me], send_sem=out_sem2.at[step], recv_sem=in_sem2.at[step],
+                src_ref=mine, dst_ref=o.at[me], send_sem=out_sem2.at[step], recv_sem=in_sem2.at[step],
                 device_id=place(step)[1], device_id_type=MESH,
             )
 
@@ -678,21 +683,34 @@
             return carry
 
         lax.fori_loop(1, count, start_piece, 0)
-        mine[...] = lax.fori_loop(1, count, add_piece, x_ref[me])
+        mine[...] = lax.fori_loop(1, count, add_piece, x[me])
         lax.fori_loop(1, count, start_total, 0)
-        o_ref[me] = mine[...]
+        o[me] = mine[...]
         lax.fori_loop(1, count, wait_total, 0)
-
+        att_out, exp_out, con_out, sums_out, gain_out, table_out = outs
+        for t in range(tiles):
+            att_out[:, t * 128 : (t + 1) * 128] = o[t]
+            gain_out[:, t * 128 : (t + 1) * 128] = o[tiles + t, 2:5, :]
+            con_out[:, t * 128 : (t + 1) * 128] = o[tiles + t, 5:6, :]
+        for t in range(wide_tiles):
+            exp_out[:, t * 128 : (t + 1) * 128] = o[tiles + t, 0:2, :]
+        for t in range(BUCKETS // 8):
+            table_out[t * 8 : (t + 1) * 8, :] = o[table_at + t, :, 0:HEADS]
+        sums_out[...] = o[sums_at]
+
+    shapes = ((8, D), (2, FF), (1, D), (8, 128), (3, D), (BUCKETS, HEADS))
     return pl.pallas_call(
         kern,
-        out_shape=jax.ShapeDtypeStruct(values.shape, F32),
-        in_specs=[VM],
-        out_specs=VM,
-        scratch_shapes=[pltpu.VMEM(values.shape, F32), pltpu.VMEM(values.shape[1:], F32)]
+        out_shape=tuple(jax.ShapeDtypeStruct(shape, F32) for shape in shapes),
+        in_specs=[VM] * 8,
+        out_specs=(VM,) * 6,
+        scratch_shapes=[pltpu.VMEM((count, 8, 128), F32)] * 3
+        + [pltpu.VMEM((8, 128), F32)]
         + [pltpu.SemaphoreType.DMA((count,))] * 4,
         compiler_params=pltpu.CompilerParams(collective_id=1, has_side_effects=True),
-        cost_estimate=cost(16.0),name="sum_everywhere",
-    )(values)
+        cost_estimate=cost(16.0),
+        name="sum_everywhere",
+    )(*arrays)
 
 
 def normalize(values, scaling):
@@ -706,7 +724,7 @@
 def factored_start(gradient, rowwise):
     square = gradient * gradient
     rowwise_new = BETA_TWO * rowwise + (1.0 - BETA_TWO) * jnp.mean(square, 2).T
-    return (rowwise_new, jnp.sum(square, 0), jnp.sum(rowwise_new, 1))
+    return (rowwise_new, jnp.sum(square, 0))
 
 
 def factored_finish(gradient, moment, rowwise_new, colwise, weight, column_sum, row_sum, total_rows):
@@ -907,7 +925,6 @@
         grad_hidden = dot_back(feed_branch, contract_full)
         hidden_wide, gated_back = jax.vjp(gated, gate_values, up_values)
         hidden = hidden_wide.astype(BF)
-        layer_output = (after_cross + dot(hidden, contract_full)).astype(BF)
         grad_gate, grad_up = gated_back(grad_hidden)
         grad_pair = jnp.concatenate((grad_gate.astype(BF), grad_up.astype(BF)), 1)
         unused_norm, norm_back = jax.vjp(normalize, after_cross, norm_gain[2])
@@ -958,81 +975,84 @@
         contract_sum = jnp.concatenate(
             [feed_sum[:, 2 * FF + g * D : 2 * FF + (g + 1) * D] for g in range(deep)], 0
         )[: deep * count - spare]
-        cross_qparts, cross_home, cross_qgrad, cross_last, *cross_grads = cross_bwd(
-            cross_query, cross_pair, cross_grad, cross_exact, cross_lse, query_side, cross_side, n
-        )
+        matched = wide == D and wd == rows * count
+        cross_out_local = outer(cross_heads, row_cross_branch).astype(BF)
+        cross_plans = [("rows", cross_out_local.reshape(rows, count, D))] if matched else []
+        cross_qparts, cross_home, cross_qgrad, *cross_grads = cross_bwd(
+            cross_query, cross_pair, cross_grad, cross_exact, cross_lse, query_side, cross_side, cross_plans, n, rows
+        )
+        cross_rows, cross_grads = cross_grads[: len(cross_plans)], cross_grads[len(cross_plans) :]
         grad_cross_query = side_by_side(cross_qparts)[:, :D]
         unused_norm, norm_back = jax.vjp(normalize, after_self, norm_gain[1])
         cross_part, cross_gain = norm_back(dot_back(grad_cross_query, cross_query_weight[:, :D]))
         grad_after_self = grad_after_cross + cross_part
         self_branch = grad_after_self.astype(BF)
         def cross_gradients(ins, outs):
-            norm_ref, query_ref, heads_ref, branch_ref = ins[:4]
-            o_ref, out_ref = outs
+            norm_ref, query_ref = ins[:2]
+            (o_ref,) = outs
             o_ref[:, 0:wd] = tn(norm_ref[...], query_ref[...]).astype(BF)
-            pair = tn(ins[4][...], ins[4 + n][...])
+            pair = tn(ins[2][...], ins[2 + n][...])
             for p in range(1, n):
-                pair = pair + tn(ins[4 + p][...], ins[4 + n + p][...])
+                pair = pair + tn(ins[2 + p][...], ins[2 + n + p][...])
             o_ref[:, wd : 3 * wd] = pair.astype(BF)
-            out_ref[...] = tn(heads_ref[...], branch_ref[...]).astype(BF)
-
-        row_self_branch, cross_local, cross_out_local = gather_seq(
+
+        row_self_branch, cross_local = gather_seq(
             self_branch, n, rows, 6,
             job=Job(
-                (row_cross_norm, cross_qgrad.reshape(-1, wd), cross_heads, row_cross_branch)
+                (row_cross_norm, cross_qgrad.reshape(-1, wd))
                 + tuple(encoder_blocks) + tuple(cross_grads),
-                (jax.ShapeDtypeStruct((D, 3 * wd), BF), jax.ShapeDtypeStruct((wd, D), BF)),
+                (jax.ShapeDtypeStruct((D, 3 * wd), BF),),
                 cross_gradients,
             ),
         )
         self_grad = dot_back(row_self_branch, own_rows(self_out_weight)).astype(BF)
         self_out_local = outer(self_heads, row_self_branch).astype(BF)
-        matched = wide == D and wd == rows * count
-        plans = [
-            ("all", cross_local.reshape(devices, count, 3 * wd)),
-            ("xor", cross_last),
-        ]
         rows_local = (self_out_local, cross_out_local)
-        if matched:
-            plans += [("rows", x.reshape(rows, count, D)) for x in rows_local]
-        self_grads, pair_bias, cross_parts, cross_last_home, *rows_parts = self_bwd(
-            self_proj, self_grad, self_exact, self_lse, bias_forward, query_side, self_side, plans, n, rows
-        )
+        self_grads, pair_bias, cross_parts = self_bwd(
+            self_proj, self_grad, self_exact, self_lse, bias_forward, query_side, self_side,
+            [("all", cross_local.reshape(devices, count, 3 * wd))], n, rows,
+        )
+        rows_plans = [("rows", self_out_local.reshape(rows, count, D))] if matched else []
+        grad_bias = pair_bias[:, 128:]
+        table_own_grad = jnp.einsum("hd,db->bh", grad_bias, onehot, precision=HIGHEST)
+        table_local = lax.dynamic_update_slice_in_dim(
+            jnp.zeros((BUCKETS, n * hpd), F32), table_own_grad, shard * hpd, 1
+        )[:, :HEADS]
+        self_back = dot_back(self_grads, first_columns).astype(BF)
+        def encoder_job(ins, outs):
+            home_ref, weight_ref, hidden_ref, down_ref, stream_ref = ins
+            total = None
+            for t in range(n):
+                for h in range(hpd):
+                    low = (t * hpd + h) * 2 * HD
+                    part = nt(home_ref[t, h], weight_ref[:, low : low + 2 * HD])
+                    total = part if total is None else total + part
+            outs[0][...] = total
+            outs[1][...] = (stream_ref[...] + nn(hidden_ref[...], down_ref[...])).astype(BF)
+
+        self_back_parts, self_parts, *rest = exchange(
+            [
+                ("seq", self_back.reshape(n, -1, D)),
+                ("all", outer(row_norm, self_grads).astype(BF).reshape(devices, count, 3 * wd)),
+            ] + rows_plans,
+            n, rows, 7,
+            job=Job(
+                (cross_home, cross_pair_weight, hidden, contract_full, after_cross),
+                (
+                    jax.ShapeDtypeStruct(encoder_output.shape[1:], F32),
+                    jax.ShapeDtypeStruct(decoder_input.shape[1:], BF),
+                ),
+                encoder_job,
+            ),
+        )
+        *rows_parts, encoder_gradient, layer_output = rest
+        rows_parts += cross_rows
         if not matched:
             padded = lax.dynamic_update_slice_in_dim(
                 jnp.zeros((wide, 2 * D), BF), jnp.concatenate(rows_local, 1), shard * wd, 0
             )[:D]
             whole = lax.psum_scatter(padded, both, scatter_dimension=0, tiled=True)[None]
             rows_parts = [whole[:, :, :D], whole[:, :, D:]]
-        grad_bias = fold_bias(pair_bias, length)
-        table_own_grad = jnp.einsum("hd,db->bh", grad_bias, onehot, precision=HIGHEST)
-        table_local = lax.dynamic_update_slice_in_dim(
-            jnp.zeros((BUCKETS, n * hpd), F32), table_own_grad, shard * hpd, 1
-        )[:, :HEADS]
-        self_back = dot_back(self_grads, first_columns).astype(BF)
-        def encoder_job(ins, outs):
-            home_ref, last_ref, weight_ref = ins
-            total = None
-            for t in range(n):
-                for h in range(hpd):
-                    grads = last_ref[t] if h == hpd - 1 else home_ref[t, h]
-                    low = (t * hpd + h) * 2 * HD
-                    part = nt(grads, weight_ref[:, low : low + 2 * HD])
-                    total = part if total is None else total + part
-            outs[0][...] = total
-
-        self_back_parts, self_parts, encoder_gradient = exchange(
-            [
-                ("seq", self_back.reshape(n, -1, D)),
-                ("all", outer(row_norm, self_grads).astype(BF).reshape(devices, count, 3 * wd)),
-            ],
-            n, rows, 7,
-            job=Job(
-                (cross_home, cross_last_home, cross_pair_weight),
-                (jax.ShapeDtypeStruct(encoder_output.shape[1:], F32),),
-                encoder_job,
-            ),
-        )
         unused_norm, norm_back = jax.vjp(normalize, inputs, norm_gain[0])
         self_part, self_gain = norm_back(jnp.sum(self_back_parts.astype(F32), 0))
         input_gradient = grad_after_self + self_part
@@ -1042,40 +1062,31 @@
         )
         attention_sum = jnp.moveaxis(attention_parts, 0, 1)
         attention_rows = BETA_TWO * attention_rowwise + (1.0 - BETA_TWO) * attention_means[:, 0:8].T
-        attention_rowsum = jnp.sum(attention_rows, 1)
-        expand_rows, expand_columns, expand_rowsum = factored_start(expand_sum, expand_rowwise)
-        contract_rows, contract_columns, contract_rowsum = factored_start(
+        expand_rows, expand_columns = factored_start(expand_sum, expand_rowwise)
+        contract_rows, contract_columns = factored_start(
             contract_sum[:, None, :], contract_rowwise[None, :]
         )
         gain_local = jnp.stack((self_gain, cross_gain, feed_gain), 0)
-        pieces = (
-            attention_columns,
-            expand_columns,
-            contract_columns,
-            attention_rowsum,
-            expand_rowsum,
-            contract_rowsum,
-            gain_local,
-            table_local,
-        )
-        flat = jnp.concatenate([piece.reshape(-1) for piece in pieces])
-        size = devices * 8 * 128 * -(-flat.shape[0] // (devices * 8 * 128))
-        flat = jnp.pad(flat, (0, size - flat.shape[0])).reshape(devices, -1, 128)
-        flat = sum_everywhere(flat, n, rows).reshape(-1)
-        sums, start = [], 0
-        for piece in pieces:
-            sums.append(flat[start : start + piece.size].reshape(piece.shape))
-            start += piece.size
-        (
-            attention_total,
-            expand_total,
-            contract_total,
-            attention_rowtotal,
-            expand_rowtotal,
-            contract_rowtotal,
-            gain_gradient,
-            table_gradient,
-        ) = sums
+        attention_total, expand_total, contract_total, row_totals, gain_gradient, table_gradient = (
+            sum_everywhere(
+                (
+                    attention_columns,
+                    expand_columns,
+                    contract_columns,
+                    attention_rows,
+                    expand_rows,
+                    contract_rows,
+                    gain_local,
+                    table_local,
+                ),
+                n, rows,
+            )
+        )
+        attention_rowtotal, expand_rowtotal, contract_rowtotal = (
+            row_totals[:, 0],
+            row_totals[:2, 1],
+            row_totals[:1, 2],
+        )
         attention_new = factored_finish(
             attention_sum,
             attention_moment,

time: 546 us -> 521 us (0.954)
  Pallas kernels: 392 us -> 372 us
    pallas_call x1, Pallas kernels: 61.2 us -> 27.3 us  [self_bwd(): pl.pallas_call(kern, grid=(H,), out_shape=(jax.ShapeDtypeStruct((Lq, 3 *...]
    pallas_call x3, Pallas kernels: 85.9 us -> 95.8 us  [exchange(): pl.pallas_call(kern, out_shape=ride.shapes + job.outs, in_specs=[ANY] * (...]
    unnamed x178 -> x223, local copies, waits for them, and re-layouts: 21 us -> 25.5 us
    dot_general x6 -> x5, matrix products: 16.2 us -> 11.7 us  [dot(): return jnp.dot(left, right, preferred_element_type=F32)]
  transfers between devices with their start and end apart: 6 -> 6, of which waited for: 0 -> 0; matrix products, arithmetic and copies ran while one was open for 12% -> 12% of each run, Pallas kernels for 66% -> 65%
where the time goes in v3:
time: 521 us; the launch traced here: 512 us
  Pallas kernels  372 us (71%)
  local copies, waits for them, and re-layouts  47.8 us (9%)
  matrix products  40.1 us (8%)
  other arithmetic  32.1 us (6%)
  between operations  16.4 us (3%)
    pallas_call x3, Pallas kernels, exchange(): pl.pallas_call(kern, out_shape=ride.shapes + job.outs, in_specs=[ANY] * (...  95.8 us
    pallas_call x4, Pallas kernels, gather_seq(): pl.pallas_call(kern, out_shape=(jax.ShapeDtypeStruct((n, length, features...  93.5 us
    pallas_call x1, Pallas kernels, cross_bwd(): pl.pallas_call(kern, grid=(H, n), out_shape=(jax.ShapeDtypeStruct((n, Lq...  86.2 us
    pallas_call x1, Pallas kernels, cross_fwd(): pl.pallas_call(kern, grid=(Lq // qb,), out_shape=(jax.ShapeDtypeStruct((L...  31.1 us
    pallas_call x1, Pallas kernels, self_bwd(): pl.pallas_call(kern, grid=(H,), out_shape=(jax.ShapeDtypeStruct((Lq, 3 *...  27.3 us
    unnamed x223, local copies, waits for them, and re-layouts  25.5 us
    dot_general x6, matrix products, dot_back(): lax.dot_general(left, right, (((1,), (1,)), ((), ())), preferred_element_...  17.5 us
    pallas_call x1, Pallas kernels, sum_everywhere(): pl.pallas_call(kern, out_shape=tuple((jax.ShapeDtypeStruct(shape, F32) fo...  17.5 us
  transfers between devices with their start and end apart: 6, of which 0 were waited for; matrix products, arithmetic and copies ran while one was open for 12% of the time, Pallas kernels for 65%

profile of v3, /device:TPU:0, one launch (start us, length us, event | category | flops | bytes accessed | tf_op | source)
XLA Modules:
  0.0 511.6 jit_solution(17355061185585336272)
XLA Ops:
  12.3 32.8 %gather_seq.4 = (bf16[4,352,768]{2,1,0:T(8,128)(2,1)}, bf16[32,24,576]{2,1,0:T(8,128)(2,1)}) custom-call(bf16[352,768]{1,0:T(8,128)(2,1)} %bitcast.112, bf16[4,24,576]{2,1,0:T(8,128)(2,1)} %reshape.316.refs_1_), custom_call_target="tpu_custom_call" | custom-call | flops 20000000000 | bytes 60000000 | tf_op jit(solution)/shard_map/gather_seq/pallas_call | solution.py:455
  49.4 2.3 fusion.4
  56.1 14.5 %self_fwd.1 = (bf16[1408,192]{1,0:T(8,128)(2,1)S(1)}, f32[1408,192]{1,0:T(8,128)S(1)}, f32[1408,128]{1,0:T(8,128)S(1)}) custom-call(bf16[1408,576]{1,0:T(8,128)(2,1)S(1)} %convolution_convert_fusion.1.qkv_ref, f32[3,1536]{1,0:T(4,128)S(1)} %concatenate.26.rev_ref, bf16[1408,64]{1,0:T(8,128)(2,1)S(1)} %fusion.28.qa_ref, ...), custom_call_target="tpu_custom_call" | custom-call | flops 15000000512 | bytes 45000000 | tf_op jit(solution)/shard_map/self_fwd/pallas_call | solution.py:234
  73.5 31.1 %exchange.3 = bf16[4,352,192]{2,1,0:T(8,128)(2,1)} custom-call(bf16[4,352,192]{2,1,0:T(8,128)(2,1)} %bitcast.109), custom_call_target="tpu_custom_call" | custom-call | flops 20000000000 | bytes 60000000 | tf_op jit(solution)/shard_map/exchange/pallas_call | solution.py:386
  109.5 3.0 select_convert_fusion.ka_ref
  112.5 2.0 multiply_reduce_fusion.5
  115.6 2.0 slice.130.refs_4_
  122.1 18.8 %gather_seq.5 = bf16[4,352,768]{2,1,0:T(8,128)(2,1)} custom-call(bf16[352,768]{1,0:T(8,128)(2,1)} %multiply_convert_fusion.7.refs_0_), custom_call_target="tpu_custom_call" | custom-call | flops 20000000000 | bytes 60000000 | tf_op jit(solution)/shard_map/gather_seq/pallas_call | solution.py:455
  140.9 3.4 convolution_convert_fusion.2.q_ref
  144.3 5.9 %project_blocks.1.kv_ref = bf16[4096,384]{1,0:T(8,128)(2,1)S(1)} custom-call(bf16[1024,768]{1,0:T(8,128)(2,1)S(1)} %bitcast.107, bf16[1024,768]{1,0:T(8,128)(2,1)} %collective-permute-done.refs_1_.refs_4_, bf16[1024,768]{1,0:T(8,128)(2,1)} %collective-permute-done.1.refs_2_.refs_5_, bf16[1024,768]{1,0:T(8,128)(2,1)S(1)} %collective-permute-done.2.refs_3_.refs_6_, ...), custom_call_target="tpu_custom_call" | custom-call | flops 8000000000 | bytes 24000000 | tf_op jit(solution)/shard_map/project_blocks/pallas_call | solution.py:481
  151.9 31.1 %cross_fwd.1 = (bf16[1408,192]{1,0:T(8,128)(2,1)}, f32[1408,192]{1,0:T(8,128)}, f32[1408,128]{1,0:T(8,128)}) custom-call(bf16[1408,192]{1,0:T(8,128)(2,1)} %convolution_convert_fusion.2.q_ref, bf16[4096,384]{1,0:T(8,128)(2,1)} %copy-done.10, bf16[1408,64]{1,0:T(8,128)(2,1)} %copy-done, bf16[4096,64]{1,0:T(8,128)(2,1)} %select_convert_fusion.ka_ref), custom_call_target="tpu_custom_call" | custom-call | flops 31000000512 | bytes 93000000 | tf_op jit(solution)/shard_map/cross_fwd/pallas_call | solution.py:72
  183.0 9.5 %exchange.4 = bf16[4,352,192]{2,1,0:T(8,128)(2,1)} custom-call(bf16[4,352,192]{2,1,0:T(8,128)(2,1)} %bitcast.152), custom_call_target="tpu_custom_call" | custom-call | flops 20000000000 | bytes 60000000 | tf_op jit(solution)/shard_map/exchange/pallas_call | solution.py:386
  193.9 2.0 multiply_reduce_fusion.4
  197.1 2.4 fusion.64
  202.2 2.4 fusion.2
  204.6 4.3 fusion.13
  210.8 3.1 multiply_reduce_fusion
  216.0 22.9 %gather_seq.6 = (bf16[4,352,768]{2,1,0:T(8,128)(2,1)}, bf16[32,24,6400]{2,1,0:T(8,128)(2,1)}) custom-call(bf16[352,768]{1,0:T(8,128)(2,1)} %fusion.58.refs_0_, bf16[352,768]{1,0:T(8,128)(2,1)} %multiply_convert_fusion.6.refs_1_, bf16[352,4096]{1,0:T(8,128)(2,1)} %pad_maximum_fusion.1.refs_2_, bf16[352,2048]{1,0:T(8,128)(2,1)} %get-tuple-element.242.refs_3_.refs_5_, ...), custom_call_target="tpu_custom_call" | custom-call | flops 20000000000 | bytes 60000000 | tf_op jit(solution)/shard_map/gather_seq/pallas_call | solution.py:455
  238.9 3.1 convolution_convert_fusion.6
  245.1 86.2 %cross_bwd.1 = (bf16[4,352,192]{2,1,0:T(8,128)(2,1)}, bf16[4,3,1024,128]{3,2,1,0:T(8,128)(2,1)}, bf16[4,352,192]{2,1,0:T(8,128)(2,1)}, bf16[8,24,768]{2,1,0:T(8,...) custom-call(bf16[1408,192]{1,0:T(8,128)(2,1)} %convolution_convert_f, ...), custom_call_target="tpu_custom_call" | custom-call | flops 67999997952 | bytes 204000000 | tf_op jit(solution)/shard_map/cross_bwd/pallas_call | solution.py:167
  332.8 2.4 multiply_reduce_fusion.1
  337.0 19.1 %gather_seq.7 = (bf16[4,352,768]{2,1,0:T(8,128)(2,1)}, bf16[768,576]{1,0:T(8,128)(2,1)}) custom-call(bf16[352,768]{1,0:T(8,128)(2,1)} %get-tuple-element.232.refs_0_, bf16[1408,768]{1,0:T(8,128)(2,1)} %bitcast.144, bf16[1408,192]{1,0:T(8,128)(2,1)} %bitcast.153, bf16[1024,768]{1,0:T(8,128)(2,1)} %bitcast.104, ...), custom_call_target="tpu_custom_call" | custom-call | flops 20000000000 | bytes 60000000 | tf_op jit(solution)/shard_map/gather_seq/pallas_call | solution.py:455
  356.1 2.6 convolution_convert_fusion.3
  361.5 27.3 %self_bwd.1 = (bf16[1408,576]{1,0:T(8,128)(2,1)}, f32[3,1536]{1,0:T(4,128)S(1)}, bf16[32,24,576]{2,1,0:T(8,128)(2,1)S(1)}) custom-call(bf16[1408,576]{1,0:T(8,128)(2,1)} %copy-done.9, bf16[1408,192]{1,0:T(8,128)(2,1)S(1)} %copy.143.do_ref, f32[1408,192]{1,0:T(8,128)S(1)} %copy-done.15, f32[1408,128]{1,0:T(8,128)S(1)} %copy-done.17, ...), custom_call_target="tpu_custom_call" | custom-call | flops 35000000512 | bytes 105000000 | tf_op jit(solution)/shard_map/self_bwd/pallas_call | solution.py:569
  388.9 3.3 fusion.18
  393.7 3.1 convolution_convert_fusion.5
  396.9 3.2 convolution_convert_fusion
  400.1 55.3 %exchange.5 = (bf16[4,352,768]{2,1,0:T(8,128)(2,1)}, bf16[32,24,576]{2,1,0:T(8,128)(2,1)}, bf16[8,24,768]{2,1,0:T(8,128)(2,1)}, f32[1024,768]{1,0:T(8,128)}, bf16[352,768]{1,0:T(8,128)(2,1)}) custom-call(bf16[4,352,768]{2,1,0:T(8,128)(2,1)} %bitcast.147, bf16[32,24,576]{2,1,0:T(8,128)(2,1)} %bitcast.122, bf16[8,24,768]{2,1,0:T(8,128)(2,1)} %bitcast.155, ...), custom_call_target="tpu_custom_call" | custom-call | flops 20000000000 | bytes 60000000 | tf_op jit(solution)/shard_map/exchange/pallas_call | solution.py:386
  455.5 2.2 convert_reduce_fusion
  462.6 2.5 fusion.22
  470.2 17.5 %sum_everywhere.1 = (f32[8,768]{1,0:T(8,128)}, f32[2,2048]{1,0:T(2,128)}, f32[1,768]{1,0:T(1,128)}, f32[8,128]{1,0:T(8,128)}, f32[3,768]{1,0:T(4,128)}, /*index=5*/f32[32,12]{1,0:T(8,128)}) custom-call(f32[8,768]{1,0:T(8,128)} %copy-done.18, f32[2,2048]{1,0:T(2,128)} %reduce_sum.154.exp, f32[1,768]{1,0:T(1,128)} %reduce_sum.156.con, ...), custom_call_target="tpu_custom_call" | custom-call | flops 16000000000 | bytes 48000000 | tf_op jit(solution)/shard_map/sum_everywhere/pallas_call | solution.py:702
  499.5 2.0 multiply_subtract_fusion.1
  (329 shorter events, 72.0 us)
Async XLA Ops:
  7.2 105.3 %all-gather.5.cloned.1.call-start = ((), (), s32[]{:S(2)}) async-start(), calls=%async_computation.2 | async-start | bytes 6082560 | tf_op jit(solution)/shard_map/all_gather | solution.py:821
  9.8 187.2 %all-gather.3.cloned.1.call-start = ((), (), s32[]{:S(2)}) async-start(), calls=%async_computation.1 | async-start | bytes 10137600 | tf_op jit(solution)/shard_map/all_gather | solution.py:836
  11.0 454.1 %reduce-scatter.2.cloned.1.call-start = ((), (), s32[]{:S(2)}) async-start(), calls=%async_computation.3 | async-start | bytes 10137600 | tf_op jit(solution)/shard_map/reduce_scatter | solution.py:972
  12.2 32.8 %copy-start.4 = (bf16[1,1024,768]{2,1,0:T(8,128)(2,1)S(1)}, bf16[1,1024,768]{2,1,0:T(8,128)(2,1)}, u32[]{:S(2)}) copy-start(bf16[1,1024,768]{2,1,0:T(8,128)(2,1)} %param.27) | copy-start | bytes 4718596
  12.2 34.6 %copy-start.72 = (s32[1,4096]{1,0:T(1,128)S(1)}, s32[1,4096]{1,0:T(1,128)}, u32[]{:S(2)}) copy-start(s32[1,4096]{1,0:T(1,128)} %param.31) | copy-start | bytes 49156
  12.2 34.6 %copy-start.73 = (s32[1,4096]{1,0:T(1,128)S(1)}, s32[1,4096]{1,0:T(1,128)}, u32[]{:S(2)}) copy-start(s32[1,4096]{1,0:T(1,128)} %param.32) | copy-start | bytes 49156
  12.2 34.7 %copy-start.80 = (f32[32,12]{0,1:T(8,128)S(1)}, f32[32,12]{0,1:T(8,128)}, u32[]{:S(2)}) copy-start(f32[32,12]{0,1:T(8,128)} %param.49) | copy-start | bytes 4612
  12.2 34.7 %copy-start.95 = (s32[1408]{0:T(1024)S(1)}, s32[1408]{0:T(1024)}, u32[]{:S(2)}) copy-start(s32[1408]{0:T(1024)} %param.33) | copy-start | bytes 16900
  12.2 36.2 %copy-start.86 = (s32[1,1408]{1,0:T(1,128)S(1)}, s32[1,1408]{1,0:T(1,128)}, u32[]{:S(2)}) copy-start(s32[1,1408]{1,0:T(1,128)} %param.29) | copy-start | bytes 16900
  12.2 36.3 %copy-start.87 = (s32[1,1408]{1,0:T(1,128)S(1)}, s32[1,1408]{1,0:T(1,128)}, u32[]{:S(2)}) copy-start(s32[1,1408]{1,0:T(1,128)} %param.30) | copy-start | bytes 16900
  12.2 36.3 %copy-start.60 = (f32[3,768]{1,0:T(4,128)S(1)}, f32[3,768]{1,0:T(4,128)}, u32[]{:S(2)}) copy-start(f32[3,768]{1,0:T(4,128)} %param.46) | copy-start | bytes 27652
  12.2 36.4 %copy-start.27 = (bf16[1,352,768]{2,1,0:T(8,128)(2,1)S(1)}, bf16[1,352,768]{2,1,0:T(8,128)(2,1)}, u32[]{:S(2)}) copy-start(bf16[1,352,768]{2,1,0:T(8,128)(2,1)} %param.26) | copy-start | bytes 1622020
  45.0 69.5 %collective-permute-start.1 = (bf16[1024,768]{1,0:T(8,128)(2,1)S(1)}, bf16[1024,768]{1,0:T(8,128)(2,1)}, u32[]{:S(2)}, u32[]{:S(2)}) collective-permute-start(bf16[1024,768]{1,0:T(8,128)(2,1)S(1)} %bitcast.105), channel_id=1, source_target_pairs={{0,2},{1,3},{2,0},{3,1},{4,6},{5,7},{6,4},{7,5},{8,10},{9,11},{10,... | collective-permute-start | bytes 4718600 | tf_op jit(solution)/shard_map/ppermute | solution.py:768
  46.7 97.6 %collective-permute-start = (bf16[1024,768]{1,0:T(8,128)(2,1)S(1)}, bf16[1024,768]{1,0:T(8,128)(2,1)}, u32[]{:S(2)}, u32[]{:S(2)}) collective-permute-start(bf16[1024,768]{1,0:T(8,128)(2,1)S(1)} %bitcast.106), channel_id=1, source_target_pairs={{0,1},{1,0},{2,3},{3,2},{4,5},{5,4},{6,7},{7,6},{8,9},{9,8},{10,11... | collective-permute-start | bytes 4718600 | tf_op jit(solution)/shard_map/ppermute | solution.py:770
  48.6 69.1 %copy-start.62 = (f32[768]{0:T(1024)}, f32[768]{0:T(1024)S(1)}, u32[]{:S(2)}) copy-start(f32[768]{0:T(1024)S(1)} %get-tuple-element.217) | copy-start | bytes 9220
  73.5 34.0 %copy-start.81 = (f32[32,12]{0,1:T(8,128)S(1)}, f32[32,12]{0,1:T(8,128)}, u32[]{:S(2)}) copy-start(f32[32,12]{0,1:T(8,128)} %param.50) | copy-start | bytes 4612
  73.5 34.7 %copy-start.82 = (f32[32,12]{0,1:T(8,128)S(1)}, f32[32,12]{0,1:T(8,128)}, u32[]{:S(2)}) copy-start(f32[32,12]{0,1:T(8,128)} %param.51) | copy-start | bytes 4612
  73.5 35.4 %copy-start.90 = (f32[768]{0:T(1024)S(1)}, f32[768]{0:T(1024)}, u32[]{:S(2)}) copy-start(f32[768]{0:T(1024)} %param.45) | copy-start | bytes 9220
  114.6 29.8 %collective-permute-start.2 = (bf16[1024,768]{1,0:T(8,128)(2,1)}, bf16[1024,768]{1,0:T(8,128)(2,1)S(1)}, u32[]{:S(2)}, u32[]{:S(2)}) collective-permute-start(bf16[1024,768]{1,0:T(8,128)(2,1)} %collective-permute-done.1.refs_2_.refs_5_), channel_id=1, source_target_pairs={{0,1},{1,0},{2,3},{3,2},{4,5},{5,4},{6,7},{7,6},{8,9},{9,8},{10,11... | collective-permute-start | bytes 4718600 | tf_op jit(solution)/shard_map/ppermute | solution.py:770
  196.0 139.3 %copy-start.19 = (f32[352,768]{1,0:T(8,128)}, f32[352,768]{1,0:T(8,128)S(1)}, u32[]{:S(2)}) copy-start(f32[352,768]{1,0:T(8,128)S(1)} %get-tuple-element.256.refs_7_) | copy-start | bytes 3244036
  216.0 22.9 %copy-start.101 = (bf16[1408,192]{1,0:T(8,128)(2,1)S(1)}, bf16[1408,192]{1,0:T(8,128)(2,1)}, u32[]{:S(2)}) copy-start(bf16[1408,192]{1,0:T(8,128)(2,1)} %get-tuple-element.70) | copy-start | bytes 1622020
  245.1 87.7 %copy-start.63 = (f32[768]{0:T(1024)S(1)}, f32[768]{0:T(1024)}, u32[]{:S(2)}) copy-start(f32[768]{0:T(1024)} %copy-done.62) | copy-start | bytes 9220
  245.1 87.7 %copy-start.66 = (f32[352]{0:T(512)S(1)}, f32[352]{0:T(512)}, u32[]{:S(2)}) copy-start(f32[352]{0:T(512)} %copy-done.65) | copy-start | bytes 4228
  361.5 27.3 %copy-start.25 = (bf16[4,352,768]{2,1,0:T(8,128)(2,1)S(1)}, bf16[4,352,768]{2,1,0:T(8,128)(2,1)}, u32[]{:S(2)}) copy-start(bf16[4,352,768]{2,1,0:T(8,128)(2,1)} %get-tuple-element.65) | copy-start | bytes 6488068
  361.5 27.3 %copy-start.57 = (f32[768]{0:T(1024)S(1)}, f32[768]{0:T(1024)}, u32[]{:S(2)}) copy-start(f32[768]{0:T(1024)} %copy-done.56) | copy-start | bytes 9220
  361.5 27.3 %copy-start.83 = (f32[1408]{0:T(1024)S(1)}, f32[1408]{0:T(1024)}, u32[]{:S(2)}) copy-start(f32[1408]{0:T(1024)} %rsqrt.47) | copy-start | bytes 16900
  466.2 32.4 %copy-start.44 = (f32[64,768]{1,0:T(8,128)}, f32[64,768]{1,0:T(8,128)S(1)}, u32[]{:S(2)}) copy-start(f32[64,768]{1,0:T(8,128)S(1)} %get-tuple-element.298) | copy-start | bytes 589828
  468.1 31.4 %copy-start.32 = (f32[24,2,2048]{2,1,0:T(2,128)}, f32[24,2,2048]{2,1,0:T(2,128)S(1)}, u32[]{:S(2)}) copy-start(f32[24,2,2048]{2,1,0:T(2,128)S(1)} %reshape.343) | copy-start | bytes 1179652
  470.2 20.5 %copy-start.64 = (f32[8,768]{1,0:T(8,128)S(1)}, f32[8,768]{1,0:T(8,128)}, u32[]{:S(2)}) copy-start(f32[8,768]{1,0:T(8,128)} %param.37) | copy-start | bytes 73732
  470.2 21.2 %copy-start.36 = (f32[24,8,768]{2,1,0:T(8,128)S(1)}, f32[24,8,768]{2,1,0:T(8,128)}, u32[]{:S(2)}) copy-start(f32[24,8,768]{2,1,0:T(8,128)} %param.34) | copy-start | bytes 1769476
  470.2 21.2 %copy-start.45 = (f32[24,8,768]{2,1,0:T(8,128)S(1)}, f32[24,8,768]{2,1,0:T(8,128)}, u32[]{:S(2)}) copy-start(f32[24,8,768]{2,1,0:T(8,128)} %param.35) | copy-start | bytes 1769476
  470.2 21.3 %copy-start.70 = (f32[8,24]{1,0:T(8,128)S(1)}, f32[8,24]{1,0:T(8,128)}, u32[]{:S(2)}) copy-start(f32[8,24]{1,0:T(8,128)} %fusion.46.att_rows) | copy-start | bytes 2308
  (77 other events, 330.0 us)
Sparse Core Ops, SparseCore 0:
  11.5 95.8 all-gather.4
  110.9 82.4 all-gather.2
  245.2 158.5 reduce-scatter.1
